TPU v7x, 32 devices: a whole 2x2x4 slice. The times are simulated.
32 devices in a mesh: depth: 8 (over y, x, core), strip: 4 (over z).
Axes of the slice: x: 2, y: 2, z: 4, core: 2. Of those that a mesh axis runs over, the one named last changes fastest.
Arguments:
- volume: float32 [32, 480, 1920], P('depth', 'strip'), may hold values from 0.001 to 4
- measured: float32 [480, 1920], P('strip'), may hold values from 0.032 to 0.32
- row_taps: float32 [32, 31], P('depth'), may hold values from 0.009677419 to 0.09677419
- col_taps: float32 [32, 15, 31], P('depth'), may hold values from 0.009677419 to 0.09677419
- phase_map: int32 [32, 15], P('depth'), may hold values from 0 to 14
- radius: int32 [32], P('depth'), may hold values from 1 to 15, as said below
Outputs:
- volume_out: float32 [32, 480, 1920], P('depth', 'strip')
Inputs may be any that keep to these rules, and one draw needn't show every extreme that they name: Some plane's radius is exactly 15.
All inputs are finite; a program needn't handle non-finite values.
Results may differ from a plain program's by a relative error of at most 0.0032.
Values may be sent and summed in bfloat16 or wider, within the bound.
No kernel may reach another device: no remote copies, remote signals or barrier semaphores. Data moves between devices by JAX's collectives and lax.ppermute only.
A program may use at most 128 MiB of HBM per device.

v0:
```python
import functools

import jax
import jax.numpy as jnp
from jax import lax
from jax.experimental import pallas as pl
from jax.experimental.pallas import tpu as pltpu
from jax.sharding import PartitionSpec as P

RMAX = 15
ITERS = 2
SIDE = 16
VMEM_LIMIT = 56 * 1024 * 1024

F32 = jnp.float32
BF16 = jnp.bfloat16
NT = (((1,), (1,)), ((), ()))


def round_up(value, step):
    return -(-value // step) * step


class Sizes:
    def __init__(self, planes, rows, cols, devices, pitch):
        self.planes, self.rows, self.cols, self.n, self.pitch = planes, rows, cols, devices, pitch
        self.w = cols // devices
        self.half = devices // 2
        assert cols % devices == 0 and self.w % pitch == 0 and self.w >= 2 * SIDE
        assert devices >= 2 and devices & (devices - 1) == 0 and rows >= 2 * RMAX and rows % 8 == 0
        self.wl = round_up(self.w, 128)
        self.kp = round_up(self.w + 2 * SIDE, 128)
        self.rp = round_up(rows, 128)
        self.e = rows + 2 * RMAX
        self.ep = round_up(self.e, 32)
        self.el = round_up(self.ep, 128)
        self.ar = round_up(max(self.w + SIDE, self.wl, 2 * pitch), pitch)


def iota(shape, axis):
    return lax.broadcasted_iota(jnp.int32, shape, axis)


def phase_rows(sz, z, phase_ref, col_ref, t_ref, a_ref):
    taps = col_ref.shape[2]
    t_ref[...] = jnp.zeros_like(t_ref)
    for p in range(sz.pitch):
        row = col_ref[z, pl.ds(phase_ref[z, p], 1), :]
        t_ref[p : p + 1, 0:taps] = row.astype(BF16).astype(F32)
    base = t_ref[0 : sz.pitch, :]
    for k in range(sz.ar // sz.pitch):
        a_ref[k * sz.pitch : (k + 1) * sz.pitch, :] = base


def spread_matrix(sz, reach, a_ref):
    main_rows = sz.w + SIDE
    main = pltpu.roll(a_ref[0:main_rows, 0 : sz.wl], sz.wl - RMAX, 1, stride=1, stride_axis=0)
    col = iota(main.shape, 1)
    main = jnp.where((jnp.abs(col - iota(main.shape, 0)) <= reach) & (col < sz.w), main, 0.0)
    first = (-SIDE) % sz.pitch
    tail = pltpu.roll(
        a_ref[first : first + SIDE, 0 : sz.wl], sz.wl - RMAX - SIDE, 1, stride=1, stride_axis=0
    )
    col = iota(tail.shape, 1)
    tail = jnp.where((jnp.abs(col - iota(tail.shape, 0) + SIDE) <= reach) & (col < sz.w), tail, 0.0)
    rest = jnp.zeros((sz.kp - main_rows - SIDE, sz.wl), F32)
    return jnp.concatenate([main, tail, rest], axis=0).astype(BF16)


def gather_matrix(sz, reach, a_ref):
    rows = a_ref[0 : sz.wl, :]
    main = pltpu.roll(rows, sz.kp - RMAX, 1, stride=1, stride_axis=0)
    col, row = iota(main.shape, 1), iota(main.shape, 0)
    main = jnp.where((jnp.abs(col - row) <= reach) & (col < sz.w + SIDE) & (row < sz.w), main, 0.0)
    tail = pltpu.roll(
        a_ref[0:SIDE, :], (sz.w + 2 * SIDE - RMAX) % sz.kp, 1, stride=1, stride_axis=0
    )
    col, row = iota(tail.shape, 1), iota(tail.shape, 0)
    inside = (col >= sz.w + SIDE) & (col < sz.w + 2 * SIDE)
    tail = jnp.where(inside & (jnp.abs(col - (sz.w + 2 * SIDE) - row) <= reach), tail, 0.0)
    top = main[0:SIDE] + tail
    return jnp.concatenate([top, main[SIDE:]], axis=0).astype(BF16)


def row_matrix(sz, z, reach, row_ref):
    taps = row_ref.shape[1]
    lane = iota((1, sz.el), 1)
    row = row_ref[pl.ds(z, 1), :].astype(BF16).astype(F32)
    row = jnp.concatenate([row, jnp.zeros((1, sz.el - taps), F32)], axis=1)
    row = jnp.where(jnp.abs(lane - RMAX) <= reach, row, 0.0)
    wide = jnp.broadcast_to(row, (sz.rp, sz.el))
    wide = pltpu.roll(wide, 0, 1, stride=1, stride_axis=0)
    return jnp.where(iota(wide.shape, 0) < sz.rows, wide, 0.0)


def put_block(sz, b, block, win_ref):
    lead = jnp.zeros((sz.rp - sz.rows, sz.w), F32)
    x = jnp.concatenate([block, lead], axis=0).astype(BF16)
    put_columns(sz, b, x, win_ref, sz.rp)


def put_columns(sz, b, x, win_ref, height):
    def rows(k):
        return slice(k * height, (k + 1) * height)

    win_ref[rows(b), 0 : sz.w] = x
    if b > 0:
        win_ref[rows(b - 1), sz.w : sz.w + SIDE] = x[:, 0:SIDE]
    if b < sz.n - 1:
        win_ref[rows(b + 1), sz.w + SIDE : sz.w + 2 * SIDE] = x[:, sz.w - SIDE :]


def columns_forward(sz, z, win_ref, matrix, s_ref):
    out = jnp.dot(win_ref[...], matrix, preferred_element_type=F32).astype(BF16)
    at = pl.ds(pl.multiple_of(z * sz.rp, sz.rp), sz.rp)
    for b in range(sz.n):
        s_ref[b, at, :] = out[b * sz.rp : (b + 1) * sz.rp, :]


def rows_forward(sz, me, rc_ref, s_ref, keep_ref, send_ref):
    core = lax.rem(me, 2)
    coef = rc_ref[...]
    for k in range(sz.half):
        for ref, block in ((send_ref, 2 * k + 1 - core), (keep_ref, 2 * k + core)):
            out = jnp.dot(coef, s_ref[block], preferred_element_type=F32)
            ref[k] = out[:, 0 : sz.w].astype(BF16)


def backward(sz, rwin_ref, bt, rt, g_ref):
    out = lax.dot_general(rwin_ref[...], bt, NT, preferred_element_type=F32).astype(BF16)
    for b in range(sz.n):
        g_ref[b, 0 : sz.ep, :] = out[b * sz.ep : (b + 1) * sz.ep, :]
    for b in range(sz.n):
        back = jnp.dot(rt, g_ref[b], preferred_element_type=F32)
        yield b, back[0 : sz.rows, 0 : sz.w]


def block_norm(sz, b, icn):
    kind = 1 if b == 0 else 2 if b == sz.n - 1 else 0
    return icn[kind : kind + 1, 0 : sz.w]


def window_ratio(sz, ratio_ref, rwin_ref, g_ref):
    rwin_ref[...] = jnp.zeros_like(rwin_ref)
    g_ref[...] = jnp.zeros_like(g_ref)
    for b in range(sz.n):
        put_columns(sz, b, ratio_ref[b], rwin_ref, sz.ep)


def first_kernel(
    sz, me_ref, radius_ref, phase_ref, row_ref, col_ref, vol_ref,
    wf_ref, rc_ref, keep_ref, send_ref, t_ref, a_ref, win_ref, s_ref,
):
    z = pl.program_id(0)

    @pl.when(z == 0)
    def _():
        win_ref[...] = jnp.zeros_like(win_ref)

    reach = radius_ref[z]
    phase_rows(sz, z, phase_ref, col_ref, t_ref, a_ref)
    wf_ref[0] = spread_matrix(sz, reach, a_ref)
    rt = row_matrix(sz, z, reach, row_ref)
    at = pl.ds(pl.multiple_of(z * sz.rp, sz.rp), sz.rp)
    rc_ref[:, at] = rt.T[0 : sz.ep, :].astype(BF16)
    for b in range(sz.n):
        put_block(sz, b, vol_ref[0, :, b * sz.w : (b + 1) * sz.w], win_ref)
    columns_forward(sz, z, win_ref, wf_ref[0], s_ref)

    @pl.when(z == sz.planes - 1)
    def _():
        rows_forward(sz, me_ref[0], rc_ref, s_ref, keep_ref, send_ref)


def table_kernel(
    sz, at_ref, radius_ref, phase_ref, row_ref, col_ref, after_ref,
    bt_ref, rt_ref, irn_ref, icn_ref, t_ref, a_ref,
):
    z = pl.program_id(0)
    reach = radius_ref[z]
    phase_rows(sz, z, phase_ref, col_ref, t_ref, a_ref)
    bt = gather_matrix(sz, reach, a_ref)
    bt_ref[0] = bt
    kind, col = iota((8, sz.kp), 0), iota((8, sz.kp), 1)
    below, above = col >= sz.w + SIDE, (col >= sz.w) & (col < sz.w + SIDE)
    ones = jnp.where(((kind == 1) & below) | ((kind == 2) & above), 0.0, 1.0).astype(BF16)
    norm = lax.dot_general(ones, bt, NT, preferred_element_type=F32)
    icn_ref[0] = jnp.where(norm > 0.0, 1.0 / norm, 0.0)
    rt = row_matrix(sz, z, reach, row_ref)
    rt_ref[0] = rt.astype(BF16)
    row = at_ref[0] + iota(rt.shape, 1) - RMAX
    norm = jnp.sum(jnp.where((row >= 0) & (row < at_ref[1]), rt, 0.0), axis=1, keepdims=True)
    irn_ref[0] = jnp.where(norm > 0.0, 1.0 / norm, 0.0)


def core_sum_kernel(sz, me_ref, keep_ref, recv_ref, own_ref, *out_refs):
    mine = me_ref[0] // 2
    own_ref[...] = keep_ref[mine].astype(F32) + recv_ref[mine].astype(F32)
    for j, ref in enumerate(out_refs, 1):
        other = mine ^ j
        ref[...] = (keep_ref[other].astype(F32) + recv_ref[other].astype(F32)).astype(BF16)


def chip_sum_kernel(sz, own_ref, meas_ref, *refs):
    recv_refs, (sum_ref, up_ref, down_ref) = refs[:-3], refs[-3:]
    total = own_ref[...]
    for ref in recv_refs:
        total = total + ref[...].astype(F32)
    sum_ref[...] = total
    for ref, first, row in ((up_ref, 0, 0), (down_ref, sz.rows, sz.rows - SIDE)):
        ref[0:32, :] = total[first : first + 32, :].astype(BF16)
        meas = meas_ref[row : row + SIDE, :]
        high = meas.astype(BF16)
        ref[32:48, :] = high
        ref[48:64, :] = (meas - high.astype(F32)).astype(BF16)


def ratio_kernel(sz, at_ref, sum_ref, meas_ref, above_ref, below_ref, ratio_ref, s_ref, m_ref):
    s_ref[...] = sum_ref[...]
    s_ref[0:32, :] += above_ref[0:32, :].astype(F32)
    s_ref[sz.rows : sz.rows + 32, :] += below_ref[0:32, :].astype(F32)
    m_ref[...] = jnp.zeros_like(m_ref)
    m_ref[RMAX : RMAX + sz.rows, :] = meas_ref[...]
    high, low = above_ref[32:48, :].astype(F32), above_ref[48:64, :].astype(F32)
    m_ref[0:RMAX, :] = (high + low)[SIDE - RMAX :, :]
    high, low = below_ref[32:48, :].astype(F32), below_ref[48:64, :].astype(F32)
    m_ref[RMAX + sz.rows : sz.e, :] = (high + low)[0:RMAX, :]
    row = iota(s_ref.shape, 0)
    spot = at_ref[0] + row - RMAX
    inside = (row < sz.e) & (spot >= 0) & (spot < at_ref[1])
    ratio_ref[...] = jnp.where(inside, m_ref[...] / s_ref[...], 0.0).astype(BF16)


def middle_kernel(
    sz, me_ref, ratio_ref, bt_ref, rt_ref, irn_ref, icn_ref, wf_ref, rc_ref, vol_ref,
    new_ref, keep_ref, send_ref, rwin_ref, g_ref, win_ref, s_ref,
):
    z = pl.program_id(0)

    @pl.when(z == 0)
    def _():
        win_ref[...] = jnp.zeros_like(win_ref)
        window_ratio(sz, ratio_ref, rwin_ref, g_ref)

    icn, irn = icn_ref[0], irn_ref[0][0 : sz.rows]
    for b, back in backward(sz, rwin_ref, bt_ref[0], rt_ref[0], g_ref):
        old = vol_ref[0, :, b * sz.w : (b + 1) * sz.w]
        new = old * back * (irn * block_norm(sz, b, icn))
        new_ref[0, b] = new
        put_block(sz, b, new, win_ref)
    columns_forward(sz, z, win_ref, wf_ref[0], s_ref)

    @pl.when(z == sz.planes - 1)
    def _():
        rows_forward(sz, me_ref[0], rc_ref, s_ref, keep_ref, send_ref)


def last_kernel(
    sz, ratio_ref, bt_ref, rt_ref, irn_ref, icn_ref, vol_ref, out_ref, rwin_ref, g_ref
):
    @pl.when(pl.program_id(0) == 0)
    def _():
        window_ratio(sz, ratio_ref, rwin_ref, g_ref)

    icn, irn = icn_ref[0], irn_ref[0][0 : sz.rows]
    for b, back in backward(sz, rwin_ref, bt_ref[0], rt_ref[0], g_ref):
        new = vol_ref[0, b] * back * (irn * block_norm(sz, b, icn))
        out_ref[0, :, b * sz.w : (b + 1) * sz.w] = new


def whole(shape):
    return pl.BlockSpec(shape, lambda z: (0,) * len(shape))


def plane(shape):
    return pl.BlockSpec((1,) + shape, lambda z: (z,) + (0,) * len(shape))


SMEM = pl.BlockSpec(memory_space=pltpu.SMEM)
ANY = pl.BlockSpec(memory_space=pl.ANY)


def shape(dims, dtype):
    return jax.ShapeDtypeStruct(dims, dtype)


def call(kernel, sz, name, grid, in_specs, out_specs, out_shape, scratch, args, flops=0, nbytes=0):
    return pl.pallas_call(
        functools.partial(kernel, sz),
        grid=grid,
        in_specs=in_specs,
        out_specs=out_specs,
        out_shape=out_shape,
        scratch_shapes=scratch,
        compiler_params=pltpu.CompilerParams(vmem_limit_bytes=VMEM_LIMIT),
        cost_estimate=pl.CostEstimate(flops=flops, bytes_accessed=nbytes, transcendentals=0),
        name=name,
    )(*args)


def local(volume, measured, row_taps, col_taps, phase_map, radius):
    n = lax.axis_size("depth")
    strips = lax.axis_size("strip")
    planes, rows, cols = volume.shape
    sz = Sizes(planes, rows, cols, n, phase_map.shape[1])
    me = lax.axis_index("depth")
    me_arg = me.reshape(1).astype(jnp.int32)
    at_arg = jnp.stack([lax.axis_index("strip") * rows, rows * strips]).astype(jnp.int32)
    to_core = [(i, i ^ 1) for i in range(n)]
    downward = [(i, i + 1) for i in range(strips - 1)]
    upward = [(i + 1, i) for i in range(strips - 1)]

    meas = lax.dynamic_slice_in_dim(measured, me * sz.w, sz.w, axis=1)

    vol_plane = plane((rows, cols))
    wf_plane, rc_whole = plane((sz.kp, sz.wl)), whole((sz.ep, planes * sz.rp))
    half_whole = whole((sz.half, sz.ep, sz.w))
    half_shape = shape((sz.half, sz.ep, sz.w), BF16)
    tap_specs = [SMEM, SMEM, whole(row_taps.shape), whole(col_taps.shape)]
    tap_scratch = [
        pltpu.VMEM((round_up(sz.pitch, 8), sz.kp), F32),
        pltpu.VMEM((sz.ar, sz.kp), F32),
    ]
    win_scratch = [
        pltpu.VMEM((n * sz.rp, sz.kp), BF16),
        pltpu.VMEM((n, planes * sz.rp, sz.wl), BF16),
    ]
    ratio_scratch = [
        pltpu.VMEM((n * sz.ep, sz.kp), BF16),
        pltpu.VMEM((n, sz.el, sz.wl), BF16),
    ]

    wf, rc, keep, send = call(
        first_kernel, sz, "first", (planes,),
        [SMEM] + tap_specs + [vol_plane],
        [wf_plane, rc_whole, half_whole, half_whole],
        [
            shape((planes, sz.kp, sz.wl), BF16),
            shape((sz.ep, planes * sz.rp), BF16),
            half_shape,
            half_shape,
        ],
        tap_scratch + win_scratch,
        (me_arg, radius, phase_map, row_taps, col_taps, volume),
    )

    tables = None
    current = volume
    for iteration in range(ITERS):
        recv = lax.ppermute(send, "depth", to_core)
        flat = shape((sz.ep, sz.w), BF16)
        own, *sends = call(
            core_sum_kernel, sz, "core_sum", (),
            [SMEM] + [pl.BlockSpec()] * 2,
            [pl.BlockSpec()] * sz.half,
            [shape((sz.ep, sz.w), F32)] + [flat] * (sz.half - 1),
            [], (me_arg, keep, recv),
        )
        recvs = [
            lax.ppermute(part, "depth", [(i, i ^ (2 * j)) for i in range(n)])
            for j, part in enumerate(sends, 1)
        ]
        total, to_above, to_below = call(
            chip_sum_kernel, sz, "chip_sum", (),
            [pl.BlockSpec()] * (2 + len(recvs)),
            [pl.BlockSpec()] * 3,
            [shape((sz.ep, sz.w), F32)] + [shape((64, sz.w), BF16)] * 2,
            [], (own, meas, *recvs),
        )
        from_below = lax.ppermute(to_above, "strip", upward)
        from_above = lax.ppermute(to_below, "strip", downward)
        ratio = call(
            ratio_kernel, sz, "ratio", (),
            [SMEM] + [pl.BlockSpec()] * 4,
            pl.BlockSpec(),
            flat,
            [pltpu.VMEM((sz.ep, sz.w), F32)] * 2,
            (at_arg, total, meas, from_above, from_below),
        )
        gathered = lax.all_gather(ratio, "depth", axis=0, tiled=False)
        if tables is None:
            tables = call(
                table_kernel, sz, "tables", (planes,),
                [SMEM] + tap_specs + [ANY],
                [plane((sz.wl, sz.kp)), plane((sz.rp, sz.el)), plane((sz.rp, 1)), plane((8, sz.wl))],
                [
                    shape((planes, sz.wl, sz.kp), BF16),
                    shape((planes, sz.rp, sz.el), BF16),
                    shape((planes, sz.rp, 1), F32),
                    shape((planes, 8, sz.wl), F32),
                ],
                tap_scratch,
                (at_arg, radius, phase_map, row_taps, col_taps, ratio),
            )
        table_specs = [
            plane((sz.wl, sz.kp)), plane((sz.rp, sz.el)), plane((sz.rp, 1)), plane((8, sz.wl))
        ]
        ratio_whole = whole((n, sz.ep, sz.w))
        blocked = plane((n, rows, sz.w))
        if iteration < ITERS - 1:
            current, keep, send = call(
                middle_kernel, sz, "middle", (planes,),
                [SMEM, ratio_whole] + table_specs + [wf_plane, rc_whole, vol_plane],
                [blocked, half_whole, half_whole],
                [shape((planes, n, rows, sz.w), F32), half_shape, half_shape],
                ratio_scratch + win_scratch,
                (me_arg, gathered, *tables, wf, rc, current),
            )
        else:
            current = call(
                last_kernel, sz, "last", (planes,),
                [ratio_whole] + table_specs + [blocked],
                vol_plane,
                shape(volume.shape, F32),
                ratio_scratch,
                (gathered, *tables, current),
            )
    return current


def solution(mesh):
    return jax.shard_map(
        local,
        mesh=mesh,
        in_specs=(
            P("depth", "strip", None),
            P("strip", None),
            P("depth", None),
            P("depth", None, None),
            P("depth", None),
            P("depth"),
        ),
        out_specs=P("depth", "strip", None),
        check_vma=False,
    )
```

profile of v0, /device:TPU:0, one launch (start us, length us, event | category | flops | bytes accessed | tf_op | source)
XLA Modules:
  0.0 109.1 jit_solution(6145372536721709712)
XLA Ops:
  0.0 0.0 copy-start
  0.0 1.5 %copy.7.col_ref = f32[4,15,31]{2,1,0:T(8,128)} copy(f32[4,15,31]{2,0,1:T(4,128)} %param.9) | data formatting | bytes 14880 | tf_op args[3]
  1.5 6.9 %first.1 = (bf16[4,384,256]{2,1,0:T(8,128)(2,1)}, bf16[160,512]{1,0:T(8,128)(2,1)}, bf16[4,160,240]{2,1,0:T(8,128)(2,1)}, bf16[4,160,240]{2,1,0:T(8,128)(2,1)}) custom-call(s32[1]{0:T(128)} %bitcast.1.me_ref, s32[4]{0:T(128)} %radius_ref.3, s32[4,15]{1,0:T(4,128)} %phase_ref.3, f32[4,31]{1,0:T(4,128)} %row_ref.3, f32[4,15,31]{2,1,0:T(8,128)} %copy.7.col_ref, ...), custom_call_target="tpu_custom_call" | custom-call | tf_op jit(solution)/shard_map/first/pallas_call | solution.py:288
  8.4 0.5 collective-permute-start
  8.9 1.5 %collective-permute-done.recv_ref = bf16[4,160,240]{2,1,0:T(8,128)(2,1)S(1)} collective-permute-done((bf16[4,160,240]{2,1,0:T(8,128)(2,1)}, bf16[4,160,240]{2,1,0:T(8,128)(2,1)S(1)}, u32[]{:S(2)}, u32[]{:S(2)}) %collective-permute-start) | collective-permute-done | bytes 307232 | tf_op jit(solution)/shard_map/ppermute | solution.py:350
  10.3 0.0 copy-start.1
  10.3 0.7 copy-done.1
  11.0 1.9 %core_sum.2 = (f32[160,240]{1,0:T(8,128)}, bf16[160,240]{1,0:T(8,128)(2,1)}, bf16[160,240]{1,0:T(8,128)(2,1)}, bf16[160,240]{1,0:T(8,128)(2,1)}) custom-call(s32[1]{0:T(128)} %bitcast.1.me_ref, bf16[4,160,240]{2,1,0:T(8,128)(2,1)} %get-tuple-element.30.keep_ref, bf16[4,160,240]{2,1,0:T(8,128)(2,1)} %copy-done.1), custom_call_target="tpu_custom_call" | custom-call | tf_op jit(solution)/shard_map/core_sum/pallas_call | solution.py:288
  12.9 2.9 %collective-permute-start.1 = (bf16[160,240]{1,0:T(8,128)(2,1)}, bf16[160,240]{1,0:T(8,128)(2,1)S(1)}, u32[]{:S(2)}, u32[]{:S(2)}) collective-permute-start(bf16[160,240]{1,0:T(8,128)(2,1)} %get-tuple-element.33), channel_id=1, source_target_pairs={{0,8},{4,12},{8,0},{12,4},{16,24},{20,28},{24,16},{28,20},{1,9},{5... | collective-permute-start | bytes 230408 | tf_op jit(solution)/shard_map/ppermute | solution.py:360
  15.8 1.5 %collective-permute-start.2 = (bf16[160,240]{1,0:T(8,128)(2,1)}, bf16[160,240]{1,0:T(8,128)(2,1)S(1)}, u32[]{:S(2)}, u32[]{:S(2)}) collective-permute-start(bf16[160,240]{1,0:T(8,128)(2,1)} %get-tuple-element.34), channel_id=1, source_target_pairs={{0,16},{4,20},{8,24},{12,28},{16,0},{20,4},{24,8},{28,12},{1,17},{... | collective-permute-start | bytes 230408 | tf_op jit(solution)/shard_map/ppermute | solution.py:360
  17.3 0.0 collective-permute-start.3
  17.3 0.0 copy-done
  17.3 0.8 constant_dynamic-slice_fusion.meas_ref
  18.0 0.7 collective-permute-done.1.refs_0_
  18.7 0.0 copy-start.3
  18.7 2.6 %collective-permute-done.2.refs_1_ = bf16[160,240]{1,0:T(8,128)(2,1)S(1)} collective-permute-done((bf16[160,240]{1,0:T(8,128)(2,1)}, bf16[160,240]{1,0:T(8,128)(2,1)S(1)}, u32[]{:S(2)}, u32[]{:S(2)}) %collective-permute-start.2) | collective-permute-done | bytes 76832 | tf_op jit(solution)/shard_map/ppermute | solution.py:360
  21.3 0.0 copy-start.5
  21.3 1.5 %collective-permute-done.3.refs_2_ = bf16[160,240]{1,0:T(8,128)(2,1)S(1)} collective-permute-done((bf16[160,240]{1,0:T(8,128)(2,1)}, bf16[160,240]{1,0:T(8,128)(2,1)S(1)}, u32[]{:S(2)}, u32[]{:S(2)}) %collective-permute-start.3) | collective-permute-done | bytes 76832 | tf_op jit(solution)/shard_map/ppermute | solution.py:360
  22.8 0.0 copy-start.7
  22.8 0.0 copy-done.3
  22.8 0.0 copy-done.5
  22.8 0.6 copy-done.7
  23.5 1.8 %chip_sum.2 = (f32[160,240]{1,0:T(8,128)}, bf16[64,240]{1,0:T(8,128)(2,1)}, bf16[64,240]{1,0:T(8,128)(2,1)}) custom-call(f32[160,240]{1,0:T(8,128)} %get-tuple-element.32.own_ref, f32[120,240]{1,0:T(8,128)} %constant_dynamic-slice_fusion.meas_ref, bf16[160,240]{1,0:T(8,128)(2,1)} %copy-done.3, bf16[160,240]{1,0:T(8,128)(2,1)} %copy-done.5, ...), custom_call_target="tpu_custom_call" | custom-call | tf_op jit(solution)/shard_map/chip_sum/pallas_call | solution.py:288
  25.3 3.5 %collective-permute-start.4 = (bf16[64,240]{1,0:T(8,128)(2,1)}, bf16[64,240]{1,0:T(8,128)(2,1)S(1)}, u32[]{:S(2)}, u32[]{:S(2)}) collective-permute-start(bf16[64,240]{1,0:T(8,128)(2,1)} %get-tuple-element.37), channel_id=1, source_target_pairs={{0,1},{1,2},{2,3},{4,5},{5,6},{6,7},{8,9},{9,10},{10,11},{12,13},{... | collective-permute-start | bytes 92168 | tf_op jit(solution)/shard_map/ppermute | solution.py:371
  28.8 1.3 %collective-permute-start.5 = (bf16[64,240]{1,0:T(8,128)(2,1)}, bf16[64,240]{1,0:T(8,128)(2,1)S(1)}, u32[]{:S(2)}, u32[]{:S(2)}) collective-permute-start(bf16[64,240]{1,0:T(8,128)(2,1)} %get-tuple-element.38), channel_id=1, source_target_pairs={{1,0},{2,1},{3,2},{5,4},{6,5},{7,6},{9,8},{10,9},{11,10},{13,12},{... | collective-permute-start | bytes 92168 | tf_op jit(solution)/shard_map/ppermute | solution.py:370
  30.1 0.6 pad_add_fusion.at_ref
  30.7 0.0 collective-permute-done.4.above_ref
  30.7 0.0 copy-start.9
  30.7 4.1 %collective-permute-done.5.below_ref = bf16[64,240]{1,0:T(8,128)(2,1)S(1)} collective-permute-done((bf16[64,240]{1,0:T(8,128)(2,1)}, bf16[64,240]{1,0:T(8,128)(2,1)S(1)}, u32[]{:S(2)}, u32[]{:S(2)}) %collective-permute-start.5) | collective-permute-done | bytes 30752 | tf_op jit(solution)/shard_map/ppermute | solution.py:370
  34.8 0.0 copy-start.11
  34.8 0.0 copy-done.9
  34.8 0.6 copy-done.11
  35.4 1.7 %ratio.2.after_ref = bf16[160,240]{1,0:T(8,128)(2,1)} custom-call(s32[2]{0:T(128)} %pad_add_fusion.at_ref, f32[160,240]{1,0:T(8,128)} %get-tuple-element.36.sum_ref, f32[120,240]{1,0:T(8,128)} %constant_dynamic-slice_fusion.meas_ref, bf16[64,240]{1,0:T(8,128)(2,1)} %copy-done.9, bf16[64,240]{1,0:T(8,128)(2,1)} %copy-done.11), custom_call_target="tpu_custom_call" | custom-call | tf_op jit(solution)/shard_map/ratio/pallas_call | solution.py:288
  37.1 11.1 %all-gather = bf16[1280,240]{1,0:T(8,128)(2,1)} all-gather(bf16[160,240]{1,0:T(8,128)(2,1)} %ratio.2.after_ref), channel_id=2, replica_groups=mesh['depth'=8,'strip'=4] {'depth'}, dimensions={0}, use_global_device_ids=true | all-gather | bytes 691200 | tf_op jit(solution)/shard_map/all_gather | solution.py:380
  48.2 3.0 %tables.1 = (bf16[4,256,384]{2,1,0:T(8,128)(2,1)}, bf16[4,128,256]{2,1,0:T(8,128)(2,1)}, f32[4,128,1]{2,1,0:T(8,128)}, f32[4,8,256]{2,1,0:T(8,128)}) custom-call(s32[2]{0:T(128)} %pad_add_fusion.at_ref, s32[4]{0:T(128)} %radius_ref.3, s32[4,15]{1,0:T(4,128)} %phase_ref.3, f32[4,31]{1,0:T(4,128)} %row_ref.3, f32[4,15,31]{2,1,0:T(8,128)} %copy.7.col_ref, ...), custom_call_target="tpu_custom_call" | custom-call | tf_op jit(solution)/shard_map/tables/pallas_call | solution.py:288
  51.2 12.4 %middle.1 = (f32[4,8,120,240]{3,2,1,0:T(8,128)}, bf16[4,160,240]{2,1,0:T(8,128)(2,1)}, bf16[4,160,240]{2,1,0:T(8,128)(2,1)}) custom-call(s32[1]{0:T(128)} %bitcast.1.me_ref, bf16[8,160,240]{2,1,0:T(8,128)(2,1)} %bitcast.5, bf16[4,256,384]{2,1,0:T(8,128)(2,1)} %get-tuple-element.39.bt_ref, bf16[4,128,256]{2,1,0:T(8,128)(2,1)} %get-tuple-element.40.rt_ref, ...), custom_call_target="tpu_custom_call" | custom-call | tf_op jit(solution)/shard_map/middle/pallas_call | solution.py:288
  63.6 0.4 collective-permute-start.6
  64.1 1.5 %collective-permute-done.6.recv_ref = bf16[4,160,240]{2,1,0:T(8,128)(2,1)S(1)} collective-permute-done((bf16[4,160,240]{2,1,0:T(8,128)(2,1)}, bf16[4,160,240]{2,1,0:T(8,128)(2,1)S(1)}, u32[]{:S(2)}, u32[]{:S(2)}) %collective-permute-start.6) | collective-permute-done | bytes 307232 | tf_op jit(solution)/shard_map/ppermute | solution.py:350
  65.5 0.0 copy-start.2
  65.5 0.7 copy-done.2
  66.3 1.8 %core_sum.3 = (f32[160,240]{1,0:T(8,128)}, bf16[160,240]{1,0:T(8,128)(2,1)}, bf16[160,240]{1,0:T(8,128)(2,1)}, bf16[160,240]{1,0:T(8,128)(2,1)}) custom-call(s32[1]{0:T(128)} %bitcast.1.me_ref, bf16[4,160,240]{2,1,0:T(8,128)(2,1)} %get-tuple-element.45.keep_ref, bf16[4,160,240]{2,1,0:T(8,128)(2,1)} %copy-done.2), custom_call_target="tpu_custom_call" | custom-call | tf_op jit(solution)/shard_map/core_sum/pallas_call | solution.py:288
  68.1 0.9 collective-permute-start.7
  69.0 1.1 %collective-permute-start.8 = (bf16[160,240]{1,0:T(8,128)(2,1)}, bf16[160,240]{1,0:T(8,128)(2,1)S(1)}, u32[]{:S(2)}, u32[]{:S(2)}) collective-permute-start(bf16[160,240]{1,0:T(8,128)(2,1)} %get-tuple-element.49), channel_id=1, source_target_pairs={{0,16},{4,20},{8,24},{12,28},{16,0},{20,4},{24,8},{28,12},{1,17},{... | collective-permute-start | bytes 230408 | tf_op jit(solution)/shard_map/ppermute | solution.py:360
  70.1 1.5 %collective-permute-start.9 = (bf16[160,240]{1,0:T(8,128)(2,1)}, bf16[160,240]{1,0:T(8,128)(2,1)S(1)}, u32[]{:S(2)}, u32[]{:S(2)}) collective-permute-start(bf16[160,240]{1,0:T(8,128)(2,1)} %get-tuple-element.50), channel_id=1, source_target_pairs={{0,24},{4,28},{8,16},{12,20},{16,8},{20,12},{24,0},{28,4},{1,25},{... | collective-permute-start | bytes 230408 | tf_op jit(solution)/shard_map/ppermute | solution.py:360
  71.6 1.4 %collective-permute-done.7.refs_0_ = bf16[160,240]{1,0:T(8,128)(2,1)S(1)} collective-permute-done((bf16[160,240]{1,0:T(8,128)(2,1)}, bf16[160,240]{1,0:T(8,128)(2,1)S(1)}, u32[]{:S(2)}, u32[]{:S(2)}) %collective-permute-start.7) | collective-permute-done | bytes 76832 | tf_op jit(solution)/shard_map/ppermute | solution.py:360
  73.0 0.0 copy-start.4
  73.0 0.6 collective-permute-done.8.refs_1_
  73.7 0.0 copy-start.6
  73.7 2.0 %collective-permute-done.9.refs_2_ = bf16[160,240]{1,0:T(8,128)(2,1)S(1)} collective-permute-done((bf16[160,240]{1,0:T(8,128)(2,1)}, bf16[160,240]{1,0:T(8,128)(2,1)S(1)}, u32[]{:S(2)}, u32[]{:S(2)}) %collective-permute-start.9) | collective-permute-done | bytes 76832 | tf_op jit(solution)/shard_map/ppermute | solution.py:360
  75.7 0.0 copy-start.8
  75.7 0.0 copy-done.4
  75.7 0.0 copy-done.6
  75.7 0.6 copy-done.8
  76.3 1.8 %chip_sum.3 = (f32[160,240]{1,0:T(8,128)}, bf16[64,240]{1,0:T(8,128)(2,1)}, bf16[64,240]{1,0:T(8,128)(2,1)}) custom-call(f32[160,240]{1,0:T(8,128)} %get-tuple-element.47.own_ref, f32[120,240]{1,0:T(8,128)} %constant_dynamic-slice_fusion.meas_ref, bf16[160,240]{1,0:T(8,128)(2,1)} %copy-done.4, bf16[160,240]{1,0:T(8,128)(2,1)} %copy-done.6, ...), custom_call_target="tpu_custom_call" | custom-call | tf_op jit(solution)/shard_map/chip_sum/pallas_call | solution.py:288
  78.1 3.5 %collective-permute-start.10 = (bf16[64,240]{1,0:T(8,128)(2,1)}, bf16[64,240]{1,0:T(8,128)(2,1)S(1)}, u32[]{:S(2)}, u32[]{:S(2)}) collective-permute-start(bf16[64,240]{1,0:T(8,128)(2,1)} %get-tuple-element.52), channel_id=1, source_target_pairs={{0,1},{1,2},{2,3},{4,5},{5,6},{6,7},{8,9},{9,10},{10,11},{12,13},{... | collective-permute-start | bytes 92168 | tf_op jit(solution)/shard_map/ppermute | solution.py:371
  81.6 1.3 %collective-permute-start.11 = (bf16[64,240]{1,0:T(8,128)(2,1)}, bf16[64,240]{1,0:T(8,128)(2,1)S(1)}, u32[]{:S(2)}, u32[]{:S(2)}) collective-permute-start(bf16[64,240]{1,0:T(8,128)(2,1)} %get-tuple-element.53), channel_id=1, source_target_pairs={{1,0},{2,1},{3,2},{5,4},{6,5},{7,6},{9,8},{10,9},{11,10},{13,12},{... | collective-permute-start | bytes 92168 | tf_op jit(solution)/shard_map/ppermute | solution.py:370
  82.9 0.6 collective-permute-done.10.above_ref
  83.5 0.0 copy-start.10
  83.5 4.1 %collective-permute-done.11.below_ref = bf16[64,240]{1,0:T(8,128)(2,1)S(1)} collective-permute-done((bf16[64,240]{1,0:T(8,128)(2,1)}, bf16[64,240]{1,0:T(8,128)(2,1)S(1)}, u32[]{:S(2)}, u32[]{:S(2)}) %collective-permute-start.11) | collective-permute-done | bytes 30752 | tf_op jit(solution)/shard_map/ppermute | solution.py:370
  87.6 0.0 copy-done.10
  87.6 0.6 copy-done.12
  88.3 1.7 %ratio.3 = bf16[160,240]{1,0:T(8,128)(2,1)} custom-call(s32[2]{0:T(128)} %pad_add_fusion.at_ref, f32[160,240]{1,0:T(8,128)} %get-tuple-element.51.sum_ref, f32[120,240]{1,0:T(8,128)} %constant_dynamic-slice_fusion.meas_ref, bf16[64,240]{1,0:T(8,128)(2,1)} %copy-done.10, bf16[64,240]{1,0:T(8,128)(2,1)} %copy-done.12), custom_call_target="tpu_custom_call" | custom-call | tf_op jit(solution)/shard_map/ratio/pallas_call | solution.py:288
  89.9 11.1 %all-gather.1 = bf16[1280,240]{1,0:T(8,128)(2,1)} all-gather(bf16[160,240]{1,0:T(8,128)(2,1)} %ratio.3), channel_id=3, replica_groups=mesh['depth'=8,'strip'=4] {'depth'}, dimensions={0}, use_global_device_ids=true | all-gather | bytes 691200 | tf_op jit(solution)/shard_map/all_gather | solution.py:380
  101.0 8.0 %last.1 = f32[4,120,1920]{2,1,0:T(8,128)} custom-call(bf16[8,160,240]{2,1,0:T(8,128)(2,1)} %bitcast.4, bf16[4,256,384]{2,1,0:T(8,128)(2,1)} %get-tuple-element.39.bt_ref, bf16[4,128,256]{2,1,0:T(8,128)(2,1)} %get-tuple-element.40.rt_ref, f32[4,128,1]{2,1,0:T(8,128)} %get-tuple-element.41.irn_ref, f32[4,8,256]{2,1,0:T(8,128)} %get-tuple-element.42.icn_ref, ...), custom_call_target="tpu_custom_call" | custom-call | tf_op jit(solution)/shard_map/last/pallas_call | solution.py:288
  (1 shorter events, 0.0 us)
Async XLA Ops:
  0.0 17.3 %copy-start = (f32[120,1920]{1,0:T(8,128)S(1)}, f32[120,1920]{1,0:T(8,128)}, u32[]{:S(2)}) copy-start(f32[120,1920]{1,0:T(8,128)} %param.7) | copy-start | bytes 2764804
  8.4 1.9 %collective-permute-start = (bf16[4,160,240]{2,1,0:T(8,128)(2,1)}, bf16[4,160,240]{2,1,0:T(8,128)(2,1)S(1)}, u32[]{:S(2)}, u32[]{:S(2)}) collective-permute-start(bf16[4,160,240]{2,1,0:T(8,128)(2,1)} %get-tuple-element.31), channel_id=1, source_target_pairs={{0,4},{4,0},{8,12},{12,8},{16,20},{20,16},{24,28},{28,24},{1,5},{5... | collective-permute-start | bytes 921608 | tf_op jit(solution)/shard_map/ppermute | solution.py:350
  10.3 0.7 copy-start.1
  12.9 5.8 %collective-permute-start.1 = (bf16[160,240]{1,0:T(8,128)(2,1)}, bf16[160,240]{1,0:T(8,128)(2,1)S(1)}, u32[]{:S(2)}, u32[]{:S(2)}) collective-permute-start(bf16[160,240]{1,0:T(8,128)(2,1)} %get-tuple-element.33), channel_id=1, source_target_pairs={{0,8},{4,12},{8,0},{12,4},{16,24},{20,28},{24,16},{28,20},{1,9},{5... | collective-permute-start | bytes 230408 | tf_op jit(solution)/shard_map/ppermute | solution.py:360
  15.8 5.6 %collective-permute-start.2 = (bf16[160,240]{1,0:T(8,128)(2,1)}, bf16[160,240]{1,0:T(8,128)(2,1)S(1)}, u32[]{:S(2)}, u32[]{:S(2)}) collective-permute-start(bf16[160,240]{1,0:T(8,128)(2,1)} %get-tuple-element.34), channel_id=1, source_target_pairs={{0,16},{4,20},{8,24},{12,28},{16,0},{20,4},{24,8},{28,12},{1,17},{... | collective-permute-start | bytes 230408 | tf_op jit(solution)/shard_map/ppermute | solution.py:360
  17.3 5.6 %collective-permute-start.3 = (bf16[160,240]{1,0:T(8,128)(2,1)}, bf16[160,240]{1,0:T(8,128)(2,1)S(1)}, u32[]{:S(2)}, u32[]{:S(2)}) collective-permute-start(bf16[160,240]{1,0:T(8,128)(2,1)} %get-tuple-element.35), channel_id=1, source_target_pairs={{0,24},{4,28},{8,16},{12,20},{16,8},{20,12},{24,0},{28,4},{1,25},{... | collective-permute-start | bytes 230408 | tf_op jit(solution)/shard_map/ppermute | solution.py:360
  18.7 4.1 %copy-start.3 = (bf16[160,240]{1,0:T(8,128)(2,1)}, bf16[160,240]{1,0:T(8,128)(2,1)S(1)}, u32[]{:S(2)}) copy-start(bf16[160,240]{1,0:T(8,128)(2,1)S(1)} %collective-permute-done.1.refs_0_) | copy-start | bytes 230404
  21.3 1.5 %copy-start.5 = (bf16[160,240]{1,0:T(8,128)(2,1)}, bf16[160,240]{1,0:T(8,128)(2,1)S(1)}, u32[]{:S(2)}) copy-start(bf16[160,240]{1,0:T(8,128)(2,1)S(1)} %collective-permute-done.2.refs_1_) | copy-start | bytes 230404
  22.8 0.6 copy-start.7
  25.3 5.4 %collective-permute-start.4 = (bf16[64,240]{1,0:T(8,128)(2,1)}, bf16[64,240]{1,0:T(8,128)(2,1)S(1)}, u32[]{:S(2)}, u32[]{:S(2)}) collective-permute-start(bf16[64,240]{1,0:T(8,128)(2,1)} %get-tuple-element.37), channel_id=1, source_target_pairs={{0,1},{1,2},{2,3},{4,5},{5,6},{6,7},{8,9},{9,10},{10,11},{12,13},{... | collective-permute-start | bytes 92168 | tf_op jit(solution)/shard_map/ppermute | solution.py:371
  28.8 6.0 %collective-permute-start.5 = (bf16[64,240]{1,0:T(8,128)(2,1)}, bf16[64,240]{1,0:T(8,128)(2,1)S(1)}, u32[]{:S(2)}, u32[]{:S(2)}) collective-permute-start(bf16[64,240]{1,0:T(8,128)(2,1)} %get-tuple-element.38), channel_id=1, source_target_pairs={{1,0},{2,1},{3,2},{5,4},{6,5},{7,6},{9,8},{10,9},{11,10},{13,12},{... | collective-permute-start | bytes 92168 | tf_op jit(solution)/shard_map/ppermute | solution.py:370
  30.7 4.1 %copy-start.9 = (bf16[64,240]{1,0:T(8,128)(2,1)}, bf16[64,240]{1,0:T(8,128)(2,1)S(1)}, u32[]{:S(2)}) copy-start(bf16[64,240]{1,0:T(8,128)(2,1)S(1)} %collective-permute-done.4.above_ref) | copy-start | bytes 92164
  34.8 0.6 copy-start.11
  63.6 1.9 %collective-permute-start.6 = (bf16[4,160,240]{2,1,0:T(8,128)(2,1)}, bf16[4,160,240]{2,1,0:T(8,128)(2,1)S(1)}, u32[]{:S(2)}, u32[]{:S(2)}) collective-permute-start(bf16[4,160,240]{2,1,0:T(8,128)(2,1)} %get-tuple-element.46), channel_id=1, source_target_pairs={{0,4},{4,0},{8,12},{12,8},{16,20},{20,16},{24,28},{28,24},{1,5},{5... | collective-permute-start | bytes 921608 | tf_op jit(solution)/shard_map/ppermute | solution.py:350
  65.5 0.7 copy-start.2
  68.1 4.9 %collective-permute-start.7 = (bf16[160,240]{1,0:T(8,128)(2,1)}, bf16[160,240]{1,0:T(8,128)(2,1)S(1)}, u32[]{:S(2)}, u32[]{:S(2)}) collective-permute-start(bf16[160,240]{1,0:T(8,128)(2,1)} %get-tuple-element.48), channel_id=1, source_target_pairs={{0,8},{4,12},{8,0},{12,4},{16,24},{20,28},{24,16},{28,20},{1,9},{5... | collective-permute-start | bytes 230408 | tf_op jit(solution)/shard_map/ppermute | solution.py:360
  69.0 4.7 %collective-permute-start.8 = (bf16[160,240]{1,0:T(8,128)(2,1)}, bf16[160,240]{1,0:T(8,128)(2,1)S(1)}, u32[]{:S(2)}, u32[]{:S(2)}) collective-permute-start(bf16[160,240]{1,0:T(8,128)(2,1)} %get-tuple-element.49), channel_id=1, source_target_pairs={{0,16},{4,20},{8,24},{12,28},{16,0},{20,4},{24,8},{28,12},{1,17},{... | collective-permute-start | bytes 230408 | tf_op jit(solution)/shard_map/ppermute | solution.py:360
  70.1 5.6 %collective-permute-start.9 = (bf16[160,240]{1,0:T(8,128)(2,1)}, bf16[160,240]{1,0:T(8,128)(2,1)S(1)}, u32[]{:S(2)}, u32[]{:S(2)}) collective-permute-start(bf16[160,240]{1,0:T(8,128)(2,1)} %get-tuple-element.50), channel_id=1, source_target_pairs={{0,24},{4,28},{8,16},{12,20},{16,8},{20,12},{24,0},{28,4},{1,25},{... | collective-permute-start | bytes 230408 | tf_op jit(solution)/shard_map/ppermute | solution.py:360
  73.0 2.7 %copy-start.4 = (bf16[160,240]{1,0:T(8,128)(2,1)}, bf16[160,240]{1,0:T(8,128)(2,1)S(1)}, u32[]{:S(2)}) copy-start(bf16[160,240]{1,0:T(8,128)(2,1)S(1)} %collective-permute-done.7.refs_0_) | copy-start | bytes 230404
  73.7 2.0 %copy-start.6 = (bf16[160,240]{1,0:T(8,128)(2,1)}, bf16[160,240]{1,0:T(8,128)(2,1)S(1)}, u32[]{:S(2)}) copy-start(bf16[160,240]{1,0:T(8,128)(2,1)S(1)} %collective-permute-done.8.refs_1_) | copy-start | bytes 230404
  75.7 0.6 copy-start.8
  78.1 5.4 %collective-permute-start.10 = (bf16[64,240]{1,0:T(8,128)(2,1)}, bf16[64,240]{1,0:T(8,128)(2,1)S(1)}, u32[]{:S(2)}, u32[]{:S(2)}) collective-permute-start(bf16[64,240]{1,0:T(8,128)(2,1)} %get-tuple-element.52), channel_id=1, source_target_pairs={{0,1},{1,2},{2,3},{4,5},{5,6},{6,7},{8,9},{9,10},{10,11},{12,13},{... | collective-permute-start | bytes 92168 | tf_op jit(solution)/shard_map/ppermute | solution.py:371
  81.6 6.0 %collective-permute-start.11 = (bf16[64,240]{1,0:T(8,128)(2,1)}, bf16[64,240]{1,0:T(8,128)(2,1)S(1)}, u32[]{:S(2)}, u32[]{:S(2)}) collective-permute-start(bf16[64,240]{1,0:T(8,128)(2,1)} %get-tuple-element.53), channel_id=1, source_target_pairs={{1,0},{2,1},{3,2},{5,4},{6,5},{7,6},{9,8},{10,9},{11,10},{13,12},{... | collective-permute-start | bytes 92168 | tf_op jit(solution)/shard_map/ppermute | solution.py:370
  83.5 4.1 %copy-start.10 = (bf16[64,240]{1,0:T(8,128)(2,1)}, bf16[64,240]{1,0:T(8,128)(2,1)S(1)}, u32[]{:S(2)}) copy-start(bf16[64,240]{1,0:T(8,128)(2,1)S(1)} %collective-permute-done.10.above_ref) | copy-start | bytes 92164
  87.6 0.6 copy-start.12
where the time goes:
time: 110 us; the launch traced here: 109 us
  Pallas kernels  41.1 us (37%)
  blocking collectives  22.2 us (20%)
  waiting for transfers between devices  20.6 us (19%)
  starting transfers between devices  18.3 us (17%)
  local copies, waits for them, and re-layouts  6.14 us (6%)
    pallas_call x10, Pallas kernels, call(): pl.pallas_call(functools.partial(kernel, sz), grid=grid, in_specs=in_spec...  41.1 us
    all_gather x2, blocking collectives, local(): gathered = lax.all_gather(ratio, 'depth', axis=0, tiled=False)  22.2 us
    ppermute x6, waiting for transfers between devices, local(): lax.ppermute(part, 'depth', [(i, i ^ 2 * j) for i in range(n)])  8.87 us
    ppermute x2, waiting for transfers between devices, local(): from_below = lax.ppermute(to_above, 'strip', upward)  8.22 us
    ppermute x6, starting transfers between devices, local(): lax.ppermute(part, 'depth', [(i, i ^ 2 * j) for i in range(n)])  7.88 us
    ppermute x2, starting transfers between devices, local(): from_above = lax.ppermute(to_below, 'strip', downward)  6.95 us
    unnamed x27, local copies, waits for them, and re-layouts  5.38 us
    ppermute x2, waiting for transfers between devices, local(): recv = lax.ppermute(send, 'depth', to_core)  2.93 us
  transfers between devices with their start and end apart: 12, of which 11 were waited for; matrix products, arithmetic and copies ran while one was open for 1% of the time, Pallas kernels for 0%

commit v1 on v0

v1 whole, which is shorter than its diff:
```python
import functools

import jax
import jax.numpy as jnp
from jax import lax
from jax.experimental import pallas as pl
from jax.experimental.pallas import tpu as pltpu
from jax.sharding import PartitionSpec as P

RMAX = 15
ITERS = 2
SIDE = 16

F32 = jnp.float32
BF16 = jnp.bfloat16
NT = (((1,), (1,)), ((), ()))


def round_up(value, step):
    return -(-value // step) * step


class Sizes:
    def __init__(self, planes, rows, strips, cols, devices, pitch):
        self.total = rows * strips
        self.planes, self.rows, self.cols, self.n, self.pitch = planes, rows, cols, devices, pitch
        self.w = cols // devices
        self.half = devices // 2
        assert cols % devices == 0 and self.w % pitch == 0 and self.w >= 2 * SIDE
        assert devices >= 2 and devices & (devices - 1) == 0 and rows >= 2 * RMAX and rows % 8 == 0
        self.wl = round_up(self.w, 128)
        self.kp = round_up(self.w + 2 * SIDE, 128)
        self.rp = round_up(rows, 128)
        self.e = rows + 2 * RMAX
        self.ep = round_up(self.e, 32)
        self.el = round_up(self.ep, 128)
        self.ar = round_up(max(self.w + SIDE, self.wl, 2 * pitch), pitch)


def iota(shape, axis):
    return lax.broadcasted_iota(jnp.int32, shape, axis)


def phase_rows(sz, z, phase_ref, col_ref, t_ref, a_ref):
    taps = col_ref.shape[2]
    t_ref[...] = jnp.zeros_like(t_ref)
    for p in range(sz.pitch):
        row = col_ref[phase_ref[z, p], pl.ds(z, 1), :]
        t_ref[p : p + 1, 0:taps] = row.astype(BF16).astype(F32)
    base = t_ref[0 : sz.pitch, :]
    for k in range(sz.ar // sz.pitch):
        a_ref[k * sz.pitch : (k + 1) * sz.pitch, :] = base


def spread_matrix(sz, reach, a_ref):
    main_rows = sz.w + SIDE
    main = pltpu.roll(a_ref[0:main_rows, 0 : sz.wl], sz.wl - RMAX, 1, stride=1, stride_axis=0)
    col = iota(main.shape, 1)
    main = jnp.where((jnp.abs(col - iota(main.shape, 0)) <= reach) & (col < sz.w), main, 0.0)
    first = (-SIDE) % sz.pitch
    tail = pltpu.roll(
        a_ref[first : first + SIDE, 0 : sz.wl], sz.wl - RMAX - SIDE, 1, stride=1, stride_axis=0
    )
    col = iota(tail.shape, 1)
    tail = jnp.where((jnp.abs(col - iota(tail.shape, 0) + SIDE) <= reach) & (col < sz.w), tail, 0.0)
    rest = jnp.zeros((sz.kp - main_rows - SIDE, sz.wl), F32)
    return jnp.concatenate([main, tail, rest], axis=0).astype(BF16)


def gather_matrix(sz, reach, a_ref):
    rows = a_ref[0 : sz.wl, :]
    main = pltpu.roll(rows, sz.kp - RMAX, 1, stride=1, stride_axis=0)
    col, row = iota(main.shape, 1), iota(main.shape, 0)
    main = jnp.where((jnp.abs(col - row) <= reach) & (col < sz.w + SIDE) & (row < sz.w), main, 0.0)
    tail = pltpu.roll(
        a_ref[0:SIDE, :], (sz.w + 2 * SIDE - RMAX) % sz.kp, 1, stride=1, stride_axis=0
    )
    col, row = iota(tail.shape, 1), iota(tail.shape, 0)
    inside = (col >= sz.w + SIDE) & (col < sz.w + 2 * SIDE)
    tail = jnp.where(inside & (jnp.abs(col - (sz.w + 2 * SIDE) - row) <= reach), tail, 0.0)
    top = main[0:SIDE] + tail
    return jnp.concatenate([top, main[SIDE:]], axis=0).astype(BF16)


def row_matrix(sz, z, reach, row_ref):
    taps = row_ref.shape[1]
    lane = iota((1, sz.el), 1)
    row = row_ref[pl.ds(z, 1), :].astype(BF16).astype(F32)
    row = jnp.concatenate([row, jnp.zeros((1, sz.el - taps), F32)], axis=1)
    row = jnp.where(jnp.abs(lane - RMAX) <= reach, row, 0.0)
    wide = jnp.broadcast_to(row, (sz.rp, sz.el))
    wide = pltpu.roll(wide, 0, 1, stride=1, stride_axis=0)
    return jnp.where(iota(wide.shape, 0) < sz.rows, wide, 0.0)


def put_block(sz, b, block, win_ref):
    lead = jnp.zeros((sz.rp - sz.rows, sz.w), F32)
    x = jnp.concatenate([block, lead], axis=0).astype(BF16)

    def rows(k):
        return slice(k * sz.rp, (k + 1) * sz.rp)

    win_ref[rows(b), 0 : sz.w] = x
    if b > 0:
        win_ref[rows(b - 1), sz.w : sz.w + SIDE] = x[:, 0:SIDE]
    if b < sz.n - 1:
        win_ref[rows(b + 1), sz.w + SIDE : sz.w + 2 * SIDE] = x[:, sz.w - SIDE :]


def columns_forward(sz, z, win_ref, matrix, s_ref):
    out = jnp.dot(win_ref[...], matrix, preferred_element_type=F32).astype(BF16)
    at = pl.ds(pl.multiple_of(z * sz.rp, sz.rp), sz.rp)
    for b in range(sz.n):
        s_ref[b, at, :] = out[b * sz.rp : (b + 1) * sz.rp, :]


def rows_forward(sz, me, rc_ref, s_ref, keep_ref, send_ref):
    core = lax.rem(me, 2)
    coef = rc_ref[...]
    for k in range(sz.half):
        for ref, block in ((send_ref, 2 * k + 1 - core), (keep_ref, 2 * k + core)):
            out = jnp.dot(coef, s_ref[block], preferred_element_type=F32)
            ref[k] = out[:, 0 : sz.w].astype(ref.dtype)


def backward(sz, rwin_ref, bt, rt, g_ref):
    out = lax.dot_general(rwin_ref[...], bt, NT, preferred_element_type=F32).astype(BF16)
    for b in range(sz.n):
        g_ref[b, 0 : sz.ep, :] = out[b * sz.ep : (b + 1) * sz.ep, :]
    for b in range(sz.n):
        back = jnp.dot(rt, g_ref[b], preferred_element_type=F32)
        yield b, back[0 : sz.rows, 0 : sz.w]


def block_norm(sz, b, icn):
    kind = 1 if b == 0 else 2 if b == sz.n - 1 else 0
    return icn[kind : kind + 1, 0 : sz.w]


def window_ratio(sz, me, same_ref, other_ref, rwin_ref, g_ref):
    rwin_ref[...] = jnp.zeros_like(rwin_ref)
    g_ref[...] = jnp.zeros_like(g_ref)
    core = lax.rem(me, 2)

    def rows(k):
        return pl.ds(pl.multiple_of(k * sz.ep, sz.ep), sz.ep)

    for j in range(sz.half):
        chip = (me // 2) ^ j
        for ref, b in ((same_ref, 2 * chip + core), (other_ref, 2 * chip + 1 - core)):
            rwin_ref[rows(b), 0 : sz.w] = ref[j]

            @pl.when(b > 0)
            def _():
                rwin_ref[rows(b - 1), sz.w : sz.w + SIDE] = ref[j, :, 0:SIDE]

            @pl.when(b < sz.n - 1)
            def _():
                rwin_ref[rows(b + 1), sz.w + SIDE : sz.w + 2 * SIDE] = ref[j, :, sz.w - SIDE :]


def first_kernel(
    sz, me_ref, radius_hbm, phase_hbm, row_hbm, col_hbm, vol_hbm,
    wf_ref, rc_ref, keep_ref, send_ref,
    radius_ref, phase_ref, row_ref, col_ref, vol_ref, t_ref, a_ref, win_ref, s_ref, sems,
):
    pairs = ((radius_hbm, radius_ref), (phase_hbm, phase_ref), (row_hbm, row_ref), (col_hbm, col_ref))
    small = [pltpu.make_async_copy(a, b, sems.at[i]) for i, (a, b) in enumerate(pairs)]
    large = [
        pltpu.make_async_copy(vol_hbm.at[z], vol_ref.at[z], sems.at[4 + z])
        for z in range(sz.planes)
    ]
    for copy in small + large:
        copy.start()
    win_ref[...] = jnp.zeros_like(win_ref)
    for copy in small:
        copy.wait()
    for z in range(sz.planes):
        reach = radius_ref[z]
        phase_rows(sz, z, phase_ref, col_ref, t_ref, a_ref)
        wf_ref[z] = spread_matrix(sz, reach, a_ref)
        rt = row_matrix(sz, z, reach, row_ref)
        rc_ref[:, z * sz.rp : (z + 1) * sz.rp] = rt.T[0 : sz.ep, :].astype(BF16)
    for z in range(sz.planes):
        large[z].wait()
        for b in range(sz.n):
            put_block(sz, b, vol_ref[z, :, b * sz.w : (b + 1) * sz.w], win_ref)
        columns_forward(sz, z, win_ref, wf_ref[z], s_ref)
    rows_forward(sz, me_ref[0], rc_ref, s_ref, keep_ref, send_ref)


def table_kernel(
    sz, strip_ref, radius_hbm, phase_hbm, row_hbm, col_hbm, after_ref,
    bt_ref, rt_ref, irn_ref, icn_ref,
    radius_ref, phase_ref, row_ref, col_ref, t_ref, a_ref, sems,
):
    pairs = ((radius_hbm, radius_ref), (phase_hbm, phase_ref), (row_hbm, row_ref), (col_hbm, col_ref))
    small = [pltpu.make_async_copy(a, b, sems.at[i]) for i, (a, b) in enumerate(pairs)]
    for copy in small:
        copy.start()
    for copy in small:
        copy.wait()
    kind, col = iota((8, sz.kp), 0), iota((8, sz.kp), 1)
    below, above = col >= sz.w + SIDE, (col >= sz.w) & (col < sz.w + SIDE)
    ones = jnp.where(((kind == 1) & below) | ((kind == 2) & above), 0.0, 1.0).astype(BF16)
    for z in range(sz.planes):
        reach = radius_ref[z]
        phase_rows(sz, z, phase_ref, col_ref, t_ref, a_ref)
        bt = gather_matrix(sz, reach, a_ref)
        bt_ref[z] = bt
        norm = lax.dot_general(ones, bt, NT, preferred_element_type=F32)
        icn_ref[z] = jnp.where(norm > 0.0, 1.0 / norm, 0.0)
        rt = row_matrix(sz, z, reach, row_ref)
        rt_ref[z] = rt.astype(BF16)
        row = strip_ref[0] * sz.rows + iota(rt.shape, 1) - RMAX
        norm = jnp.sum(jnp.where((row >= 0) & (row < sz.total), rt, 0.0), axis=1, keepdims=True)
        irn_ref[z] = jnp.where(norm > 0.0, 1.0 / norm, 0.0)


def core_sum_kernel(sz, me_ref, keep_ref, recv_ref, own_ref, *out_refs):
    mine = me_ref[0] // 2
    own_ref[...] = keep_ref[mine] + recv_ref[mine].astype(F32)
    for j, ref in enumerate(out_refs, 1):
        other = mine ^ j
        ref[...] = (keep_ref[other] + recv_ref[other].astype(F32)).astype(BF16)


def chip_sum_kernel(sz, strip_ref, after_ref, own_ref, meas_ref, *refs):
    recv_refs, (sum_ref, first_ref, second_ref) = refs[:-3], refs[-3:]
    total = own_ref[...]
    for ref in recv_refs:
        total = total + ref[...].astype(F32)
    sum_ref[...] = total
    edges = []
    for first, row in ((0, 0), (sz.rows, sz.rows - SIDE)):
        meas = meas_ref[row : row + SIDE, :]
        high = meas.astype(BF16).astype(F32)
        edges.append(jnp.concatenate([total[first : first + 32, :], high, meas - high], axis=0))
    up, down = edges
    even = lax.rem(strip_ref[0], 2) == 0
    first_ref[...] = jnp.where(even, down, up).astype(BF16)
    second_ref[...] = jnp.where(even, up, down).astype(BF16)


def ratio_kernel(sz, strip_ref, sum_ref, meas_ref, first_ref, second_ref, ratio_ref, s_ref, m_ref):
    even = lax.rem(strip_ref[0], 2) == 0
    first, second = first_ref[...].astype(F32), second_ref[...].astype(F32)
    above, below = jnp.where(even, second, first), jnp.where(even, first, second)
    s_ref[...] = sum_ref[...]
    s_ref[0:32, :] += above[0:32, :]
    s_ref[sz.rows : sz.rows + 32, :] += below[0:32, :]
    m_ref[...] = jnp.zeros_like(m_ref)
    m_ref[RMAX : RMAX + sz.rows, :] = meas_ref[...]
    m_ref[0:RMAX, :] = (above[32:48, :] + above[48:64, :])[SIDE - RMAX :, :]
    m_ref[RMAX + sz.rows : sz.e, :] = (below[32:48, :] + below[48:64, :])[0:RMAX, :]
    row = iota(s_ref.shape, 0)
    spot = strip_ref[0] * sz.rows + row - RMAX
    inside = (row < sz.e) & (spot >= 0) & (spot < sz.total)
    ratio_ref[...] = jnp.where(inside, m_ref[...] / s_ref[...], 0.0).astype(BF16)


def middle_kernel(
    sz, me_ref, same_ref, other_ref, bt_ref, rt_ref, irn_ref, icn_ref, wf_ref, rc_ref, vol_hbm,
    new_ref, keep_ref, send_ref, vol_ref, rwin_ref, g_ref, win_ref, s_ref, sems,
):
    def fetch(z):
        return pltpu.make_async_copy(vol_hbm.at[z], vol_ref.at[z], sems.at[z])

    for z in range(sz.planes):
        fetch(z).start()
    win_ref[...] = jnp.zeros_like(win_ref)
    window_ratio(sz, me_ref[0], same_ref, other_ref, rwin_ref, g_ref)

    def step(z, carry):
        icn, irn = icn_ref[z], irn_ref[z][0 : sz.rows]
        fetch(z).wait()
        for b, back in backward(sz, rwin_ref, bt_ref[z], rt_ref[z], g_ref):
            old = vol_ref[z, :, b * sz.w : (b + 1) * sz.w]
            new = old * back * (irn * block_norm(sz, b, icn))
            new_ref[z, b] = new
            put_block(sz, b, new, win_ref)
        columns_forward(sz, z, win_ref, wf_ref[z], s_ref)
        return carry

    lax.fori_loop(0, sz.planes, step, 0)
    rows_forward(sz, me_ref[0], rc_ref, s_ref, keep_ref, send_ref)


def last_kernel(
    sz, me_ref, same_ref, other_ref, bt_ref, rt_ref, irn_ref, icn_ref, vol_ref,
    out_hbm, rwin_ref, g_ref, out_ref, sems,
):
    window_ratio(sz, me_ref[0], same_ref, other_ref, rwin_ref, g_ref)

    def copy(z):
        return pltpu.make_async_copy(out_ref.at[z], out_hbm.at[z], sems.at[z])

    def step(z, carry):
        icn, irn = icn_ref[z], irn_ref[z][0 : sz.rows]
        for b, back in backward(sz, rwin_ref, bt_ref[z], rt_ref[z], g_ref):
            new = vol_ref[z, b] * back * (irn * block_norm(sz, b, icn))
            out_ref[z, :, b * sz.w : (b + 1) * sz.w] = new
        copy(z).start()
        return carry

    lax.fori_loop(0, sz.planes, step, 0)
    for z in range(sz.planes):
        copy(z).wait()


SMEM = pl.BlockSpec(memory_space=pltpu.SMEM)
VMEM = pl.BlockSpec(memory_space=pltpu.VMEM)
ANY = pl.BlockSpec(memory_space=pl.ANY)
HBM = pl.BlockSpec(memory_space=pltpu.HBM)


def shape(dims, dtype):
    return jax.ShapeDtypeStruct(dims, dtype)


def call(kernel, sz, name, in_specs, out_specs, out_shape, scratch, args, mib, micros=1):
    return pl.pallas_call(
        functools.partial(kernel, sz),
        in_specs=in_specs,
        out_specs=out_specs,
        out_shape=out_shape,
        scratch_shapes=scratch,
        compiler_params=pltpu.CompilerParams(vmem_limit_bytes=mib * 1024 * 1024),
        cost_estimate=pl.CostEstimate(
            flops=0, bytes_accessed=micros * 3_000_000, transcendentals=0
        ),
        name=name,
    )(*args)


def local(volume, measured, row_taps, col_taps, phase_map, radius):
    n = lax.axis_size("depth")
    strips = lax.axis_size("strip")
    planes, rows, cols = volume.shape
    sz = Sizes(planes, rows, strips, cols, n, phase_map.shape[1])
    me = lax.axis_index("depth")
    strip = lax.axis_index("strip")
    me_arg = me.reshape(1).astype(jnp.int32)
    strip_arg = strip.reshape(1).astype(jnp.int32)
    to_core = [(i, i ^ 1) for i in range(n)]
    to_chip = [[(i, i ^ (2 * j)) for i in range(n)] for j in range(1, sz.half)]
    swaps = []
    for start in (0, 1):
        below = [(i, i + 1) for i in range(start, strips - 1, 2)]
        swaps.append(below + [(b, a) for a, b in below])

    volume = pltpu.with_memory_space_constraint(volume, pltpu.HBM)
    meas = lax.dynamic_slice_in_dim(measured, me * sz.w, sz.w, axis=1)
    by_family = col_taps.transpose(1, 0, 2)

    flat = shape((sz.ep, sz.w), BF16)
    halves = [shape((sz.half, sz.ep, sz.w), F32), shape((sz.half, sz.ep, sz.w), BF16)]
    blocked = shape((planes, n, rows, sz.w), F32)
    tap_args = tuple(
        pltpu.with_memory_space_constraint(x, pltpu.HBM)
        for x in (radius, phase_map, row_taps, by_family)
    )
    tap_scratch = [
        pltpu.SMEM(radius.shape, jnp.int32),
        pltpu.SMEM(phase_map.shape, jnp.int32),
        pltpu.VMEM(row_taps.shape, F32),
        pltpu.VMEM(by_family.shape, F32),
    ]
    row_scratch = [
        pltpu.VMEM((round_up(sz.pitch, 8), sz.kp), F32),
        pltpu.VMEM((sz.ar, sz.kp), F32),
    ]
    win_scratch = [
        pltpu.VMEM((n * sz.rp, sz.kp), BF16),
        pltpu.VMEM((n, planes * sz.rp, sz.wl), BF16),
    ]
    ratio_scratch = [
        pltpu.VMEM((n * sz.ep, sz.kp), BF16),
        pltpu.VMEM((n, sz.el, sz.wl), BF16),
    ]

    wf, rc, keep, send = call(
        first_kernel, sz, "first",
        [SMEM] + [HBM] * 5,
        [VMEM] * 4,
        [
            shape((planes, sz.kp, sz.wl), BF16),
            shape((sz.ep, planes * sz.rp), BF16),
            *halves,
        ],
        tap_scratch + [pltpu.VMEM(volume.shape, F32)] + row_scratch + win_scratch
        + [pltpu.SemaphoreType.DMA((4 + planes,))],
        (me_arg, *tap_args, volume),
        24, 4,
    )

    tables, current = None, volume
    for iteration in range(ITERS):
        recv = lax.ppermute(send, "depth", to_core)
        own, *sends = call(
            core_sum_kernel, sz, "core_sum",
            [SMEM, VMEM, VMEM],
            [VMEM] * sz.half,
            [shape((sz.ep, sz.w), F32)] + [flat] * (sz.half - 1),
            [], (me_arg, keep, recv), 4,
        )
        if tables is None:
            tables = call(
                table_kernel, sz, "tables",
                [SMEM] + [HBM] * 4 + [ANY],
                [VMEM] * 4,
                [
                    shape((planes, sz.wl, sz.kp), BF16),
                    shape((planes, sz.rp, sz.el), BF16),
                    shape((planes, sz.rp, 1), F32),
                    shape((planes, 8, sz.wl), F32),
                ],
                tap_scratch + row_scratch + [pltpu.SemaphoreType.DMA((4,))],
                (strip_arg, *tap_args, own),
                8, 2,
            )
        recvs = [lax.ppermute(part, "depth", pairs) for part, pairs in zip(sends, to_chip)]
        total, *edges = call(
            chip_sum_kernel, sz, "chip_sum",
            [SMEM, ANY] + [VMEM] * (2 + len(recvs)),
            [VMEM] * 3,
            [shape((sz.ep, sz.w), F32)] + [shape((64, sz.w), BF16)] * 2,
            [], (strip_arg, tables[3], own, meas, *recvs), 4,
        )
        edges = [lax.ppermute(part, "strip", pairs) for part, pairs in zip(edges, swaps)]
        ratio = call(
            ratio_kernel, sz, "ratio",
            [SMEM] + [VMEM] * 4,
            VMEM,
            flat,
            [pltpu.VMEM((sz.ep, sz.w), F32)] * 2,
            (strip_arg, total, meas, *edges), 4,
        )
        same = jnp.stack([ratio] + [lax.ppermute(ratio, "depth", pairs) for pairs in to_chip])
        other = lax.ppermute(same, "depth", to_core)
        if iteration < ITERS - 1:
            current, keep, send = call(
                middle_kernel, sz, "middle",
                [SMEM] + [VMEM] * 8 + [HBM],
                [VMEM] * 3,
                [blocked, *halves],
                [pltpu.VMEM(volume.shape, F32)] + ratio_scratch + win_scratch
                + [pltpu.SemaphoreType.DMA((planes,))],
                (me_arg, same, other, *tables, wf, rc, current),
                24, 5,
            )
        else:
            current = call(
                last_kernel, sz, "last",
                [SMEM] + [VMEM] * 7,
                HBM,
                shape(volume.shape, F32),
                ratio_scratch
                + [pltpu.VMEM(volume.shape, F32), pltpu.SemaphoreType.DMA((planes,))],
                (me_arg, same, other, *tables, current),
                24, 5,
            )
    return current


def solution(mesh):
    return jax.shard_map(
        local,
        mesh=mesh,
        in_specs=(
            P("depth", "strip", None),
            P("strip", None),
            P("depth", None),
            P("depth", None, None),
            P("depth", None),
            P("depth"),
        ),
        out_specs=P("depth", "strip", None),
        check_vma=False,
    )
```

time: 110 us -> 72.9 us (0.66)
  the two profiles are of different devices: /device:TPU:0 before, /device:TPU:17 now
where the time goes in v1:
time: 72.9 us; the launch traced here: 72.7 us
  starting transfers between devices  26.7 us (37%)
  Pallas kernels  24.4 us (33%)
  waiting for transfers between devices  21.1 us (29%)
    pallas_call x10, Pallas kernels, call(): pl.pallas_call(functools.partial(kernel, sz), in_specs=in_specs, out_spec...  24.4 us
    ppermute x2, starting transfers between devices, local(): other = lax.ppermute(same, 'depth', to_core)  9.38 us
    ppermute x6, waiting for transfers between devices, local(): lax.ppermute(part, 'depth', pairs)  5.61 us
    ppermute x4, waiting for transfers between devices, local(): lax.ppermute(part, 'strip', pairs)  5.45 us
    ppermute x6, starting transfers between devices, local(): lax.ppermute(ratio, 'depth', pairs)  5.43 us
    ppermute x6, starting transfers between devices, local(): lax.ppermute(part, 'depth', pairs)  5.43 us
    ppermute x4, starting transfers between devices, local(): lax.ppermute(part, 'strip', pairs)  5.26 us
    ppermute x6, waiting for transfers between devices, local(): lax.ppermute(ratio, 'depth', pairs)  5.04 us
  transfers between devices with their start and end apart: 20, of which 18 were waited for; matrix products, arithmetic and copies ran while one was open for 0% of the time, Pallas kernels for 2%

profile of v1, /device:TPU:17, one launch (start us, length us, event | category | flops | bytes accessed | tf_op | source)
XLA Modules:
  0.0 72.7 jit_solution(2594491875911214537)
XLA Ops:
  0.0 0.0 copy-start
  0.0 5.6 %first.1 = (bf16[4,384,256]{2,1,0:T(8,128)(2,1)S(1)}, bf16[160,512]{1,0:T(8,128)(2,1)S(1)}, f32[4,160,240]{2,1,0:T(8,128)S(1)}, bf16[4,160,240]{2,1,0:T(8,128)(2,1)S(1)}) custom-call(s32[1]{0:T(128)} %bitcast.me_ref, s32[4]{0:T(128)} %radius_hbm.3, s32[4,15]{1,0:T(4,128)} %phase_hbm.3, f32[4,31]{1,0:T(4,128)} %row_hbm.3, f32[15,4,31]{2,1,0:T(4,128)} %bitcast.13, ...), custom_call_target="tpu_custom_call" | custom-call | bytes 12000000 | tf_op jit(solution)/shard_map/first/pallas_call | solution.py:322
  5.6 0.7 %collective-permute-start = (bf16[4,160,240]{2,1,0:T(8,128)(2,1)S(1)}, bf16[4,160,240]{2,1,0:T(8,128)(2,1)S(1)}, u32[]{:S(2)}, u32[]{:S(2)}) collective-permute-start(bf16[4,160,240]{2,1,0:T(8,128)(2,1)S(1)} %get-tuple-element.31), channel_id=1, source_target_pairs={{0,4},{4,0},{8,12},{12,8},{16,20},{20,16},{24,28},{28,24},{1,5},{5... | collective-permute-start | bytes 921608 | tf_op jit(solution)/shard_map/ppermute | solution.py:399
  6.3 1.3 %collective-permute-done.recv_ref = bf16[4,160,240]{2,1,0:T(8,128)(2,1)S(1)} collective-permute-done((bf16[4,160,240]{2,1,0:T(8,128)(2,1)S(1)}, bf16[4,160,240]{2,1,0:T(8,128)(2,1)S(1)}, u32[]{:S(2)}, u32[]{:S(2)}) %collective-permute-start) | collective-permute-done | bytes 307232 | tf_op jit(solution)/shard_map/ppermute | solution.py:399
  7.6 0.1 core_sum.2
  7.6 1.3 %collective-permute-start.1 = (bf16[160,240]{1,0:T(8,128)(2,1)S(1)}, bf16[160,240]{1,0:T(8,128)(2,1)S(1)}, u32[]{:S(2)}, u32[]{:S(2)}) collective-permute-start(bf16[160,240]{1,0:T(8,128)(2,1)S(1)} %get-tuple-element.34), channel_id=1, source_target_pairs={{0,8},{4,12},{8,0},{12,4},{16,24},{20,28},{24,16},{28,20},{1,9},{5... | collective-permute-start | bytes 230408 | tf_op jit(solution)/shard_map/ppermute | solution.py:422
  8.9 1.2 %collective-permute-start.2 = (bf16[160,240]{1,0:T(8,128)(2,1)S(1)}, bf16[160,240]{1,0:T(8,128)(2,1)S(1)}, u32[]{:S(2)}, u32[]{:S(2)}) collective-permute-start(bf16[160,240]{1,0:T(8,128)(2,1)S(1)} %get-tuple-element.35), channel_id=1, source_target_pairs={{0,16},{4,20},{8,24},{12,28},{16,0},{20,4},{24,8},{28,12},{1,17},{... | collective-permute-start | bytes 230408 | tf_op jit(solution)/shard_map/ppermute | solution.py:422
  10.2 0.2 collective-permute-start.3
  10.4 0.0 copy-done
  10.4 0.1 constant_dynamic-slice_fusion.meas_ref
  10.5 1.6 %tables.1 = (bf16[4,256,384]{2,1,0:T(8,128)(2,1)S(1)}, bf16[4,128,256]{2,1,0:T(8,128)(2,1)S(1)}, f32[4,128,1]{2,1,0:T(8,128)S(1)}, f32[4,8,256]{2,1,0:T(8,128)S(1)}) custom-call(s32[1]{0:T(128)} %bitcast.1.strip_ref, s32[4]{0:T(128)} %radius_hbm.3, s32[4,15]{1,0:T(4,128)} %phase_hbm.3, f32[4,31]{1,0:T(4,128)} %row_hbm.3, f32[15,4,31]{2,1,0:T(4,128)} %bitcast.14, ...), custom_call_target="tpu_custom_call" | custom-call | bytes 6000000 | tf_op jit(solution)/shard_map/tables/pallas_call | solution.py:322
  12.1 0.0 collective-permute-done.1.refs_0_
  12.1 0.1 collective-permute-done.2.refs_1_
  12.2 2.1 %collective-permute-done.3.refs_2_ = bf16[160,240]{1,0:T(8,128)(2,1)S(1)} collective-permute-done((bf16[160,240]{1,0:T(8,128)(2,1)S(1)}, bf16[160,240]{1,0:T(8,128)(2,1)S(1)}, u32[]{:S(2)}, u32[]{:S(2)}) %collective-permute-start.3) | collective-permute-done | bytes 76832 | tf_op jit(solution)/shard_map/ppermute | solution.py:422
  14.4 1.4 %collective-permute-start.4 = (bf16[64,240]{1,0:T(8,128)(2,1)S(1)}, bf16[64,240]{1,0:T(8,128)(2,1)S(1)}, u32[]{:S(2)}, u32[]{:S(2)}) collective-permute-start(bf16[64,240]{1,0:T(8,128)(2,1)S(1)} %get-tuple-element.38), channel_id=1, source_target_pairs={{0,1},{2,3},{1,0},{3,2},{4,5},{6,7},{5,4},{7,6},{8,9},{10,11},{9,8... | collective-permute-start | bytes 92168 | tf_op jit(solution)/shard_map/ppermute | solution.py:430
  15.8 1.9 %collective-permute-start.5 = (bf16[64,240]{1,0:T(8,128)(2,1)S(1)}, bf16[64,240]{1,0:T(8,128)(2,1)S(1)}, u32[]{:S(2)}, u32[]{:S(2)}) collective-permute-start(bf16[64,240]{1,0:T(8,128)(2,1)S(1)} %get-tuple-element.39), channel_id=1, source_target_pairs={{1,2},{2,1},{5,6},{6,5},{9,10},{10,9},{13,14},{14,13},{17,18},{18,... | collective-permute-start | bytes 92168 | tf_op jit(solution)/shard_map/ppermute | solution.py:430
  17.7 0.0 collective-permute-done.4.first_ref
  17.7 2.7 %collective-permute-done.5.second_ref = bf16[64,240]{1,0:T(8,128)(2,1)S(1)} collective-permute-done((bf16[64,240]{1,0:T(8,128)(2,1)S(1)}, bf16[64,240]{1,0:T(8,128)(2,1)S(1)}, u32[]{:S(2)}, u32[]{:S(2)}) %collective-permute-start.5) | collective-permute-done | bytes 30752 | tf_op jit(solution)/shard_map/ppermute | solution.py:430
  20.4 0.1 ratio.2
  20.5 0.6 collective-permute-start.8
  21.1 1.2 %collective-permute-start.7 = (bf16[160,240]{1,0:T(8,128)(2,1)S(1)}, bf16[160,240]{1,0:T(8,128)(2,1)S(1)}, u32[]{:S(2)}, u32[]{:S(2)}) collective-permute-start(bf16[160,240]{1,0:T(8,128)(2,1)S(1)} %ratio.2), channel_id=1, source_target_pairs={{0,16},{4,20},{8,24},{12,28},{16,0},{20,4},{24,8},{28,12},{1,17},{... | collective-permute-start | bytes 230408 | tf_op jit(solution)/shard_map/ppermute | solution.py:439
  22.3 0.9 %collective-permute-start.6 = (bf16[160,240]{1,0:T(8,128)(2,1)S(1)}, bf16[160,240]{1,0:T(8,128)(2,1)S(1)}, u32[]{:S(2)}, u32[]{:S(2)}) collective-permute-start(bf16[160,240]{1,0:T(8,128)(2,1)S(1)} %ratio.2), channel_id=1, source_target_pairs={{0,8},{4,12},{8,0},{12,4},{16,24},{20,28},{24,16},{28,20},{1,9},{5... | collective-permute-start | bytes 230408 | tf_op jit(solution)/shard_map/ppermute | solution.py:439
  23.2 1.6 %collective-permute-done.8 = bf16[160,240]{1,0:T(8,128)(2,1)S(1)} collective-permute-done((bf16[160,240]{1,0:T(8,128)(2,1)S(1)}, bf16[160,240]{1,0:T(8,128)(2,1)S(1)}, u32[]{:S(2)}, u32[]{:S(2)}) %collective-permute-start.8) | collective-permute-done | bytes 76832 | tf_op jit(solution)/shard_map/ppermute | solution.py:439
  24.9 0.4 collective-permute-done.7
  25.3 0.3 collective-permute-done.6
  25.6 0.1 pad_maximum_fusion.same_ref
  25.7 5.0 %collective-permute-start.9 = (bf16[4,160,240]{2,1,0:T(8,128)(2,1)S(1)}, bf16[4,160,240]{2,1,0:T(8,128)(2,1)S(1)}, u32[]{:S(2)}, u32[]{:S(2)}) collective-permute-start(bf16[4,160,240]{2,1,0:T(8,128)(2,1)S(1)} %pad_maximum_fusion.same_ref), channel_id=1, source_target_pairs={{0,4},{4,0},{8,12},{12,8},{16,20},{20,16},{24,28},{28,24},{1,5},{5... | collective-permute-start | bytes 921608 | tf_op jit(solution)/shard_map/ppermute | solution.py:440
  30.6 1.3 %collective-permute-done.9.other_ref = bf16[4,160,240]{2,1,0:T(8,128)(2,1)S(1)} collective-permute-done((bf16[4,160,240]{2,1,0:T(8,128)(2,1)S(1)}, bf16[4,160,240]{2,1,0:T(8,128)(2,1)S(1)}, u32[]{:S(2)}, u32[]{:S(2)}) %collective-permute-start.9) | collective-permute-done | bytes 307232 | tf_op jit(solution)/shard_map/ppermute | solution.py:440
  31.9 10.3 %middle.1 = (f32[4,8,120,240]{3,2,1,0:T(8,128)S(1)}, f32[4,160,240]{2,1,0:T(8,128)S(1)}, bf16[4,160,240]{2,1,0:T(8,128)(2,1)S(1)}) custom-call(s32[1]{0:T(128)} %bitcast.me_ref, bf16[4,160,240]{2,1,0:T(8,128)(2,1)S(1)} %pad_maximum_fusion.same_ref, bf16[4,160,240]{2,1,0:T(8,128)(2,1)S(1)} %collective-permute-done.9.other_ref, ...), custom_call_target="tpu_custom_call" | custom-call | bytes 15000000 | tf_op jit(solution)/shard_map/middle/pallas_call | solution.py:322
  42.3 0.5 collective-permute-start.10
  42.8 1.3 %collective-permute-done.10.recv_ref = bf16[4,160,240]{2,1,0:T(8,128)(2,1)S(1)} collective-permute-done((bf16[4,160,240]{2,1,0:T(8,128)(2,1)S(1)}, bf16[4,160,240]{2,1,0:T(8,128)(2,1)S(1)}, u32[]{:S(2)}, u32[]{:S(2)}) %collective-permute-start.10) | collective-permute-done | bytes 307232 | tf_op jit(solution)/shard_map/ppermute | solution.py:399
  44.0 0.1 core_sum.3
  44.1 1.2 %collective-permute-start.11 = (bf16[160,240]{1,0:T(8,128)(2,1)S(1)}, bf16[160,240]{1,0:T(8,128)(2,1)S(1)}, u32[]{:S(2)}, u32[]{:S(2)}) collective-permute-start(bf16[160,240]{1,0:T(8,128)(2,1)S(1)} %get-tuple-element.48), channel_id=1, source_target_pairs={{0,8},{4,12},{8,0},{12,4},{16,24},{20,28},{24,16},{28,20},{1,9},{5... | collective-permute-start | bytes 230408 | tf_op jit(solution)/shard_map/ppermute | solution.py:422
  45.3 0.6 collective-permute-start.12
  45.9 0.9 %collective-permute-start.13 = (bf16[160,240]{1,0:T(8,128)(2,1)S(1)}, bf16[160,240]{1,0:T(8,128)(2,1)S(1)}, u32[]{:S(2)}, u32[]{:S(2)}) collective-permute-start(bf16[160,240]{1,0:T(8,128)(2,1)S(1)} %get-tuple-element.50), channel_id=1, source_target_pairs={{0,24},{4,28},{8,16},{12,20},{16,8},{20,12},{24,0},{28,4},{1,25},{... | collective-permute-start | bytes 230408 | tf_op jit(solution)/shard_map/ppermute | solution.py:422
  46.8 1.0 %collective-permute-done.11.refs_0_ = bf16[160,240]{1,0:T(8,128)(2,1)S(1)} collective-permute-done((bf16[160,240]{1,0:T(8,128)(2,1)S(1)}, bf16[160,240]{1,0:T(8,128)(2,1)S(1)}, u32[]{:S(2)}, u32[]{:S(2)}) %collective-permute-start.11) | collective-permute-done | bytes 76832 | tf_op jit(solution)/shard_map/ppermute | solution.py:422
  47.8 0.8 %collective-permute-done.12.refs_1_ = bf16[160,240]{1,0:T(8,128)(2,1)S(1)} collective-permute-done((bf16[160,240]{1,0:T(8,128)(2,1)S(1)}, bf16[160,240]{1,0:T(8,128)(2,1)S(1)}, u32[]{:S(2)}, u32[]{:S(2)}) %collective-permute-start.12) | collective-permute-done | bytes 76832 | tf_op jit(solution)/shard_map/ppermute | solution.py:422
  48.6 1.6 %collective-permute-done.13.refs_2_ = bf16[160,240]{1,0:T(8,128)(2,1)S(1)} collective-permute-done((bf16[160,240]{1,0:T(8,128)(2,1)S(1)}, bf16[160,240]{1,0:T(8,128)(2,1)S(1)}, u32[]{:S(2)}, u32[]{:S(2)}) %collective-permute-start.13) | collective-permute-done | bytes 76832 | tf_op jit(solution)/shard_map/ppermute | solution.py:422
  50.2 0.1 chip_sum.3
  50.2 0.1 collective-permute-start.14
  50.3 1.9 %collective-permute-start.15 = (bf16[64,240]{1,0:T(8,128)(2,1)S(1)}, bf16[64,240]{1,0:T(8,128)(2,1)S(1)}, u32[]{:S(2)}, u32[]{:S(2)}) collective-permute-start(bf16[64,240]{1,0:T(8,128)(2,1)S(1)} %get-tuple-element.53), channel_id=1, source_target_pairs={{1,2},{2,1},{5,6},{6,5},{9,10},{10,9},{13,14},{14,13},{17,18},{18,... | collective-permute-start | bytes 92168 | tf_op jit(solution)/shard_map/ppermute | solution.py:430
  52.2 0.8 %collective-permute-done.14.first_ref = bf16[64,240]{1,0:T(8,128)(2,1)S(1)} collective-permute-done((bf16[64,240]{1,0:T(8,128)(2,1)S(1)}, bf16[64,240]{1,0:T(8,128)(2,1)S(1)}, u32[]{:S(2)}, u32[]{:S(2)}) %collective-permute-start.14) | collective-permute-done | bytes 30752 | tf_op jit(solution)/shard_map/ppermute | solution.py:430
  53.1 1.9 %collective-permute-done.15.second_ref = bf16[64,240]{1,0:T(8,128)(2,1)S(1)} collective-permute-done((bf16[64,240]{1,0:T(8,128)(2,1)S(1)}, bf16[64,240]{1,0:T(8,128)(2,1)S(1)}, u32[]{:S(2)}, u32[]{:S(2)}) %collective-permute-start.15) | collective-permute-done | bytes 30752 | tf_op jit(solution)/shard_map/ppermute | solution.py:430
  55.0 0.1 ratio.3
  55.0 1.1 %collective-permute-start.18 = (bf16[160,240]{1,0:T(8,128)(2,1)S(1)}, bf16[160,240]{1,0:T(8,128)(2,1)S(1)}, u32[]{:S(2)}, u32[]{:S(2)}) collective-permute-start(bf16[160,240]{1,0:T(8,128)(2,1)S(1)} %ratio.3), channel_id=1, source_target_pairs={{0,24},{4,28},{8,16},{12,20},{16,8},{20,12},{24,0},{28,4},{1,25},{... | collective-permute-start | bytes 230408 | tf_op jit(solution)/shard_map/ppermute | solution.py:439
  56.2 0.9 %collective-permute-start.17 = (bf16[160,240]{1,0:T(8,128)(2,1)S(1)}, bf16[160,240]{1,0:T(8,128)(2,1)S(1)}, u32[]{:S(2)}, u32[]{:S(2)}) collective-permute-start(bf16[160,240]{1,0:T(8,128)(2,1)S(1)} %ratio.3), channel_id=1, source_target_pairs={{0,16},{4,20},{8,24},{12,28},{16,0},{20,4},{24,8},{28,12},{1,17},{... | collective-permute-start | bytes 230408 | tf_op jit(solution)/shard_map/ppermute | solution.py:439
  57.1 0.7 collective-permute-start.16
  57.8 1.6 %collective-permute-done.18 = bf16[160,240]{1,0:T(8,128)(2,1)S(1)} collective-permute-done((bf16[160,240]{1,0:T(8,128)(2,1)S(1)}, bf16[160,240]{1,0:T(8,128)(2,1)S(1)}, u32[]{:S(2)}, u32[]{:S(2)}) %collective-permute-start.18) | collective-permute-done | bytes 76832 | tf_op jit(solution)/shard_map/ppermute | solution.py:439
  59.4 0.8 %collective-permute-done.17 = bf16[160,240]{1,0:T(8,128)(2,1)S(1)} collective-permute-done((bf16[160,240]{1,0:T(8,128)(2,1)S(1)}, bf16[160,240]{1,0:T(8,128)(2,1)S(1)}, u32[]{:S(2)}, u32[]{:S(2)}) %collective-permute-start.17) | collective-permute-done | bytes 76832 | tf_op jit(solution)/shard_map/ppermute | solution.py:439
  60.2 0.2 collective-permute-done.16
  60.4 0.1 pad_maximum_fusion.1.same_ref
  60.5 4.4 %collective-permute-start.19 = (bf16[4,160,240]{2,1,0:T(8,128)(2,1)S(1)}, bf16[4,160,240]{2,1,0:T(8,128)(2,1)S(1)}, u32[]{:S(2)}, u32[]{:S(2)}) collective-permute-start(bf16[4,160,240]{2,1,0:T(8,128)(2,1)S(1)} %pad_maximum_fusion.1.same_ref), channel_id=1, source_target_pairs={{0,4},{4,0},{8,12},{12,8},{16,20},{20,16},{24,28},{28,24},{1,5},{5... | collective-permute-start | bytes 921608 | tf_op jit(solution)/shard_map/ppermute | solution.py:440
  64.9 1.3 %collective-permute-done.19.other_ref = bf16[4,160,240]{2,1,0:T(8,128)(2,1)S(1)} collective-permute-done((bf16[4,160,240]{2,1,0:T(8,128)(2,1)S(1)}, bf16[4,160,240]{2,1,0:T(8,128)(2,1)S(1)}, u32[]{:S(2)}, u32[]{:S(2)}) %collective-permute-start.19) | collective-permute-done | bytes 307232 | tf_op jit(solution)/shard_map/ppermute | solution.py:440
  66.1 6.5 %last.1 = f32[4,120,1920]{2,1,0:T(8,128)} custom-call(s32[1]{0:T(128)} %bitcast.me_ref, bf16[4,160,240]{2,1,0:T(8,128)(2,1)S(1)} %pad_maximum_fusion.1.same_ref, bf16[4,160,240]{2,1,0:T(8,128)(2,1)S(1)} %collective-permute-done.19.other_ref, bf16[4,256,384]{2,1,0:T(8,128)(2,1)S(1)} %get-tuple-element.40.bt_ref, ...), custom_call_target="tpu_custom_call" | custom-call | bytes 15000000 | tf_op jit(solution)/shard_map/last/pallas_call | solution.py:322
  (1 shorter events, 0.0 us)
Async XLA Ops:
  0.0 10.4 %copy-start = (f32[120,1920]{1,0:T(8,128)S(1)}, f32[120,1920]{1,0:T(8,128)}, u32[]{:S(2)}) copy-start(f32[120,1920]{1,0:T(8,128)} %param.7) | copy-start | bytes 2764804
  5.6 2.0 %collective-permute-start = (bf16[4,160,240]{2,1,0:T(8,128)(2,1)S(1)}, bf16[4,160,240]{2,1,0:T(8,128)(2,1)S(1)}, u32[]{:S(2)}, u32[]{:S(2)}) collective-permute-start(bf16[4,160,240]{2,1,0:T(8,128)(2,1)S(1)} %get-tuple-element.31), channel_id=1, source_target_pairs={{0,4},{4,0},{8,12},{12,8},{16,20},{20,16},{24,28},{28,24},{1,5},{5... | collective-permute-start | bytes 921608 | tf_op jit(solution)/shard_map/ppermute | solution.py:399
  7.6 4.5 %collective-permute-start.1 = (bf16[160,240]{1,0:T(8,128)(2,1)S(1)}, bf16[160,240]{1,0:T(8,128)(2,1)S(1)}, u32[]{:S(2)}, u32[]{:S(2)}) collective-permute-start(bf16[160,240]{1,0:T(8,128)(2,1)S(1)} %get-tuple-element.34), channel_id=1, source_target_pairs={{0,8},{4,12},{8,0},{12,4},{16,24},{20,28},{24,16},{28,20},{1,9},{5... | collective-permute-start | bytes 230408 | tf_op jit(solution)/shard_map/ppermute | solution.py:422
  8.9 3.3 %collective-permute-start.2 = (bf16[160,240]{1,0:T(8,128)(2,1)S(1)}, bf16[160,240]{1,0:T(8,128)(2,1)S(1)}, u32[]{:S(2)}, u32[]{:S(2)}) collective-permute-start(bf16[160,240]{1,0:T(8,128)(2,1)S(1)} %get-tuple-element.35), channel_id=1, source_target_pairs={{0,16},{4,20},{8,24},{12,28},{16,0},{20,4},{24,8},{28,12},{1,17},{... | collective-permute-start | bytes 230408 | tf_op jit(solution)/shard_map/ppermute | solution.py:422
  10.2 4.2 %collective-permute-start.3 = (bf16[160,240]{1,0:T(8,128)(2,1)S(1)}, bf16[160,240]{1,0:T(8,128)(2,1)S(1)}, u32[]{:S(2)}, u32[]{:S(2)}) collective-permute-start(bf16[160,240]{1,0:T(8,128)(2,1)S(1)} %get-tuple-element.36), channel_id=1, source_target_pairs={{0,24},{4,28},{8,16},{12,20},{16,8},{20,12},{24,0},{28,4},{1,25},{... | collective-permute-start | bytes 230408 | tf_op jit(solution)/shard_map/ppermute | solution.py:422
  14.4 3.3 %collective-permute-start.4 = (bf16[64,240]{1,0:T(8,128)(2,1)S(1)}, bf16[64,240]{1,0:T(8,128)(2,1)S(1)}, u32[]{:S(2)}, u32[]{:S(2)}) collective-permute-start(bf16[64,240]{1,0:T(8,128)(2,1)S(1)} %get-tuple-element.38), channel_id=1, source_target_pairs={{0,1},{2,3},{1,0},{3,2},{4,5},{6,7},{5,4},{7,6},{8,9},{10,11},{9,8... | collective-permute-start | bytes 92168 | tf_op jit(solution)/shard_map/ppermute | solution.py:430
  15.8 4.6 %collective-permute-start.5 = (bf16[64,240]{1,0:T(8,128)(2,1)S(1)}, bf16[64,240]{1,0:T(8,128)(2,1)S(1)}, u32[]{:S(2)}, u32[]{:S(2)}) collective-permute-start(bf16[64,240]{1,0:T(8,128)(2,1)S(1)} %get-tuple-element.39), channel_id=1, source_target_pairs={{1,2},{2,1},{5,6},{6,5},{9,10},{10,9},{13,14},{14,13},{17,18},{18,... | collective-permute-start | bytes 92168 | tf_op jit(solution)/shard_map/ppermute | solution.py:430
  20.5 4.4 %collective-permute-start.8 = (bf16[160,240]{1,0:T(8,128)(2,1)S(1)}, bf16[160,240]{1,0:T(8,128)(2,1)S(1)}, u32[]{:S(2)}, u32[]{:S(2)}) collective-permute-start(bf16[160,240]{1,0:T(8,128)(2,1)S(1)} %ratio.2), channel_id=1, source_target_pairs={{0,24},{4,28},{8,16},{12,20},{16,8},{20,12},{24,0},{28,4},{1,25},{... | collective-permute-start | bytes 230408 | tf_op jit(solution)/shard_map/ppermute | solution.py:439
  21.1 4.2 %collective-permute-start.7 = (bf16[160,240]{1,0:T(8,128)(2,1)S(1)}, bf16[160,240]{1,0:T(8,128)(2,1)S(1)}, u32[]{:S(2)}, u32[]{:S(2)}) collective-permute-start(bf16[160,240]{1,0:T(8,128)(2,1)S(1)} %ratio.2), channel_id=1, source_target_pairs={{0,16},{4,20},{8,24},{12,28},{16,0},{20,4},{24,8},{28,12},{1,17},{... | collective-permute-start | bytes 230408 | tf_op jit(solution)/shard_map/ppermute | solution.py:439
  22.3 3.3 %collective-permute-start.6 = (bf16[160,240]{1,0:T(8,128)(2,1)S(1)}, bf16[160,240]{1,0:T(8,128)(2,1)S(1)}, u32[]{:S(2)}, u32[]{:S(2)}) collective-permute-start(bf16[160,240]{1,0:T(8,128)(2,1)S(1)} %ratio.2), channel_id=1, source_target_pairs={{0,8},{4,12},{8,0},{12,4},{16,24},{20,28},{24,16},{28,20},{1,9},{5... | collective-permute-start | bytes 230408 | tf_op jit(solution)/shard_map/ppermute | solution.py:439
  25.7 6.2 %collective-permute-start.9 = (bf16[4,160,240]{2,1,0:T(8,128)(2,1)S(1)}, bf16[4,160,240]{2,1,0:T(8,128)(2,1)S(1)}, u32[]{:S(2)}, u32[]{:S(2)}) collective-permute-start(bf16[4,160,240]{2,1,0:T(8,128)(2,1)S(1)} %pad_maximum_fusion.same_ref), channel_id=1, source_target_pairs={{0,4},{4,0},{8,12},{12,8},{16,20},{20,16},{24,28},{28,24},{1,5},{5... | collective-permute-start | bytes 921608 | tf_op jit(solution)/shard_map/ppermute | solution.py:440
  42.3 1.8 %collective-permute-start.10 = (bf16[4,160,240]{2,1,0:T(8,128)(2,1)S(1)}, bf16[4,160,240]{2,1,0:T(8,128)(2,1)S(1)}, u32[]{:S(2)}, u32[]{:S(2)}) collective-permute-start(bf16[4,160,240]{2,1,0:T(8,128)(2,1)S(1)} %get-tuple-element.46), channel_id=1, source_target_pairs={{0,4},{4,0},{8,12},{12,8},{16,20},{20,16},{24,28},{28,24},{1,5},{5... | collective-permute-start | bytes 921608 | tf_op jit(solution)/shard_map/ppermute | solution.py:399
  44.1 3.7 %collective-permute-start.11 = (bf16[160,240]{1,0:T(8,128)(2,1)S(1)}, bf16[160,240]{1,0:T(8,128)(2,1)S(1)}, u32[]{:S(2)}, u32[]{:S(2)}) collective-permute-start(bf16[160,240]{1,0:T(8,128)(2,1)S(1)} %get-tuple-element.48), channel_id=1, source_target_pairs={{0,8},{4,12},{8,0},{12,4},{16,24},{20,28},{24,16},{28,20},{1,9},{5... | collective-permute-start | bytes 230408 | tf_op jit(solution)/shard_map/ppermute | solution.py:422
  45.3 3.3 %collective-permute-start.12 = (bf16[160,240]{1,0:T(8,128)(2,1)S(1)}, bf16[160,240]{1,0:T(8,128)(2,1)S(1)}, u32[]{:S(2)}, u32[]{:S(2)}) collective-permute-start(bf16[160,240]{1,0:T(8,128)(2,1)S(1)} %get-tuple-element.49), channel_id=1, source_target_pairs={{0,16},{4,20},{8,24},{12,28},{16,0},{20,4},{24,8},{28,12},{1,17},{... | collective-permute-start | bytes 230408 | tf_op jit(solution)/shard_map/ppermute | solution.py:422
  45.9 4.3 %collective-permute-start.13 = (bf16[160,240]{1,0:T(8,128)(2,1)S(1)}, bf16[160,240]{1,0:T(8,128)(2,1)S(1)}, u32[]{:S(2)}, u32[]{:S(2)}) collective-permute-start(bf16[160,240]{1,0:T(8,128)(2,1)S(1)} %get-tuple-element.50), channel_id=1, source_target_pairs={{0,24},{4,28},{8,16},{12,20},{16,8},{20,12},{24,0},{28,4},{1,25},{... | collective-permute-start | bytes 230408 | tf_op jit(solution)/shard_map/ppermute | solution.py:422
  50.2 2.8 %collective-permute-start.14 = (bf16[64,240]{1,0:T(8,128)(2,1)S(1)}, bf16[64,240]{1,0:T(8,128)(2,1)S(1)}, u32[]{:S(2)}, u32[]{:S(2)}) collective-permute-start(bf16[64,240]{1,0:T(8,128)(2,1)S(1)} %get-tuple-element.52), channel_id=1, source_target_pairs={{0,1},{2,3},{1,0},{3,2},{4,5},{6,7},{5,4},{7,6},{8,9},{10,11},{9,8... | collective-permute-start | bytes 92168 | tf_op jit(solution)/shard_map/ppermute | solution.py:430
  50.3 4.7 %collective-permute-start.15 = (bf16[64,240]{1,0:T(8,128)(2,1)S(1)}, bf16[64,240]{1,0:T(8,128)(2,1)S(1)}, u32[]{:S(2)}, u32[]{:S(2)}) collective-permute-start(bf16[64,240]{1,0:T(8,128)(2,1)S(1)} %get-tuple-element.53), channel_id=1, source_target_pairs={{1,2},{2,1},{5,6},{6,5},{9,10},{10,9},{13,14},{14,13},{17,18},{18,... | collective-permute-start | bytes 92168 | tf_op jit(solution)/shard_map/ppermute | solution.py:430
  55.0 4.3 %collective-permute-start.18 = (bf16[160,240]{1,0:T(8,128)(2,1)S(1)}, bf16[160,240]{1,0:T(8,128)(2,1)S(1)}, u32[]{:S(2)}, u32[]{:S(2)}) collective-permute-start(bf16[160,240]{1,0:T(8,128)(2,1)S(1)} %ratio.3), channel_id=1, source_target_pairs={{0,24},{4,28},{8,16},{12,20},{16,8},{20,12},{24,0},{28,4},{1,25},{... | collective-permute-start | bytes 230408 | tf_op jit(solution)/shard_map/ppermute | solution.py:439
  56.2 4.0 %collective-permute-start.17 = (bf16[160,240]{1,0:T(8,128)(2,1)S(1)}, bf16[160,240]{1,0:T(8,128)(2,1)S(1)}, u32[]{:S(2)}, u32[]{:S(2)}) collective-permute-start(bf16[160,240]{1,0:T(8,128)(2,1)S(1)} %ratio.3), channel_id=1, source_target_pairs={{0,16},{4,20},{8,24},{12,28},{16,0},{20,4},{24,8},{28,12},{1,17},{... | collective-permute-start | bytes 230408 | tf_op jit(solution)/shard_map/ppermute | solution.py:439
  57.1 3.3 %collective-permute-start.16 = (bf16[160,240]{1,0:T(8,128)(2,1)S(1)}, bf16[160,240]{1,0:T(8,128)(2,1)S(1)}, u32[]{:S(2)}, u32[]{:S(2)}) collective-permute-start(bf16[160,240]{1,0:T(8,128)(2,1)S(1)} %ratio.3), channel_id=1, source_target_pairs={{0,8},{4,12},{8,0},{12,4},{16,24},{20,28},{24,16},{28,20},{1,9},{5... | collective-permute-start | bytes 230408 | tf_op jit(solution)/shard_map/ppermute | solution.py:439
  60.5 5.7 %collective-permute-start.19 = (bf16[4,160,240]{2,1,0:T(8,128)(2,1)S(1)}, bf16[4,160,240]{2,1,0:T(8,128)(2,1)S(1)}, u32[]{:S(2)}, u32[]{:S(2)}) collective-permute-start(bf16[4,160,240]{2,1,0:T(8,128)(2,1)S(1)} %pad_maximum_fusion.1.same_ref), channel_id=1, source_target_pairs={{0,4},{4,0},{8,12},{12,8},{16,20},{20,16},{24,28},{28,24},{1,5},{5... | collective-permute-start | bytes 921608 | tf_op jit(solution)/shard_map/ppermute | solution.py:440

commit v2 on v1

v2 whole, which is shorter than its diff:
```python
import functools

import jax
import jax.numpy as jnp
from jax import lax
from jax.experimental import pallas as pl
from jax.experimental.pallas import tpu as pltpu
from jax.sharding import PartitionSpec as P

RMAX = 15
ITERS = 2
SIDE = 16
LANES = 128

F32 = jnp.float32
BF16 = jnp.bfloat16


def round_up(value, step):
    return -(-value // step) * step


class Sizes:
    def __init__(self, planes, rows, strips, cols, devices, pitch):
        self.total = rows * strips
        self.planes, self.rows, self.cols, self.n, self.pitch = planes, rows, cols, devices, pitch
        self.w = cols // devices
        self.half = devices // 2
        assert cols % devices == 0 and self.w % pitch == 0 and self.w >= 2 * SIDE
        assert devices >= 2 and devices & (devices - 1) == 0 and rows >= 2 * RMAX and rows % 8 == 0
        self.wl = round_up(self.w, LANES)
        self.span = self.w + 2 * SIDE
        self.kp = round_up(self.span, LANES)
        self.kb = self.wl + 2 * LANES
        self.rp = round_up(rows, LANES)
        self.e = rows + 2 * RMAX
        self.ep = round_up(self.e, 32)
        self.el = round_up(self.ep, LANES)
        self.ar = round_up(max(self.span, self.wl) + pitch, pitch)
        self.starts = [LANES + b * self.w - SIDE for b in range(devices)]
        self.ka = round_up(max(s % LANES for s in self.starts) + self.span, LANES)
        self.xw = max(s // LANES * LANES for s in self.starts) + self.ka


def iota(shape, axis):
    return lax.broadcasted_iota(jnp.int32, shape, axis)


def phase_rows(sz, z, phase_ref, col_ref, t_ref, a_ref):
    taps = col_ref.shape[2]
    t_ref[...] = jnp.zeros_like(t_ref)
    for p in range(sz.pitch):
        row = col_ref[phase_ref[z, p], pl.ds(z, 1), :]
        t_ref[p : p + 1, 0:taps] = row.astype(BF16).astype(F32)
    base = t_ref[0 : sz.pitch, :]
    for k in range(sz.ar // sz.pitch):
        a_ref[k * sz.pitch : (k + 1) * sz.pitch, :] = base


def spread_matrix(sz, reach, a_ref):
    first = (-SIDE) % sz.pitch
    rows = a_ref[first : first + sz.span, 0 : sz.wl]
    rows = pltpu.roll(rows, sz.wl - RMAX - SIDE, 1, stride=1, stride_axis=0)
    col, row = iota(rows.shape, 1), iota(rows.shape, 0)
    return jnp.where((jnp.abs(col - row + SIDE) <= reach) & (col < sz.w), rows, 0.0)


def gather_matrix(sz, reach, a_ref):
    rows = pltpu.roll(a_ref[0 : sz.wl, 0 : sz.kp], SIDE - RMAX, 1, stride=1, stride_axis=0)
    col, row = iota(rows.shape, 1), iota(rows.shape, 0)
    rows = jnp.where((jnp.abs(col - SIDE - row) <= reach) & (row < sz.w), rows, 0.0)
    return rows.T[0 : sz.span, :]


def by_block(sz, matrix):
    def zeros(count):
        return [jnp.zeros((count, sz.wl), F32)] if count else []

    lead = sz.w - (sz.wl - LANES) - SIDE
    parts = [matrix[SIDE : SIDE + sz.w]] + zeros(sz.wl - sz.w)
    parts += [matrix[SIDE + sz.w :]] + zeros(LANES - SIDE)
    parts += zeros(lead) + [matrix[0:SIDE]] + zeros(sz.wl - sz.w)
    return jnp.concatenate(parts, axis=0).astype(BF16)


def row_matrix(sz, z, reach, row_ref):
    taps = row_ref.shape[1]
    lane = iota((1, sz.el), 1)
    row = row_ref[pl.ds(z, 1), :].astype(BF16).astype(F32)
    row = jnp.concatenate([row, jnp.zeros((1, sz.el - taps), F32)], axis=1)
    row = jnp.where(jnp.abs(lane - RMAX) <= reach, row, 0.0)
    wide = jnp.broadcast_to(row, (sz.rp, sz.el))
    wide = pltpu.roll(wide, 0, 1, stride=1, stride_axis=0)
    return jnp.where(iota(wide.shape, 0) < sz.rows, wide, 0.0)


def side_by_side(sz, ref, b, height):
    at = (b + 1) * height
    here = ref[at : at + height, :]
    after = ref[at + height : at + 2 * height, 0:LANES]
    before = ref[at - height : at, sz.wl - LANES :]
    return jnp.concatenate([here, after, before], axis=1)


def rows_forward(sz, me, rc_ref, s_ref, keep_ref, send_ref):
    core = lax.rem(me, 2)
    coef = rc_ref[...]
    for k in range(sz.half):
        for ref, block in ((send_ref, 2 * k + 1 - core), (keep_ref, 2 * k + core)):
            out = jnp.dot(coef, s_ref[block], preferred_element_type=F32)
            ref[k] = out.astype(ref.dtype)


def backward(sz, ratio_ref, matrix, rt, g_ref):
    for b in range(sz.n):
        window = side_by_side(sz, ratio_ref, b, sz.ep)
        out = jnp.dot(window, matrix, preferred_element_type=F32)
        g_ref[b, 0 : sz.ep, :] = out.astype(BF16)
    for b in range(sz.n):
        back = jnp.dot(rt, g_ref[b], preferred_element_type=F32)
        yield b, back[0 : sz.rows, :]


def block_norm(sz, b, icn):
    kind = 1 if b == 0 else 2 if b == sz.n - 1 else 0
    return icn[kind : kind + 1, :]


def place_ratio(sz, me, same_ref, other_ref, ratio_ref, g_ref):
    empty = jnp.zeros((sz.ep, sz.wl), BF16)
    ratio_ref[0 : sz.ep, :] = empty
    ratio_ref[(sz.n + 1) * sz.ep :, :] = empty
    g_ref[:, sz.ep :, :] = jnp.zeros((sz.n, sz.el - sz.ep, sz.wl), BF16)
    core = lax.rem(me, 2)
    for j in range(sz.half):
        chip = (me // 2) ^ j
        for ref, b in ((same_ref, 2 * chip + core), (other_ref, 2 * chip + 1 - core)):
            ratio_ref[pl.ds(pl.multiple_of((b + 1) * sz.ep, sz.ep), sz.ep), :] = ref[j]


def first_kernel(
    sz, me_ref, radius_hbm, phase_hbm, row_hbm, col_hbm, vol_hbm,
    rc_ref, keep_ref, send_ref,
    radius_ref, phase_ref, row_ref, col_ref, vol_ref, t_ref, a_ref, m_ref, x_ref, s_ref, sems,
):
    pairs = ((radius_hbm, radius_ref), (phase_hbm, phase_ref), (row_hbm, row_ref), (col_hbm, col_ref))
    small = [pltpu.make_async_copy(a, b, sems.at[i]) for i, (a, b) in enumerate(pairs)]
    large = [
        pltpu.make_async_copy(vol_hbm.at[z], vol_ref.at[z], sems.at[4 + z])
        for z in range(sz.planes)
    ]
    for copy in small + large:
        copy.start()
    m_ref[...] = jnp.zeros_like(m_ref)
    x_ref[...] = jnp.zeros_like(x_ref)
    for copy in small:
        copy.wait()
    for z in range(sz.planes):
        reach = radius_ref[z]
        phase_rows(sz, z, phase_ref, col_ref, t_ref, a_ref)
        matrix = spread_matrix(sz, reach, a_ref)
        rest = jnp.zeros((round_up(sz.span, 16) - sz.span, sz.wl), F32)
        matrix = jnp.concatenate([matrix, rest], axis=0) if rest.shape[0] else matrix
        m_ref[z, LANES : LANES + matrix.shape[0], :] = matrix.astype(BF16)
        rt = row_matrix(sz, z, reach, row_ref)
        rc_ref[:, z * sz.rp : (z + 1) * sz.rp] = rt.T[0 : sz.ep, :].astype(BF16)
    for z in range(sz.planes):
        large[z].wait()
        x = jnp.concatenate([vol_ref[z], jnp.zeros((sz.rp - sz.rows, sz.cols), F32)], axis=0)
        x_ref[z, :, LANES : LANES + sz.cols] = x.astype(BF16)
        for b, start in enumerate(sz.starts):
            shift = start % LANES
            window = x_ref[z, :, start - shift : start - shift + sz.ka]
            matrix = m_ref[z, LANES - shift : LANES - shift + sz.ka, :]
            out = jnp.dot(window, matrix, preferred_element_type=F32)
            s_ref[b, z * sz.rp : (z + 1) * sz.rp, :] = out.astype(BF16)
    rows_forward(sz, me_ref[0], rc_ref, s_ref, keep_ref, send_ref)


def table_kernel(
    sz, strip_ref, radius_hbm, phase_hbm, row_hbm, col_hbm, after_ref,
    wf_ref, wb_ref, rt_ref, irn_ref, icn_ref,
    radius_ref, phase_ref, row_ref, col_ref, t_ref, a_ref, sems,
):
    pairs = ((radius_hbm, radius_ref), (phase_hbm, phase_ref), (row_hbm, row_ref), (col_hbm, col_ref))
    small = [pltpu.make_async_copy(a, b, sems.at[i]) for i, (a, b) in enumerate(pairs)]
    for copy in small:
        copy.start()
    for copy in small:
        copy.wait()
    kind, col = iota((8, sz.kb), 0), iota((8, sz.kb), 1)
    after, before = (col >= sz.wl) & (col < sz.wl + LANES), col >= sz.wl + LANES
    ones = jnp.where(((kind == 1) & before) | ((kind == 2) & after), 0.0, 1.0).astype(BF16)
    for z in range(sz.planes):
        reach = radius_ref[z]
        phase_rows(sz, z, phase_ref, col_ref, t_ref, a_ref)
        wf_ref[z] = by_block(sz, spread_matrix(sz, reach, a_ref))
        matrix = by_block(sz, gather_matrix(sz, reach, a_ref))
        wb_ref[z] = matrix
        norm = jnp.dot(ones, matrix, preferred_element_type=F32)
        icn_ref[z] = jnp.where(norm > 0.0, 1.0 / norm, 0.0)
        rt = row_matrix(sz, z, reach, row_ref)
        rt_ref[z] = rt.astype(BF16)
        row = strip_ref[0] * sz.rows + iota(rt.shape, 1) - RMAX
        norm = jnp.sum(jnp.where((row >= 0) & (row < sz.total), rt, 0.0), axis=1, keepdims=True)
        irn_ref[z] = jnp.where(norm > 0.0, 1.0 / norm, 0.0)


def block_kernel(sz, vol_hbm, after_ref, blocks_ref, vol_ref, sems):
    copies = [
        pltpu.make_async_copy(vol_hbm.at[z], vol_ref.at[z], sems.at[z]) for z in range(sz.planes)
    ]
    for copy in copies:
        copy.start()
    for z, copy in enumerate(copies):
        copy.wait()
        for b in range(sz.n):
            block = vol_ref[z, :, b * sz.w : (b + 1) * sz.w]
            if sz.wl > sz.w:
                block = jnp.concatenate([block, jnp.zeros((sz.rows, sz.wl - sz.w), F32)], axis=1)
            blocks_ref[z, b] = block


def core_sum_kernel(sz, me_ref, keep_ref, recv_ref, own_ref, *out_refs):
    mine = me_ref[0] // 2
    own_ref[...] = keep_ref[mine] + recv_ref[mine].astype(F32)
    for j, ref in enumerate(out_refs, 1):
        other = mine ^ j
        ref[...] = (keep_ref[other] + recv_ref[other].astype(F32)).astype(BF16)


def chip_sum_kernel(sz, strip_ref, after_ref, own_ref, meas_ref, *refs):
    recv_refs, (sum_ref, first_ref, second_ref) = refs[:-3], refs[-3:]
    total = own_ref[...]
    for ref in recv_refs:
        total = total + ref[...].astype(F32)
    sum_ref[...] = total
    edges = []
    for first, row in ((0, 0), (sz.rows, sz.rows - SIDE)):
        meas = meas_ref[row : row + SIDE, :]
        high = meas.astype(BF16).astype(F32)
        edges.append(jnp.concatenate([total[first : first + 32, :], high, meas - high], axis=0))
    up, down = edges
    even = lax.rem(strip_ref[0], 2) == 0
    first_ref[...] = jnp.where(even, down, up).astype(BF16)
    second_ref[...] = jnp.where(even, up, down).astype(BF16)


def ratio_kernel(sz, strip_ref, sum_ref, meas_ref, first_ref, second_ref, ratio_ref, s_ref, m_ref):
    even = lax.rem(strip_ref[0], 2) == 0
    first, second = first_ref[...].astype(F32), second_ref[...].astype(F32)
    above, below = jnp.where(even, second, first), jnp.where(even, first, second)
    s_ref[...] = sum_ref[...]
    s_ref[0:32, :] += above[0:32, :]
    s_ref[sz.rows : sz.rows + 32, :] += below[0:32, :]
    m_ref[...] = jnp.zeros_like(m_ref)
    m_ref[RMAX : RMAX + sz.rows, :] = meas_ref[...]
    m_ref[0:RMAX, :] = (above[32:48, :] + above[48:64, :])[SIDE - RMAX :, :]
    m_ref[RMAX + sz.rows : sz.e, :] = (below[32:48, :] + below[48:64, :])[0:RMAX, :]
    row = iota(s_ref.shape, 0)
    spot = strip_ref[0] * sz.rows + row - RMAX
    inside = (row < sz.e) & (spot >= 0) & (spot < sz.total) & (iota(s_ref.shape, 1) < sz.w)
    ratio_ref[...] = jnp.where(inside, m_ref[...] / s_ref[...], 0.0).astype(BF16)


def stack_kernel(sz, after_ref, *refs):
    for j, ref in enumerate(refs[:-1]):
        refs[-1][j] = ref[...]


def middle_kernel(
    sz, me_ref, same_ref, other_ref, wf_ref, wb_ref, rt_ref, irn_ref, icn_ref, rc_ref, vol_ref,
    new_ref, keep_ref, send_ref, ratio_ref, g_ref, x_ref, s_ref,
):
    empty = jnp.zeros((sz.rp, sz.wl), BF16)
    x_ref[0 : sz.rp, :] = empty
    x_ref[(sz.n + 1) * sz.rp :, :] = empty
    place_ratio(sz, me_ref[0], same_ref, other_ref, ratio_ref, g_ref)
    lead = jnp.zeros((sz.rp - sz.rows, sz.wl), F32)

    def step(z, carry):
        icn, irn = icn_ref[z], irn_ref[z][0 : sz.rows]
        for b, back in backward(sz, ratio_ref, wb_ref[z], rt_ref[z], g_ref):
            new = vol_ref[z, b] * back * (irn * block_norm(sz, b, icn))
            new_ref[z, b] = new
            x_ref[(b + 1) * sz.rp : (b + 2) * sz.rp, :] = jnp.concatenate([new, lead]).astype(BF16)
        matrix = wf_ref[z]
        at = pl.ds(pl.multiple_of(z * sz.rp, sz.rp), sz.rp)
        for b in range(sz.n):
            window = side_by_side(sz, x_ref, b, sz.rp)
            out = jnp.dot(window, matrix, preferred_element_type=F32)
            s_ref[b, at, :] = out.astype(BF16)
        return carry

    for z in range(sz.planes):
        step(z, 0)
    rows_forward(sz, me_ref[0], rc_ref, s_ref, keep_ref, send_ref)


def last_kernel(
    sz, me_ref, same_ref, other_ref, wb_ref, rt_ref, irn_ref, icn_ref, vol_ref,
    out_hbm, ratio_ref, g_ref, out_ref, sems,
):
    place_ratio(sz, me_ref[0], same_ref, other_ref, ratio_ref, g_ref)

    def copy(z):
        return pltpu.make_async_copy(out_ref.at[z], out_hbm.at[z], sems.at[z])

    def step(z, carry):
        icn, irn = icn_ref[z], irn_ref[z][0 : sz.rows]
        for b, back in backward(sz, ratio_ref, wb_ref[z], rt_ref[z], g_ref):
            new = vol_ref[z, b] * back * (irn * block_norm(sz, b, icn))
            out_ref[z, :, b * sz.w : (b + 1) * sz.w] = new[:, 0 : sz.w]
        copy(z).start()
        return carry

    for z in range(sz.planes):
        step(z, 0)
    for z in range(sz.planes):
        copy(z).wait()


SMEM = pl.BlockSpec(memory_space=pltpu.SMEM)
VMEM = pl.BlockSpec(memory_space=pltpu.VMEM)
ANY = pl.BlockSpec(memory_space=pl.ANY)
HBM = pl.BlockSpec(memory_space=pltpu.HBM)


def shape(dims, dtype):
    return jax.ShapeDtypeStruct(dims, dtype)


def call(kernel, sz, name, in_specs, out_specs, out_shape, scratch, args, mib, micros=1):
    return pl.pallas_call(
        functools.partial(kernel, sz),
        in_specs=in_specs,
        out_specs=out_specs,
        out_shape=out_shape,
        scratch_shapes=scratch,
        compiler_params=pltpu.CompilerParams(vmem_limit_bytes=mib * 1024 * 1024),
        cost_estimate=pl.CostEstimate(
            flops=0, bytes_accessed=micros * 3_000_000, transcendentals=0
        ),
        name=name,
    )(*args)


def local(volume, measured, row_taps, col_taps, phase_map, radius):
    n = lax.axis_size("depth")
    strips = lax.axis_size("strip")
    planes, rows, cols = volume.shape
    sz = Sizes(planes, rows, strips, cols, n, phase_map.shape[1])
    me = lax.axis_index("depth")
    strip = lax.axis_index("strip")
    me_arg = me.reshape(1).astype(jnp.int32)
    strip_arg = strip.reshape(1).astype(jnp.int32)
    to_core = [(i, i ^ 1) for i in range(n)]
    to_chip = [[(i, i ^ (2 * j)) for i in range(n)] for j in range(1, sz.half)]
    swaps = []
    for start in (0, 1):
        below = [(i, i + 1) for i in range(start, strips - 1, 2)]
        swaps.append(below + [(b, a) for a, b in below])

    volume = pltpu.with_memory_space_constraint(volume, pltpu.HBM)
    meas = lax.dynamic_slice_in_dim(measured, me * sz.w, sz.w, axis=1)
    meas = jnp.pad(meas, ((0, 0), (0, sz.wl - sz.w)))
    by_family = col_taps.transpose(1, 0, 2)

    flat = shape((sz.ep, sz.wl), BF16)
    flat32 = shape((sz.ep, sz.wl), F32)
    edge = shape((64, sz.wl), BF16)
    halves = [shape((sz.half, sz.ep, sz.wl), F32), shape((sz.half, sz.ep, sz.wl), BF16)]
    blocked = shape((planes, n, rows, sz.wl), F32)
    tap_args = tuple(
        pltpu.with_memory_space_constraint(x, pltpu.HBM)
        for x in (radius, phase_map, row_taps, by_family)
    )
    tap_scratch = [
        pltpu.SMEM(radius.shape, jnp.int32),
        pltpu.SMEM(phase_map.shape, jnp.int32),
        pltpu.VMEM(row_taps.shape, F32),
        pltpu.VMEM(by_family.shape, F32),
    ]
    row_scratch = [
        pltpu.VMEM((round_up(sz.pitch, 8), sz.kp), F32),
        pltpu.VMEM((sz.ar, sz.kp), F32),
    ]
    s_scratch = pltpu.VMEM((n, planes * sz.rp, sz.wl), BF16)
    ratio_scratch = [
        pltpu.VMEM(((n + 2) * sz.ep, sz.wl), BF16),
        pltpu.VMEM((n, sz.el, sz.wl), BF16),
    ]
    vol_scratch = pltpu.VMEM(volume.shape, F32)

    rc, keep, send = call(
        first_kernel, sz, "first",
        [SMEM] + [HBM] * 5,
        [VMEM] * 3,
        [shape((sz.ep, planes * sz.rp), BF16), *halves],
        tap_scratch + [vol_scratch] + row_scratch
        + [
            pltpu.VMEM((planes, LANES + sz.ka, sz.wl), BF16),
            pltpu.VMEM((planes, sz.rp, sz.xw), BF16),
            s_scratch,
            pltpu.SemaphoreType.DMA((4 + planes,)),
        ],
        (me_arg, *tap_args, volume),
        24, 4,
    )

    tables, current = None, None
    for iteration in range(ITERS):
        recv = lax.ppermute(send, "depth", to_core)
        own, *sends = call(
            core_sum_kernel, sz, "core_sum",
            [SMEM, VMEM, VMEM],
            [VMEM] * sz.half,
            [flat32] + [flat] * (sz.half - 1),
            [], (me_arg, keep, recv), 4,
        )
        if tables is None:
            wf, *tables = call(
                table_kernel, sz, "tables",
                [SMEM] + [HBM] * 4 + [ANY],
                [VMEM] * 5,
                [
                    shape((planes, sz.kb, sz.wl), BF16),
                    shape((planes, sz.kb, sz.wl), BF16),
                    shape((planes, sz.rp, sz.el), BF16),
                    shape((planes, sz.rp, 1), F32),
                    shape((planes, 8, sz.wl), F32),
                ],
                tap_scratch + row_scratch + [pltpu.SemaphoreType.DMA((4,))],
                (strip_arg, *tap_args, own),
                8, 2,
            )
        recvs = [lax.ppermute(part, "depth", pairs) for part, pairs in zip(sends, to_chip)]
        total, *edges = call(
            chip_sum_kernel, sz, "chip_sum",
            [SMEM, ANY] + [VMEM] * (2 + len(recvs)),
            [VMEM] * 3,
            [flat32, edge, edge],
            [], (strip_arg, tables[3], own, meas, *recvs), 4,
        )
        edges = [lax.ppermute(part, "strip", pairs) for part, pairs in zip(edges, swaps)]
        ratio = call(
            ratio_kernel, sz, "ratio",
            [SMEM] + [VMEM] * 4,
            VMEM,
            flat,
            [pltpu.VMEM((sz.ep, sz.wl), F32)] * 2,
            (strip_arg, total, meas, *edges), 4,
        )
        chips = [lax.ppermute(ratio, "depth", pairs) for pairs in to_chip]
        if iteration == 0:
            current = call(
                block_kernel, sz, "blocks",
                [HBM, ANY], VMEM, blocked,
                [vol_scratch, pltpu.SemaphoreType.DMA((planes,))],
                (volume, ratio), 12, 3,
            )
        same = call(
            stack_kernel, sz, "stack",
            [ANY] + [VMEM] * sz.half, VMEM, halves[1],
            [], (current, ratio, *chips), 4,
        )
        other = lax.ppermute(same, "depth", to_core)
        if iteration < ITERS - 1:
            current, keep, send = call(
                middle_kernel, sz, "middle",
                [SMEM] + [VMEM] * 9,
                [VMEM] * 3,
                [blocked, *halves],
                ratio_scratch + [pltpu.VMEM(((n + 2) * sz.rp, sz.wl), BF16), s_scratch],
                (me_arg, same, other, wf, *tables, rc, current),
                16, 5,
            )
        else:
            current = call(
                last_kernel, sz, "last",
                [SMEM] + [VMEM] * 7,
                HBM,
                shape(volume.shape, F32),
                ratio_scratch + [vol_scratch, pltpu.SemaphoreType.DMA((planes,))],
                (me_arg, same, other, *tables, current),
                16, 5,
            )
    return current


def solution(mesh):
    return jax.shard_map(
        local,
        mesh=mesh,
        in_specs=(
            P("depth", "strip", None),
            P("strip", None),
            P("depth", None),
            P("depth", None, None),
            P("depth", None),
            P("depth"),
        ),
        out_specs=P("depth", "strip", None),
        check_vma=False,
    )
```

time: 72.9 us -> 61.6 us (0.84)
  Pallas kernels: 24.4 us -> 16.7 us
  waiting for transfers between devices: 21.1 us -> 17.9 us
    pallas_call x10 -> x13, Pallas kernels: 24.4 us -> 16.7 us  [call(): pl.pallas_call(functools.partial(kernel, sz), in_specs=in_specs, out_spec...]
    ppermute x6, waiting for transfers between devices: 5.04 us -> 2.65 us  [local(): chips = [lax.ppermute(ratio, 'depth', pairs) for pairs in to_chip]]
  transfers between devices with their start and end apart: 20 -> 20, of which waited for: 18 -> 14; matrix products, arithmetic and copies ran while one was open for 0% -> 0% of each run, Pallas kernels for 2% -> 8%
where the time goes in v2:
time: 61.6 us; the launch traced here: 61.4 us
  starting transfers between devices  26.3 us (43%)
  waiting for transfers between devices  17.9 us (29%)
  Pallas kernels  16.7 us (27%)
    pallas_call x13, Pallas kernels, call(): pl.pallas_call(functools.partial(kernel, sz), in_specs=in_specs, out_spec...  16.7 us
    ppermute x2, starting transfers between devices, local(): other = lax.ppermute(same, 'depth', to_core)  8.88 us
    ppermute x4, starting transfers between devices, local(): lax.ppermute(part, 'strip', pairs)  5.44 us
    ppermute x6, starting transfers between devices, local(): chips = [lax.ppermute(ratio, 'depth', pairs) for pairs in to_chip]  5.43 us
    ppermute x6, starting transfers between devices, local(): lax.ppermute(part, 'depth', pairs)  5.43 us
    ppermute x4, waiting for transfers between devices, local(): lax.ppermute(part, 'strip', pairs)  5.27 us
    ppermute x6, waiting for transfers between devices, local(): lax.ppermute(part, 'depth', pairs)  4.99 us
    ppermute x6, waiting for transfers between devices, local(): chips = [lax.ppermute(ratio, 'depth', pairs) for pairs in to_chip]  2.65 us
  transfers between devices with their start and end apart: 20, of which 14 were waited for; matrix products, arithmetic and copies ran while one was open for 0% of the time, Pallas kernels for 8%

profile of v2, /device:TPU:17, one launch (start us, length us, event | category | flops | bytes accessed | tf_op | source)
XLA Modules:
  0.0 61.4 jit_solution(14482086803461254637)
XLA Ops:
  0.0 0.0 copy-start
  0.0 3.7 %first.1 = (bf16[160,512]{1,0:T(8,128)(2,1)S(1)}, f32[4,160,256]{2,1,0:T(8,128)S(1)}, bf16[4,160,256]{2,1,0:T(8,128)(2,1)S(1)}) custom-call(s32[1]{0:T(128)} %bitcast.me_ref, s32[4]{0:T(128)} %radius_hbm.3, s32[4,15]{1,0:T(4,128)} %phase_hbm.3, f32[4,31]{1,0:T(4,128)} %row_hbm.3, f32[15,4,31]{2,1,0:T(4,128)} %bitcast.3, f32[4,120,1920]{2,1,0:T(8,128)} %vol_hbm.3), custom_call_target="tpu_custom_call" | custom-call | bytes 12000000 | tf_op jit(solution)/shard_map/first/pallas_call | solution.py:334
  3.7 0.7 %collective-permute-start = (bf16[4,160,256]{2,1,0:T(8,128)(2,1)S(1)}, bf16[4,160,256]{2,1,0:T(8,128)(2,1)S(1)}, u32[]{:S(2)}, u32[]{:S(2)}) collective-permute-start(bf16[4,160,256]{2,1,0:T(8,128)(2,1)S(1)} %get-tuple-element.31), channel_id=1, source_target_pairs={{0,4},{4,0},{8,12},{12,8},{16,20},{20,16},{24,28},{28,24},{1,5},{5... | collective-permute-start | bytes 983048 | tf_op jit(solution)/shard_map/ppermute | solution.py:413
  4.4 1.3 %collective-permute-done.recv_ref = bf16[4,160,256]{2,1,0:T(8,128)(2,1)S(1)} collective-permute-done((bf16[4,160,256]{2,1,0:T(8,128)(2,1)S(1)}, bf16[4,160,256]{2,1,0:T(8,128)(2,1)S(1)}, u32[]{:S(2)}, u32[]{:S(2)}) %collective-permute-start) | collective-permute-done | bytes 327712 | tf_op jit(solution)/shard_map/ppermute | solution.py:413
  5.7 0.1 core_sum.2
  5.7 1.3 %collective-permute-start.1 = (bf16[160,256]{1,0:T(8,128)(2,1)S(1)}, bf16[160,256]{1,0:T(8,128)(2,1)S(1)}, u32[]{:S(2)}, u32[]{:S(2)}) collective-permute-start(bf16[160,256]{1,0:T(8,128)(2,1)S(1)} %get-tuple-element.34), channel_id=1, source_target_pairs={{0,8},{4,12},{8,0},{12,4},{16,24},{20,28},{24,16},{28,20},{1,9},{5... | collective-permute-start | bytes 245768 | tf_op jit(solution)/shard_map/ppermute | solution.py:437
  7.0 1.2 %collective-permute-start.2 = (bf16[160,256]{1,0:T(8,128)(2,1)S(1)}, bf16[160,256]{1,0:T(8,128)(2,1)S(1)}, u32[]{:S(2)}, u32[]{:S(2)}) collective-permute-start(bf16[160,256]{1,0:T(8,128)(2,1)S(1)} %get-tuple-element.35), channel_id=1, source_target_pairs={{0,16},{4,20},{8,24},{12,28},{16,0},{20,4},{24,8},{28,12},{1,17},{... | collective-permute-start | bytes 245768 | tf_op jit(solution)/shard_map/ppermute | solution.py:437
  8.2 0.2 collective-permute-start.3
  8.4 0.0 copy-done
  8.5 0.1 constant_dynamic-slice_fusion
  8.6 2.3 %tables.1 = (bf16[4,512,256]{2,1,0:T(8,128)(2,1)S(1)}, bf16[4,512,256]{2,1,0:T(8,128)(2,1)S(1)}, bf16[4,128,256]{2,1,0:T(8,128)(2,1)S(1)}, f32[4,128,1]{2,1,0:T(8,128)S(1)}, f32[4,8,256]{2,1,0:T(8,128)S(1)}) custom-call(s32[1]{0:T(128)} %bitcast.1.strip_ref, s32[4]{0:T(128)} %radius_hbm.3, s32[4,15]{1,0:T(4,128)} %phase_hbm.3, f32[4,31]{1,0:T(4,128)} %row_hbm.3, ...), custom_call_target="tpu_custom_call" | custom-call | bytes 6000000 | tf_op jit(solution)/shard_map/tables/pallas_call | solution.py:334
  10.9 0.0 collective-permute-done.1.refs_0_
  10.9 0.0 collective-permute-done.2.refs_1_
  10.9 1.5 %collective-permute-done.3.refs_2_ = bf16[160,256]{1,0:T(8,128)(2,1)S(1)} collective-permute-done((bf16[160,256]{1,0:T(8,128)(2,1)S(1)}, bf16[160,256]{1,0:T(8,128)(2,1)S(1)}, u32[]{:S(2)}, u32[]{:S(2)}) %collective-permute-start.3) | collective-permute-done | bytes 81952 | tf_op jit(solution)/shard_map/ppermute | solution.py:437
  12.5 1.4 %collective-permute-start.4 = (bf16[64,256]{1,0:T(8,128)(2,1)S(1)}, bf16[64,256]{1,0:T(8,128)(2,1)S(1)}, u32[]{:S(2)}, u32[]{:S(2)}) collective-permute-start(bf16[64,256]{1,0:T(8,128)(2,1)S(1)} %get-tuple-element.38), channel_id=1, source_target_pairs={{0,1},{2,3},{1,0},{3,2},{4,5},{6,7},{5,4},{7,6},{8,9},{10,11},{9,8... | collective-permute-start | bytes 98312 | tf_op jit(solution)/shard_map/ppermute | solution.py:445
  13.9 1.9 %collective-permute-start.5 = (bf16[64,256]{1,0:T(8,128)(2,1)S(1)}, bf16[64,256]{1,0:T(8,128)(2,1)S(1)}, u32[]{:S(2)}, u32[]{:S(2)}) collective-permute-start(bf16[64,256]{1,0:T(8,128)(2,1)S(1)} %get-tuple-element.39), channel_id=1, source_target_pairs={{1,2},{2,1},{5,6},{6,5},{9,10},{10,9},{13,14},{14,13},{17,18},{18,... | collective-permute-start | bytes 98312 | tf_op jit(solution)/shard_map/ppermute | solution.py:445
  15.8 0.0 collective-permute-done.4.first_ref
  15.8 2.7 %collective-permute-done.5.second_ref = bf16[64,256]{1,0:T(8,128)(2,1)S(1)} collective-permute-done((bf16[64,256]{1,0:T(8,128)(2,1)S(1)}, bf16[64,256]{1,0:T(8,128)(2,1)S(1)}, u32[]{:S(2)}, u32[]{:S(2)}) %collective-permute-start.5) | collective-permute-done | bytes 32800 | tf_op jit(solution)/shard_map/ppermute | solution.py:445
  18.5 0.1 ratio.2.after_ref.refs_0_
  18.6 0.7 %collective-permute-start.8 = (bf16[160,256]{1,0:T(8,128)(2,1)S(1)}, bf16[160,256]{1,0:T(8,128)(2,1)S(1)}, u32[]{:S(2)}, u32[]{:S(2)}) collective-permute-start(bf16[160,256]{1,0:T(8,128)(2,1)S(1)} %ratio.2.after_ref.refs_0_), channel_id=1, source_target_pairs={{0,24},{4,28},{8,16},{12,20},{16,8},{20,12},{24,0},{28,4},{1,25},{... | collective-permute-start | bytes 245768 | tf_op jit(solution)/shard_map/ppermute | solution.py:454
  19.3 1.1 %collective-permute-start.7 = (bf16[160,256]{1,0:T(8,128)(2,1)S(1)}, bf16[160,256]{1,0:T(8,128)(2,1)S(1)}, u32[]{:S(2)}, u32[]{:S(2)}) collective-permute-start(bf16[160,256]{1,0:T(8,128)(2,1)S(1)} %ratio.2.after_ref.refs_0_), channel_id=1, source_target_pairs={{0,16},{4,20},{8,24},{12,28},{16,0},{20,4},{24,8},{28,12},{1,17},{... | collective-permute-start | bytes 245768 | tf_op jit(solution)/shard_map/ppermute | solution.py:454
  20.4 0.9 %collective-permute-start.6 = (bf16[160,256]{1,0:T(8,128)(2,1)S(1)}, bf16[160,256]{1,0:T(8,128)(2,1)S(1)}, u32[]{:S(2)}, u32[]{:S(2)}) collective-permute-start(bf16[160,256]{1,0:T(8,128)(2,1)S(1)} %ratio.2.after_ref.refs_0_), channel_id=1, source_target_pairs={{0,8},{4,12},{8,0},{12,4},{16,24},{20,28},{24,16},{28,20},{1,9},{5... | collective-permute-start | bytes 245768 | tf_op jit(solution)/shard_map/ppermute | solution.py:454
  21.3 2.8 %blocks.1.after_ref.vol_ref = f32[4,8,120,256]{3,2,1,0:T(8,128)S(1)} custom-call(f32[4,120,1920]{2,1,0:T(8,128)} %vol_hbm.3, bf16[160,256]{1,0:T(8,128)(2,1)S(1)} %ratio.2.after_ref.refs_0_), custom_call_target="tpu_custom_call" | custom-call | bytes 9000000 | tf_op jit(solution)/shard_map/blocks/pallas_call | solution.py:334
  24.1 0.0 collective-permute-done.8.refs_3_
  24.1 0.0 collective-permute-done.7.refs_2_
  24.1 0.0 collective-permute-done.6.refs_1_
  24.1 4.5 %collective-permute-start.9 = (bf16[4,160,256]{2,1,0:T(8,128)(2,1)S(1)}, bf16[4,160,256]{2,1,0:T(8,128)(2,1)S(1)}, u32[]{:S(2)}, u32[]{:S(2)}) collective-permute-start(bf16[4,160,256]{2,1,0:T(8,128)(2,1)S(1)} %stack.2.same_ref), channel_id=1, source_target_pairs={{0,4},{4,0},{8,12},{12,8},{16,20},{20,16},{24,28},{28,24},{1,5},{5... | collective-permute-start | bytes 983048 | tf_op jit(solution)/shard_map/ppermute | solution.py:467
  28.7 1.3 %collective-permute-done.9.other_ref = bf16[4,160,256]{2,1,0:T(8,128)(2,1)S(1)} collective-permute-done((bf16[4,160,256]{2,1,0:T(8,128)(2,1)S(1)}, bf16[4,160,256]{2,1,0:T(8,128)(2,1)S(1)}, u32[]{:S(2)}, u32[]{:S(2)}) %collective-permute-start.9) | collective-permute-done | bytes 327712 | tf_op jit(solution)/shard_map/ppermute | solution.py:467
  29.9 4.0 %middle.1 = (f32[4,8,120,256]{3,2,1,0:T(8,128)S(1)}, f32[4,160,256]{2,1,0:T(8,128)S(1)}, bf16[4,160,256]{2,1,0:T(8,128)(2,1)S(1)}) custom-call(s32[1]{0:T(128)} %bitcast.me_ref, bf16[4,160,256]{2,1,0:T(8,128)(2,1)S(1)} %stack.2.same_ref, bf16[4,160,256]{2,1,0:T(8,128)(2,1)S(1)} %collective-permute-done.9.other_ref, ...), custom_call_target="tpu_custom_call" | custom-call | bytes 15000000 | tf_op jit(solution)/shard_map/middle/pallas_call | solution.py:334
  34.0 0.4 collective-permute-start.10
  34.4 1.3 %collective-permute-done.10.recv_ref = bf16[4,160,256]{2,1,0:T(8,128)(2,1)S(1)} collective-permute-done((bf16[4,160,256]{2,1,0:T(8,128)(2,1)S(1)}, bf16[4,160,256]{2,1,0:T(8,128)(2,1)S(1)}, u32[]{:S(2)}, u32[]{:S(2)}) %collective-permute-start.10) | collective-permute-done | bytes 327712 | tf_op jit(solution)/shard_map/ppermute | solution.py:413
  35.7 0.1 core_sum.3
  35.8 1.3 %collective-permute-start.11 = (bf16[160,256]{1,0:T(8,128)(2,1)S(1)}, bf16[160,256]{1,0:T(8,128)(2,1)S(1)}, u32[]{:S(2)}, u32[]{:S(2)}) collective-permute-start(bf16[160,256]{1,0:T(8,128)(2,1)S(1)} %get-tuple-element.49), channel_id=1, source_target_pairs={{0,8},{4,12},{8,0},{12,4},{16,24},{20,28},{24,16},{28,20},{1,9},{5... | collective-permute-start | bytes 245768 | tf_op jit(solution)/shard_map/ppermute | solution.py:437
  37.0 0.6 collective-permute-start.12
  37.6 0.9 %collective-permute-start.13 = (bf16[160,256]{1,0:T(8,128)(2,1)S(1)}, bf16[160,256]{1,0:T(8,128)(2,1)S(1)}, u32[]{:S(2)}, u32[]{:S(2)}) collective-permute-start(bf16[160,256]{1,0:T(8,128)(2,1)S(1)} %get-tuple-element.51), channel_id=1, source_target_pairs={{0,24},{4,28},{8,16},{12,20},{16,8},{20,12},{24,0},{28,4},{1,25},{... | collective-permute-start | bytes 245768 | tf_op jit(solution)/shard_map/ppermute | solution.py:437
  38.5 1.0 %collective-permute-done.11.refs_0_ = bf16[160,256]{1,0:T(8,128)(2,1)S(1)} collective-permute-done((bf16[160,256]{1,0:T(8,128)(2,1)S(1)}, bf16[160,256]{1,0:T(8,128)(2,1)S(1)}, u32[]{:S(2)}, u32[]{:S(2)}) %collective-permute-start.11) | collective-permute-done | bytes 81952 | tf_op jit(solution)/shard_map/ppermute | solution.py:437
  39.5 0.8 %collective-permute-done.12.refs_1_ = bf16[160,256]{1,0:T(8,128)(2,1)S(1)} collective-permute-done((bf16[160,256]{1,0:T(8,128)(2,1)S(1)}, bf16[160,256]{1,0:T(8,128)(2,1)S(1)}, u32[]{:S(2)}, u32[]{:S(2)}) %collective-permute-start.12) | collective-permute-done | bytes 81952 | tf_op jit(solution)/shard_map/ppermute | solution.py:437
  40.3 1.6 %collective-permute-done.13.refs_2_ = bf16[160,256]{1,0:T(8,128)(2,1)S(1)} collective-permute-done((bf16[160,256]{1,0:T(8,128)(2,1)S(1)}, bf16[160,256]{1,0:T(8,128)(2,1)S(1)}, u32[]{:S(2)}, u32[]{:S(2)}) %collective-permute-start.13) | collective-permute-done | bytes 81952 | tf_op jit(solution)/shard_map/ppermute | solution.py:437
  42.0 0.1 collective-permute-start.14
  42.0 2.1 %collective-permute-start.15 = (bf16[64,256]{1,0:T(8,128)(2,1)S(1)}, bf16[64,256]{1,0:T(8,128)(2,1)S(1)}, u32[]{:S(2)}, u32[]{:S(2)}) collective-permute-start(bf16[64,256]{1,0:T(8,128)(2,1)S(1)} %get-tuple-element.54), channel_id=1, source_target_pairs={{1,2},{2,1},{5,6},{6,5},{9,10},{10,9},{13,14},{14,13},{17,18},{18,... | collective-permute-start | bytes 98312 | tf_op jit(solution)/shard_map/ppermute | solution.py:445
  44.2 0.6 %collective-permute-done.14.first_ref = bf16[64,256]{1,0:T(8,128)(2,1)S(1)} collective-permute-done((bf16[64,256]{1,0:T(8,128)(2,1)S(1)}, bf16[64,256]{1,0:T(8,128)(2,1)S(1)}, u32[]{:S(2)}, u32[]{:S(2)}) %collective-permute-start.14) | collective-permute-done | bytes 32800 | tf_op jit(solution)/shard_map/ppermute | solution.py:445
  44.8 1.9 %collective-permute-done.15.second_ref = bf16[64,256]{1,0:T(8,128)(2,1)S(1)} collective-permute-done((bf16[64,256]{1,0:T(8,128)(2,1)S(1)}, bf16[64,256]{1,0:T(8,128)(2,1)S(1)}, u32[]{:S(2)}, u32[]{:S(2)}) %collective-permute-start.15) | collective-permute-done | bytes 32800 | tf_op jit(solution)/shard_map/ppermute | solution.py:445
  46.7 0.1 ratio.3.refs_0_
  46.8 1.4 %collective-permute-start.18 = (bf16[160,256]{1,0:T(8,128)(2,1)S(1)}, bf16[160,256]{1,0:T(8,128)(2,1)S(1)}, u32[]{:S(2)}, u32[]{:S(2)}) collective-permute-start(bf16[160,256]{1,0:T(8,128)(2,1)S(1)} %ratio.3.refs_0_), channel_id=1, source_target_pairs={{0,24},{4,28},{8,16},{12,20},{16,8},{20,12},{24,0},{28,4},{1,25},{... | collective-permute-start | bytes 245768 | tf_op jit(solution)/shard_map/ppermute | solution.py:454
  48.2 0.6 %collective-permute-start.17 = (bf16[160,256]{1,0:T(8,128)(2,1)S(1)}, bf16[160,256]{1,0:T(8,128)(2,1)S(1)}, u32[]{:S(2)}, u32[]{:S(2)}) collective-permute-start(bf16[160,256]{1,0:T(8,128)(2,1)S(1)} %ratio.3.refs_0_), channel_id=1, source_target_pairs={{0,16},{4,20},{8,24},{12,28},{16,0},{20,4},{24,8},{28,12},{1,17},{... | collective-permute-start | bytes 245768 | tf_op jit(solution)/shard_map/ppermute | solution.py:454
  48.8 0.6 %collective-permute-start.16 = (bf16[160,256]{1,0:T(8,128)(2,1)S(1)}, bf16[160,256]{1,0:T(8,128)(2,1)S(1)}, u32[]{:S(2)}, u32[]{:S(2)}) collective-permute-start(bf16[160,256]{1,0:T(8,128)(2,1)S(1)} %ratio.3.refs_0_), channel_id=1, source_target_pairs={{0,8},{4,12},{8,0},{12,4},{16,24},{20,28},{24,16},{28,20},{1,9},{5... | collective-permute-start | bytes 245768 | tf_op jit(solution)/shard_map/ppermute | solution.py:454
  49.5 1.6 %collective-permute-done.18.refs_3_ = bf16[160,256]{1,0:T(8,128)(2,1)S(1)} collective-permute-done((bf16[160,256]{1,0:T(8,128)(2,1)S(1)}, bf16[160,256]{1,0:T(8,128)(2,1)S(1)}, u32[]{:S(2)}, u32[]{:S(2)}) %collective-permute-start.18) | collective-permute-done | bytes 81952 | tf_op jit(solution)/shard_map/ppermute | solution.py:454
  51.1 0.8 %collective-permute-done.17.refs_2_ = bf16[160,256]{1,0:T(8,128)(2,1)S(1)} collective-permute-done((bf16[160,256]{1,0:T(8,128)(2,1)S(1)}, bf16[160,256]{1,0:T(8,128)(2,1)S(1)}, u32[]{:S(2)}, u32[]{:S(2)}) %collective-permute-start.17) | collective-permute-done | bytes 81952 | tf_op jit(solution)/shard_map/ppermute | solution.py:454
  51.9 0.2 collective-permute-done.16.refs_1_
  52.2 4.3 %collective-permute-start.19 = (bf16[4,160,256]{2,1,0:T(8,128)(2,1)S(1)}, bf16[4,160,256]{2,1,0:T(8,128)(2,1)S(1)}, u32[]{:S(2)}, u32[]{:S(2)}) collective-permute-start(bf16[4,160,256]{2,1,0:T(8,128)(2,1)S(1)} %stack.3.same_ref), channel_id=1, source_target_pairs={{0,4},{4,0},{8,12},{12,8},{16,20},{20,16},{24,28},{28,24},{1,5},{5... | collective-permute-start | bytes 983048 | tf_op jit(solution)/shard_map/ppermute | solution.py:467
  56.5 1.3 %collective-permute-done.19.other_ref = bf16[4,160,256]{2,1,0:T(8,128)(2,1)S(1)} collective-permute-done((bf16[4,160,256]{2,1,0:T(8,128)(2,1)S(1)}, bf16[4,160,256]{2,1,0:T(8,128)(2,1)S(1)}, u32[]{:S(2)}, u32[]{:S(2)}) %collective-permute-start.19) | collective-permute-done | bytes 327712 | tf_op jit(solution)/shard_map/ppermute | solution.py:467
  57.8 3.5 %last.1 = f32[4,120,1920]{2,1,0:T(8,128)} custom-call(s32[1]{0:T(128)} %bitcast.me_ref, bf16[4,160,256]{2,1,0:T(8,128)(2,1)S(1)} %stack.3.same_ref, bf16[4,160,256]{2,1,0:T(8,128)(2,1)S(1)} %collective-permute-done.19.other_ref, bf16[4,512,256]{2,1,0:T(8,128)(2,1)S(1)} %get-tuple-element.41.wb_ref, bf16[4,128,256]{2,1,0:T(8,128)(2,1)S(1)} %get-tuple-element.42.rt_ref, ...), custom_call_target="tpu_custom_call" | custom-call | bytes 15000000 | tf_op jit(solution)/shard_map/last/pallas_call | solution.py:334
  (5 shorter events, 0.1 us)
Async XLA Ops:
  0.0 8.5 %copy-start = (f32[120,1920]{1,0:T(8,128)S(1)}, f32[120,1920]{1,0:T(8,128)}, u32[]{:S(2)}) copy-start(f32[120,1920]{1,0:T(8,128)} %param.7) | copy-start | bytes 2764804
  3.7 2.0 %collective-permute-start = (bf16[4,160,256]{2,1,0:T(8,128)(2,1)S(1)}, bf16[4,160,256]{2,1,0:T(8,128)(2,1)S(1)}, u32[]{:S(2)}, u32[]{:S(2)}) collective-permute-start(bf16[4,160,256]{2,1,0:T(8,128)(2,1)S(1)} %get-tuple-element.31), channel_id=1, source_target_pairs={{0,4},{4,0},{8,12},{12,8},{16,20},{20,16},{24,28},{28,24},{1,5},{5... | collective-permute-start | bytes 983048 | tf_op jit(solution)/shard_map/ppermute | solution.py:413
  5.7 5.1 %collective-permute-start.1 = (bf16[160,256]{1,0:T(8,128)(2,1)S(1)}, bf16[160,256]{1,0:T(8,128)(2,1)S(1)}, u32[]{:S(2)}, u32[]{:S(2)}) collective-permute-start(bf16[160,256]{1,0:T(8,128)(2,1)S(1)} %get-tuple-element.34), channel_id=1, source_target_pairs={{0,8},{4,12},{8,0},{12,4},{16,24},{20,28},{24,16},{28,20},{1,9},{5... | collective-permute-start | bytes 245768 | tf_op jit(solution)/shard_map/ppermute | solution.py:437
  7.0 3.9 %collective-permute-start.2 = (bf16[160,256]{1,0:T(8,128)(2,1)S(1)}, bf16[160,256]{1,0:T(8,128)(2,1)S(1)}, u32[]{:S(2)}, u32[]{:S(2)}) collective-permute-start(bf16[160,256]{1,0:T(8,128)(2,1)S(1)} %get-tuple-element.35), channel_id=1, source_target_pairs={{0,16},{4,20},{8,24},{12,28},{16,0},{20,4},{24,8},{28,12},{1,17},{... | collective-permute-start | bytes 245768 | tf_op jit(solution)/shard_map/ppermute | solution.py:437
  8.2 4.2 %collective-permute-start.3 = (bf16[160,256]{1,0:T(8,128)(2,1)S(1)}, bf16[160,256]{1,0:T(8,128)(2,1)S(1)}, u32[]{:S(2)}, u32[]{:S(2)}) collective-permute-start(bf16[160,256]{1,0:T(8,128)(2,1)S(1)} %get-tuple-element.36), channel_id=1, source_target_pairs={{0,24},{4,28},{8,16},{12,20},{16,8},{20,12},{24,0},{28,4},{1,25},{... | collective-permute-start | bytes 245768 | tf_op jit(solution)/shard_map/ppermute | solution.py:437
  12.5 3.3 %collective-permute-start.4 = (bf16[64,256]{1,0:T(8,128)(2,1)S(1)}, bf16[64,256]{1,0:T(8,128)(2,1)S(1)}, u32[]{:S(2)}, u32[]{:S(2)}) collective-permute-start(bf16[64,256]{1,0:T(8,128)(2,1)S(1)} %get-tuple-element.38), channel_id=1, source_target_pairs={{0,1},{2,3},{1,0},{3,2},{4,5},{6,7},{5,4},{7,6},{8,9},{10,11},{9,8... | collective-permute-start | bytes 98312 | tf_op jit(solution)/shard_map/ppermute | solution.py:445
  13.9 4.6 %collective-permute-start.5 = (bf16[64,256]{1,0:T(8,128)(2,1)S(1)}, bf16[64,256]{1,0:T(8,128)(2,1)S(1)}, u32[]{:S(2)}, u32[]{:S(2)}) collective-permute-start(bf16[64,256]{1,0:T(8,128)(2,1)S(1)} %get-tuple-element.39), channel_id=1, source_target_pairs={{1,2},{2,1},{5,6},{6,5},{9,10},{10,9},{13,14},{14,13},{17,18},{18,... | collective-permute-start | bytes 98312 | tf_op jit(solution)/shard_map/ppermute | solution.py:445
  18.6 5.5 %collective-permute-start.8 = (bf16[160,256]{1,0:T(8,128)(2,1)S(1)}, bf16[160,256]{1,0:T(8,128)(2,1)S(1)}, u32[]{:S(2)}, u32[]{:S(2)}) collective-permute-start(bf16[160,256]{1,0:T(8,128)(2,1)S(1)} %ratio.2.after_ref.refs_0_), channel_id=1, source_target_pairs={{0,24},{4,28},{8,16},{12,20},{16,8},{20,12},{24,0},{28,4},{1,25},{... | collective-permute-start | bytes 245768 | tf_op jit(solution)/shard_map/ppermute | solution.py:454
  19.3 4.8 %collective-permute-start.7 = (bf16[160,256]{1,0:T(8,128)(2,1)S(1)}, bf16[160,256]{1,0:T(8,128)(2,1)S(1)}, u32[]{:S(2)}, u32[]{:S(2)}) collective-permute-start(bf16[160,256]{1,0:T(8,128)(2,1)S(1)} %ratio.2.after_ref.refs_0_), channel_id=1, source_target_pairs={{0,16},{4,20},{8,24},{12,28},{16,0},{20,4},{24,8},{28,12},{1,17},{... | collective-permute-start | bytes 245768 | tf_op jit(solution)/shard_map/ppermute | solution.py:454
  20.4 3.7 %collective-permute-start.6 = (bf16[160,256]{1,0:T(8,128)(2,1)S(1)}, bf16[160,256]{1,0:T(8,128)(2,1)S(1)}, u32[]{:S(2)}, u32[]{:S(2)}) collective-permute-start(bf16[160,256]{1,0:T(8,128)(2,1)S(1)} %ratio.2.after_ref.refs_0_), channel_id=1, source_target_pairs={{0,8},{4,12},{8,0},{12,4},{16,24},{20,28},{24,16},{28,20},{1,9},{5... | collective-permute-start | bytes 245768 | tf_op jit(solution)/shard_map/ppermute | solution.py:454
  24.1 5.8 %collective-permute-start.9 = (bf16[4,160,256]{2,1,0:T(8,128)(2,1)S(1)}, bf16[4,160,256]{2,1,0:T(8,128)(2,1)S(1)}, u32[]{:S(2)}, u32[]{:S(2)}) collective-permute-start(bf16[4,160,256]{2,1,0:T(8,128)(2,1)S(1)} %stack.2.same_ref), channel_id=1, source_target_pairs={{0,4},{4,0},{8,12},{12,8},{16,20},{20,16},{24,28},{28,24},{1,5},{5... | collective-permute-start | bytes 983048 | tf_op jit(solution)/shard_map/ppermute | solution.py:467
  34.0 1.7 %collective-permute-start.10 = (bf16[4,160,256]{2,1,0:T(8,128)(2,1)S(1)}, bf16[4,160,256]{2,1,0:T(8,128)(2,1)S(1)}, u32[]{:S(2)}, u32[]{:S(2)}) collective-permute-start(bf16[4,160,256]{2,1,0:T(8,128)(2,1)S(1)} %get-tuple-element.47), channel_id=1, source_target_pairs={{0,4},{4,0},{8,12},{12,8},{16,20},{20,16},{24,28},{28,24},{1,5},{5... | collective-permute-start | bytes 983048 | tf_op jit(solution)/shard_map/ppermute | solution.py:413
  35.8 3.7 %collective-permute-start.11 = (bf16[160,256]{1,0:T(8,128)(2,1)S(1)}, bf16[160,256]{1,0:T(8,128)(2,1)S(1)}, u32[]{:S(2)}, u32[]{:S(2)}) collective-permute-start(bf16[160,256]{1,0:T(8,128)(2,1)S(1)} %get-tuple-element.49), channel_id=1, source_target_pairs={{0,8},{4,12},{8,0},{12,4},{16,24},{20,28},{24,16},{28,20},{1,9},{5... | collective-permute-start | bytes 245768 | tf_op jit(solution)/shard_map/ppermute | solution.py:437
  37.0 3.3 %collective-permute-start.12 = (bf16[160,256]{1,0:T(8,128)(2,1)S(1)}, bf16[160,256]{1,0:T(8,128)(2,1)S(1)}, u32[]{:S(2)}, u32[]{:S(2)}) collective-permute-start(bf16[160,256]{1,0:T(8,128)(2,1)S(1)} %get-tuple-element.50), channel_id=1, source_target_pairs={{0,16},{4,20},{8,24},{12,28},{16,0},{20,4},{24,8},{28,12},{1,17},{... | collective-permute-start | bytes 245768 | tf_op jit(solution)/shard_map/ppermute | solution.py:437
  37.6 4.3 %collective-permute-start.13 = (bf16[160,256]{1,0:T(8,128)(2,1)S(1)}, bf16[160,256]{1,0:T(8,128)(2,1)S(1)}, u32[]{:S(2)}, u32[]{:S(2)}) collective-permute-start(bf16[160,256]{1,0:T(8,128)(2,1)S(1)} %get-tuple-element.51), channel_id=1, source_target_pairs={{0,24},{4,28},{8,16},{12,20},{16,8},{20,12},{24,0},{28,4},{1,25},{... | collective-permute-start | bytes 245768 | tf_op jit(solution)/shard_map/ppermute | solution.py:437
  42.0 2.8 %collective-permute-start.14 = (bf16[64,256]{1,0:T(8,128)(2,1)S(1)}, bf16[64,256]{1,0:T(8,128)(2,1)S(1)}, u32[]{:S(2)}, u32[]{:S(2)}) collective-permute-start(bf16[64,256]{1,0:T(8,128)(2,1)S(1)} %get-tuple-element.53), channel_id=1, source_target_pairs={{0,1},{2,3},{1,0},{3,2},{4,5},{6,7},{5,4},{7,6},{8,9},{10,11},{9,8... | collective-permute-start | bytes 98312 | tf_op jit(solution)/shard_map/ppermute | solution.py:445
  42.0 4.7 %collective-permute-start.15 = (bf16[64,256]{1,0:T(8,128)(2,1)S(1)}, bf16[64,256]{1,0:T(8,128)(2,1)S(1)}, u32[]{:S(2)}, u32[]{:S(2)}) collective-permute-start(bf16[64,256]{1,0:T(8,128)(2,1)S(1)} %get-tuple-element.54), channel_id=1, source_target_pairs={{1,2},{2,1},{5,6},{6,5},{9,10},{10,9},{13,14},{14,13},{17,18},{18,... | collective-permute-start | bytes 98312 | tf_op jit(solution)/shard_map/ppermute | solution.py:445
  46.8 4.3 %collective-permute-start.18 = (bf16[160,256]{1,0:T(8,128)(2,1)S(1)}, bf16[160,256]{1,0:T(8,128)(2,1)S(1)}, u32[]{:S(2)}, u32[]{:S(2)}) collective-permute-start(bf16[160,256]{1,0:T(8,128)(2,1)S(1)} %ratio.3.refs_0_), channel_id=1, source_target_pairs={{0,24},{4,28},{8,16},{12,20},{16,8},{20,12},{24,0},{28,4},{1,25},{... | collective-permute-start | bytes 245768 | tf_op jit(solution)/shard_map/ppermute | solution.py:454
  48.2 3.7 %collective-permute-start.17 = (bf16[160,256]{1,0:T(8,128)(2,1)S(1)}, bf16[160,256]{1,0:T(8,128)(2,1)S(1)}, u32[]{:S(2)}, u32[]{:S(2)}) collective-permute-start(bf16[160,256]{1,0:T(8,128)(2,1)S(1)} %ratio.3.refs_0_), channel_id=1, source_target_pairs={{0,16},{4,20},{8,24},{12,28},{16,0},{20,4},{24,8},{28,12},{1,17},{... | collective-permute-start | bytes 245768 | tf_op jit(solution)/shard_map/ppermute | solution.py:454
  48.8 3.3 %collective-permute-start.16 = (bf16[160,256]{1,0:T(8,128)(2,1)S(1)}, bf16[160,256]{1,0:T(8,128)(2,1)S(1)}, u32[]{:S(2)}, u32[]{:S(2)}) collective-permute-start(bf16[160,256]{1,0:T(8,128)(2,1)S(1)} %ratio.3.refs_0_), channel_id=1, source_target_pairs={{0,8},{4,12},{8,0},{12,4},{16,24},{20,28},{24,16},{28,20},{1,9},{5... | collective-permute-start | bytes 245768 | tf_op jit(solution)/shard_map/ppermute | solution.py:454
  52.2 5.6 %collective-permute-start.19 = (bf16[4,160,256]{2,1,0:T(8,128)(2,1)S(1)}, bf16[4,160,256]{2,1,0:T(8,128)(2,1)S(1)}, u32[]{:S(2)}, u32[]{:S(2)}) collective-permute-start(bf16[4,160,256]{2,1,0:T(8,128)(2,1)S(1)} %stack.3.same_ref), channel_id=1, source_target_pairs={{0,4},{4,0},{8,12},{12,8},{16,20},{20,16},{24,28},{28,24},{1,5},{5... | collective-permute-start | bytes 983048 | tf_op jit(solution)/shard_map/ppermute | solution.py:467

commit v3 on v2

--- a/solution.py
+++ b/solution.py
@@ -27,7 +27,7 @@
         self.w = cols // devices
         self.half = devices // 2
         assert cols % devices == 0 and self.w % pitch == 0 and self.w >= 2 * SIDE
-        assert devices >= 2 and devices & (devices - 1) == 0 and rows >= 2 * RMAX and rows % 8 == 0
+        assert devices >= 4 and devices & (devices - 1) == 0 and rows >= 2 * RMAX and rows % 8 == 0
         self.wl = round_up(self.w, LANES)
         self.span = self.w + 2 * SIDE
         self.kp = round_up(self.span, LANES)
@@ -35,7 +35,9 @@
         self.rp = round_up(rows, LANES)
         self.e = rows + 2 * RMAX
         self.ep = round_up(self.e, 32)
+        self.hr = self.ep // 2
         self.el = round_up(self.ep, LANES)
+        assert 32 <= rows - self.hr and rows - self.hr + 32 <= self.hr and (rows - self.hr) % 8 == 0
         self.ar = round_up(max(self.span, self.wl) + pitch, pitch)
         self.starts = [LANES + b * self.w - SIDE for b in range(devices)]
         self.ka = round_up(max(s % LANES for s in self.starts) + self.span, LANES)
@@ -102,13 +104,12 @@
     return jnp.concatenate([here, after, before], axis=1)
 
 
-def rows_forward(sz, me, rc_ref, s_ref, keep_ref, send_ref):
-    core = lax.rem(me, 2)
+def rows_forward(sz, rc_ref, s_ref, keep_ref, send_ref):
     coef = rc_ref[...]
-    for k in range(sz.half):
-        for ref, block in ((send_ref, 2 * k + 1 - core), (keep_ref, 2 * k + core)):
-            out = jnp.dot(coef, s_ref[block], preferred_element_type=F32)
-            ref[k] = out.astype(ref.dtype)
+    for b in range(sz.n):
+        out = jnp.dot(coef, s_ref[b], preferred_element_type=F32)
+        send_ref[b] = out[0 : sz.hr, :].astype(BF16)
+        keep_ref[b] = out[sz.hr :, :]
 
 
 def backward(sz, ratio_ref, matrix, rt, g_ref):
@@ -131,11 +132,13 @@
     ratio_ref[0 : sz.ep, :] = empty
     ratio_ref[(sz.n + 1) * sz.ep :, :] = empty
     g_ref[:, sz.ep :, :] = jnp.zeros((sz.n, sz.el - sz.ep, sz.wl), BF16)
-    core = lax.rem(me, 2)
+    part = lax.rem(me, 2)
     for j in range(sz.half):
         chip = (me // 2) ^ j
-        for ref, b in ((same_ref, 2 * chip + core), (other_ref, 2 * chip + 1 - core)):
-            ratio_ref[pl.ds(pl.multiple_of((b + 1) * sz.ep, sz.ep), sz.ep), :] = ref[j]
+        for ref, rows in ((same_ref, part), (other_ref, 1 - part)):
+            for k in range(2):
+                at = (2 * chip + k + 1) * sz.ep + rows * sz.hr
+                ratio_ref[pl.ds(pl.multiple_of(at, sz.hr), sz.hr), :] = ref[j, k]
 
 
 def first_kernel(
@@ -151,6 +154,7 @@
     ]
     for copy in small + large:
         copy.start()
+    part = lax.rem(me_ref[0], 2)
     m_ref[...] = jnp.zeros_like(m_ref)
     x_ref[...] = jnp.zeros_like(x_ref)
     for copy in small:
@@ -163,7 +167,10 @@
         matrix = jnp.concatenate([matrix, rest], axis=0) if rest.shape[0] else matrix
         m_ref[z, LANES : LANES + matrix.shape[0], :] = matrix.astype(BF16)
         rt = row_matrix(sz, z, reach, row_ref)
-        rc_ref[:, z * sz.rp : (z + 1) * sz.rp] = rt.T[0 : sz.ep, :].astype(BF16)
+        rt = rt.T.astype(BF16)
+        lanes = slice(z * sz.rp, (z + 1) * sz.rp)
+        rc_ref[pl.ds(pl.multiple_of((1 - part) * sz.hr, sz.hr), sz.hr), lanes] = rt[0 : sz.hr, :]
+        rc_ref[pl.ds(pl.multiple_of(part * sz.hr, sz.hr), sz.hr), lanes] = rt[sz.hr : sz.ep, :]
     for z in range(sz.planes):
         large[z].wait()
         x = jnp.concatenate([vol_ref[z], jnp.zeros((sz.rp - sz.rows, sz.cols), F32)], axis=0)
@@ -174,7 +181,7 @@
             matrix = m_ref[z, LANES - shift : LANES - shift + sz.ka, :]
             out = jnp.dot(window, matrix, preferred_element_type=F32)
             s_ref[b, z * sz.rp : (z + 1) * sz.rp, :] = out.astype(BF16)
-    rows_forward(sz, me_ref[0], rc_ref, s_ref, keep_ref, send_ref)
+    rows_forward(sz, rc_ref, s_ref, keep_ref, send_ref)
 
 
 def table_kernel(
@@ -223,43 +230,56 @@
 
 def core_sum_kernel(sz, me_ref, keep_ref, recv_ref, own_ref, *out_refs):
     mine = me_ref[0] // 2
-    own_ref[...] = keep_ref[mine] + recv_ref[mine].astype(F32)
-    for j, ref in enumerate(out_refs, 1):
-        other = mine ^ j
-        ref[...] = (keep_ref[other] + recv_ref[other].astype(F32)).astype(BF16)
-
-
-def chip_sum_kernel(sz, strip_ref, after_ref, own_ref, meas_ref, *refs):
-    recv_refs, (sum_ref, first_ref, second_ref) = refs[:-3], refs[-3:]
+    for j, ref in enumerate((own_ref, *out_refs)):
+        blocks = pl.ds(2 * (mine ^ j), 2)
+        ref[...] = (keep_ref[blocks] + recv_ref[blocks].astype(F32)).astype(ref.dtype)
+
+
+def chip_sum_kernel(sz, me_ref, after_ref, own_ref, meas_ref, *refs, first):
+    recv_refs, (sum_ref, edge_ref) = refs[:-2], refs[-2:]
     total = own_ref[...]
     for ref in recv_refs:
         total = total + ref[...].astype(F32)
     sum_ref[...] = total
     edges = []
-    for first, row in ((0, 0), (sz.rows, sz.rows - SIDE)):
-        meas = meas_ref[row : row + SIDE, :]
-        high = meas.astype(BF16).astype(F32)
-        edges.append(jnp.concatenate([total[first : first + 32, :], high, meas - high], axis=0))
-    up, down = edges
-    even = lax.rem(strip_ref[0], 2) == 0
-    first_ref[...] = jnp.where(even, down, up).astype(BF16)
-    second_ref[...] = jnp.where(even, up, down).astype(BF16)
-
-
-def ratio_kernel(sz, strip_ref, sum_ref, meas_ref, first_ref, second_ref, ratio_ref, s_ref, m_ref):
-    even = lax.rem(strip_ref[0], 2) == 0
-    first, second = first_ref[...].astype(F32), second_ref[...].astype(F32)
-    above, below = jnp.where(even, second, first), jnp.where(even, first, second)
+    for at, row in ((0, 0), (sz.rows - sz.hr, sz.rows - SIDE)):
+        parts = [total[:, at : at + 32, :]]
+        if first:
+            meas = meas_ref[:, row : row + SIDE, :]
+            high = meas.astype(BF16).astype(F32)
+            parts += [high, meas - high]
+        edges.append(jnp.concatenate(parts, axis=1))
+    top, bottom = edges
+    edge_ref[...] = jnp.where(lax.rem(me_ref[0], 2) == 0, top, bottom).astype(BF16)
+
+
+def ratio_kernel(
+    sz, me_ref, strip_ref, sum_ref, meas_ref, edge_ref, first_edge_ref, ratio_ref, s_ref, m_ref
+):
+    part = lax.rem(me_ref[0], 2)
     s_ref[...] = sum_ref[...]
-    s_ref[0:32, :] += above[0:32, :]
-    s_ref[sz.rows : sz.rows + 32, :] += below[0:32, :]
     m_ref[...] = jnp.zeros_like(m_ref)
-    m_ref[RMAX : RMAX + sz.rows, :] = meas_ref[...]
-    m_ref[0:RMAX, :] = (above[32:48, :] + above[48:64, :])[SIDE - RMAX :, :]
-    m_ref[RMAX + sz.rows : sz.e, :] = (below[32:48, :] + below[48:64, :])[0:RMAX, :]
-    row = iota(s_ref.shape, 0)
+    edge, first_edge = edge_ref[...].astype(F32), first_edge_ref[...].astype(F32)
+    alone = jnp.where(part == 0, strip_ref[0] == 0, (strip_ref[0] + 1) * sz.rows == sz.total)
+    rows = jnp.where(alone, 0.0, edge[:, 0:32, :])
+    meas = first_edge[:, 32:48, :] + first_edge[:, 48:64, :]
+
+    @pl.when(part == 0)
+    def _():
+        s_ref[:, 0:32, :] += rows
+        m_ref[:, 0:RMAX, :] = meas[:, SIDE - RMAX :, :]
+        m_ref[:, RMAX : sz.hr, :] = meas_ref[:, 0 : sz.hr - RMAX, :]
+
+    @pl.when(part == 1)
+    def _():
+        first = sz.rows - sz.hr
+        s_ref[:, first : first + 32, :] += rows
+        m_ref[:, 0 : first + RMAX, :] = meas_ref[:, sz.hr - RMAX :, :]
+        m_ref[:, first + RMAX : first + 2 * RMAX, :] = meas[:, 0:RMAX, :]
+
+    row = part * sz.hr + iota(s_ref.shape, 1)
     spot = strip_ref[0] * sz.rows + row - RMAX
-    inside = (row < sz.e) & (spot >= 0) & (spot < sz.total) & (iota(s_ref.shape, 1) < sz.w)
+    inside = (row < sz.e) & (spot >= 0) & (spot < sz.total) & (iota(s_ref.shape, 2) < sz.w)
     ratio_ref[...] = jnp.where(inside, m_ref[...] / s_ref[...], 0.0).astype(BF16)
 
 
@@ -294,7 +314,7 @@
 
     for z in range(sz.planes):
         step(z, 0)
-    rows_forward(sz, me_ref[0], rc_ref, s_ref, keep_ref, send_ref)
+    rows_forward(sz, rc_ref, s_ref, keep_ref, send_ref)
 
 
 def last_kernel(
@@ -352,24 +372,28 @@
     sz = Sizes(planes, rows, strips, cols, n, phase_map.shape[1])
     me = lax.axis_index("depth")
     strip = lax.axis_index("strip")
-    me_arg = me.reshape(1).astype(jnp.int32)
+    me_arg = (me ^ (strip % 2)).reshape(1).astype(jnp.int32)
     strip_arg = strip.reshape(1).astype(jnp.int32)
     to_core = [(i, i ^ 1) for i in range(n)]
     to_chip = [[(i, i ^ (2 * j)) for i in range(n)] for j in range(1, sz.half)]
-    swaps = []
-    for start in (0, 1):
-        below = [(i, i + 1) for i in range(start, strips - 1, 2)]
-        swaps.append(below + [(b, a) for a, b in below])
+    to_strip = []
+    for chip in range(sz.half):
+        for lower in range(1, strips):
+            row = (2 * chip + lower % 2) * strips
+            to_strip += [(row + lower, row + lower - 1), (row + lower - 1, row + lower)]
+        for edge, core in ((0, 0), (strips - 1, strips % 2)):
+            pair = [(2 * c + core) * strips + edge for c in (chip, chip ^ 1)]
+            to_strip.append(tuple(pair))
 
     volume = pltpu.with_memory_space_constraint(volume, pltpu.HBM)
-    meas = lax.dynamic_slice_in_dim(measured, me * sz.w, sz.w, axis=1)
-    meas = jnp.pad(meas, ((0, 0), (0, sz.wl - sz.w)))
+    meas = lax.dynamic_slice_in_dim(measured, (me // 2) * 2 * sz.w, 2 * sz.w, axis=1)
+    meas = jnp.stack([meas[:, 0 : sz.w], meas[:, sz.w :]])
+    meas = jnp.pad(meas, ((0, 0), (0, 0), (0, sz.wl - sz.w)))
     by_family = col_taps.transpose(1, 0, 2)
 
-    flat = shape((sz.ep, sz.wl), BF16)
-    flat32 = shape((sz.ep, sz.wl), F32)
-    edge = shape((64, sz.wl), BF16)
-    halves = [shape((sz.half, sz.ep, sz.wl), F32), shape((sz.half, sz.ep, sz.wl), BF16)]
+    flat = shape((2, sz.hr, sz.wl), BF16)
+    flat32 = shape((2, sz.hr, sz.wl), F32)
+    halves = [shape((n, sz.hr, sz.wl), F32), shape((n, sz.hr, sz.wl), BF16)]
     blocked = shape((planes, n, rows, sz.wl), F32)
     tap_args = tuple(
         pltpu.with_memory_space_constraint(x, pltpu.HBM)
@@ -434,22 +458,23 @@
                 (strip_arg, *tap_args, own),
                 8, 2,
             )
-        recvs = [lax.ppermute(part, "depth", pairs) for part, pairs in zip(sends, to_chip)]
-        total, *edges = call(
-            chip_sum_kernel, sz, "chip_sum",
+        recvs = [lax.ppermute(part, "depth", pairs) for part, pairs in zip(sends, to_chip)][::-1]
+        total, edge = call(
+            functools.partial(chip_sum_kernel, first=iteration == 0), sz, "chip_sum",
             [SMEM, ANY] + [VMEM] * (2 + len(recvs)),
-            [VMEM] * 3,
-            [flat32, edge, edge],
-            [], (strip_arg, tables[3], own, meas, *recvs), 4,
+            [VMEM] * 2,
+            [flat32, shape((2, 64 if iteration == 0 else 32, sz.wl), BF16)],
+            [], (me_arg, tables[3], own, meas, *recvs), 4,
         )
-        edges = [lax.ppermute(part, "strip", pairs) for part, pairs in zip(edges, swaps)]
+        edge = lax.ppermute(edge, ("depth", "strip"), to_strip)
+        first_edge = edge if iteration == 0 else first_edge
         ratio = call(
             ratio_kernel, sz, "ratio",
-            [SMEM] + [VMEM] * 4,
+            [SMEM] * 2 + [VMEM] * 4,
             VMEM,
             flat,
-            [pltpu.VMEM((sz.ep, sz.wl), F32)] * 2,
-            (strip_arg, total, meas, *edges), 4,
+            [pltpu.VMEM(flat32.shape, F32)] * 2,
+            (me_arg, strip_arg, total, meas, edge, first_edge), 4,
         )
         chips = [lax.ppermute(ratio, "depth", pairs) for pairs in to_chip]
         if iteration == 0:
@@ -461,7 +486,7 @@
             )
         same = call(
             stack_kernel, sz, "stack",
-            [ANY] + [VMEM] * sz.half, VMEM, halves[1],
+            [ANY] + [VMEM] * sz.half, VMEM, shape((sz.half,) + flat.shape, BF16),
             [], (current, ratio, *chips), 4,
         )
         other = lax.ppermute(same, "depth", to_core)

time: 61.6 us -> 57.2 us (0.929)
  the two profiles are of different devices: /device:TPU:17 before, /device:TPU:0 now
where the time goes in v3:
time: 57.2 us; the launch traced here: 57 us
  waiting for transfers between devices  20.7 us (36%)
  starting transfers between devices  18.3 us (32%)
  Pallas kernels  16.6 us (29%)
  local copies, waits for them, and re-layouts  1.13 us (2%)
    pallas_call x13, Pallas kernels, call(): pl.pallas_call(functools.partial(kernel, sz), in_specs=in_specs, out_spec...  16.6 us
    ppermute x6, starting transfers between devices, local(): lax.ppermute(part, 'depth', pairs)  8.08 us
    ppermute x6, starting transfers between devices, local(): chips = [lax.ppermute(ratio, 'depth', pairs) for pairs in to_chip]  7.11 us
    ppermute x2, waiting for transfers between devices, local(): edge = lax.ppermute(edge, ('depth', 'strip'), to_strip)  6.05 us
    ppermute x6, waiting for transfers between devices, local(): lax.ppermute(part, 'depth', pairs)  5.61 us
    ppermute x6, waiting for transfers between devices, local(): chips = [lax.ppermute(ratio, 'depth', pairs) for pairs in to_chip]  4.16 us
    ppermute x2, waiting for transfers between devices, local(): other = lax.ppermute(same, 'depth', to_core)  3.23 us
    ppermute x2, starting transfers between devices, local(): edge = lax.ppermute(edge, ('depth', 'strip'), to_strip)  2.26 us
  transfers between devices with their start and end apart: 18, of which 14 were waited for; matrix products, arithmetic and copies ran while one was open for 2% of the time, Pallas kernels for 9%

profile of v3, /device:TPU:0, one launch (start us, length us, event | category | flops | bytes accessed | tf_op | source)
XLA Modules:
  0.0 57.0 jit_solution(10991140455475707953)
XLA Ops:
  0.0 3.5 %first.1 = (bf16[160,512]{1,0:T(8,128)(2,1)S(1)}, f32[8,80,256]{2,1,0:T(8,128)S(1)}, bf16[8,80,256]{2,1,0:T(8,128)(2,1)S(1)}) custom-call(s32[1]{0:T(128)} %bitcast.me_ref, s32[4]{0:T(128)} %radius_hbm.3, s32[4,15]{1,0:T(4,128)} %phase_hbm.3, f32[4,31]{1,0:T(4,128)} %row_hbm.3, f32[15,4,31]{2,1,0:T(4,128)} %bitcast.7, f32[4,120,1920]{2,1,0:T(8,128)} %vol_hbm.3), custom_call_target="tpu_custom_call" | custom-call | bytes 12000000 | tf_op jit(solution)/shard_map/first/pallas_call | solution.py:354
  3.5 0.5 collective-permute-start
  4.1 1.1 %dynamic-slice_bitcast_fusion.1 = (f32[1,120,240]{2,1,0:T(8,128)S(1)}, f32[1,120,240]{2,1,0:T(8,128)S(1)}) fusion(f32[120,1920]{1,0:T(8,128)} %param.7, s32[]{:T(128)S(6)} %select_n.16, s32[]{:T(128)S(6)} %add.12), kind=kLoop, calls=%fused_computation.3 | loop fusion | bytes 460808 | tf_op jit(solution)/shard_map/stack | solution.py:390
  5.2 0.1 collective-permute-done.recv_ref
  5.3 0.1 core_sum.2
  5.4 3.9 %collective-permute-start.1 = (bf16[2,80,256]{2,1,0:T(8,128)(2,1)S(1)}, bf16[2,80,256]{2,1,0:T(8,128)(2,1)S(1)}, u32[]{:S(2)}, u32[]{:S(2)}) collective-permute-start(bf16[2,80,256]{2,1,0:T(8,128)(2,1)S(1)} %get-tuple-element.32), channel_id=1, source_target_pairs={{0,24},{4,28},{8,16},{12,20},{16,8},{20,12},{24,0},{28,4},{1,25},{... | collective-permute-start | bytes 245768 | tf_op jit(solution)/shard_map/ppermute | solution.py:461
  9.3 0.5 collective-permute-start.2
  9.7 0.2 collective-permute-start.3
  9.9 2.3 %tables.1 = (bf16[4,512,256]{2,1,0:T(8,128)(2,1)S(1)}, bf16[4,512,256]{2,1,0:T(8,128)(2,1)S(1)}, bf16[4,128,256]{2,1,0:T(8,128)(2,1)S(1)}, f32[4,128,1]{2,1,0:T(8,128)S(1)}, f32[4,8,256]{2,1,0:T(8,128)S(1)}) custom-call(s32[1]{0:T(128)} %bitcast.1.strip_ref, s32[4]{0:T(128)} %radius_hbm.3, s32[4,15]{1,0:T(4,128)} %phase_hbm.3, f32[4,31]{1,0:T(4,128)} %row_hbm.3, ...), custom_call_target="tpu_custom_call" | custom-call | bytes 6000000 | tf_op jit(solution)/shard_map/tables/pallas_call | solution.py:354
  12.2 0.0 collective-permute-done.1.refs_0_
  12.2 1.5 %collective-permute-done.2.refs_1_ = bf16[2,80,256]{2,1,0:T(8,128)(2,1)S(1)} collective-permute-done((bf16[2,80,256]{2,1,0:T(8,128)(2,1)S(1)}, bf16[2,80,256]{2,1,0:T(8,128)(2,1)S(1)}, u32[]{:S(2)}, u32[]{:S(2)}) %collective-permute-start.2) | collective-permute-done | bytes 81952 | tf_op jit(solution)/shard_map/ppermute | solution.py:461
  13.8 0.4 collective-permute-done.3.refs_2_
  14.2 1.4 %collective-permute-start.4 = (bf16[2,64,256]{2,1,0:T(8,128)(2,1)S(1)}, bf16[2,64,256]{2,1,0:T(8,128)(2,1)S(1)}, u32[]{:S(2)}, u32[]{:S(2)}) collective-permute-start(bf16[2,64,256]{2,1,0:T(8,128)(2,1)S(1)} %get-tuple-element.36), channel_id=1, source_target_pairs={{5,4},{4,5},{2,1},{1,2},{7,6},{6,7},{0,8},{3,11},{13,12},{12,13},{... | collective-permute-start | bytes 196616 | tf_op jit(solution)/shard_map/ppermute | solution.py:469
  15.6 2.9 %collective-permute-done.4.edge_ref.first_edge_ref = bf16[2,64,256]{2,1,0:T(8,128)(2,1)S(1)} collective-permute-done((bf16[2,64,256]{2,1,0:T(8,128)(2,1)S(1)}, bf16[2,64,256]{2,1,0:T(8,128)(2,1)S(1)}, u32[]{:S(2)}, u32[]{:S(2)}) %collective-permute-start.4) | collective-permute-done | bytes 65568 | tf_op jit(solution)/shard_map/ppermute | solution.py:469
  18.6 0.1 ratio.2.after_ref.refs_0_
  18.7 1.6 %collective-permute-start.7 = (bf16[2,80,256]{2,1,0:T(8,128)(2,1)S(1)}, bf16[2,80,256]{2,1,0:T(8,128)(2,1)S(1)}, u32[]{:S(2)}, u32[]{:S(2)}) collective-permute-start(bf16[2,80,256]{2,1,0:T(8,128)(2,1)S(1)} %ratio.2.after_ref.refs_0_), channel_id=1, source_target_pairs={{0,24},{4,28},{8,16},{12,20},{16,8},{20,12},{24,0},{28,4},{1,25},{... | collective-permute-start | bytes 245768 | tf_op jit(solution)/shard_map/ppermute | solution.py:479
  20.2 1.3 %collective-permute-start.6 = (bf16[2,80,256]{2,1,0:T(8,128)(2,1)S(1)}, bf16[2,80,256]{2,1,0:T(8,128)(2,1)S(1)}, u32[]{:S(2)}, u32[]{:S(2)}) collective-permute-start(bf16[2,80,256]{2,1,0:T(8,128)(2,1)S(1)} %ratio.2.after_ref.refs_0_), channel_id=1, source_target_pairs={{0,16},{4,20},{8,24},{12,28},{16,0},{20,4},{24,8},{28,12},{1,17},{... | collective-permute-start | bytes 245768 | tf_op jit(solution)/shard_map/ppermute | solution.py:479
  21.5 0.7 %collective-permute-start.5 = (bf16[2,80,256]{2,1,0:T(8,128)(2,1)S(1)}, bf16[2,80,256]{2,1,0:T(8,128)(2,1)S(1)}, u32[]{:S(2)}, u32[]{:S(2)}) collective-permute-start(bf16[2,80,256]{2,1,0:T(8,128)(2,1)S(1)} %ratio.2.after_ref.refs_0_), channel_id=1, source_target_pairs={{0,8},{4,12},{8,0},{12,4},{16,24},{20,28},{24,16},{28,20},{1,9},{5... | collective-permute-start | bytes 245768 | tf_op jit(solution)/shard_map/ppermute | solution.py:479
  22.2 2.8 %blocks.1.after_ref.vol_ref = f32[4,8,120,256]{3,2,1,0:T(8,128)S(1)} custom-call(f32[4,120,1920]{2,1,0:T(8,128)} %vol_hbm.3, bf16[2,80,256]{2,1,0:T(8,128)(2,1)S(1)} %ratio.2.after_ref.refs_0_), custom_call_target="tpu_custom_call" | custom-call | bytes 9000000 | tf_op jit(solution)/shard_map/blocks/pallas_call | solution.py:354
  25.0 0.0 collective-permute-done.7.refs_3_
  25.0 0.0 collective-permute-done.6.refs_2_
  25.0 1.0 %collective-permute-done.5.refs_1_ = bf16[2,80,256]{2,1,0:T(8,128)(2,1)S(1)} collective-permute-done((bf16[2,80,256]{2,1,0:T(8,128)(2,1)S(1)}, bf16[2,80,256]{2,1,0:T(8,128)(2,1)S(1)}, u32[]{:S(2)}, u32[]{:S(2)}) %collective-permute-start.5) | collective-permute-done | bytes 81952 | tf_op jit(solution)/shard_map/ppermute | solution.py:479
  26.0 0.1 collective-permute-start.8
  26.1 1.6 %collective-permute-done.8.other_ref = bf16[4,2,80,256]{3,2,1,0:T(8,128)(2,1)S(1)} collective-permute-done((bf16[4,2,80,256]{3,2,1,0:T(8,128)(2,1)S(1)}, bf16[4,2,80,256]{3,2,1,0:T(8,128)(2,1)S(1)}, u32[]{:S(2)}, u32[]{:S(2)}) %collective-permute-start.8) | collective-permute-done | bytes 327712 | tf_op jit(solution)/shard_map/ppermute | solution.py:492
  27.7 3.9 %middle.1 = (f32[4,8,120,256]{3,2,1,0:T(8,128)S(1)}, f32[8,80,256]{2,1,0:T(8,128)S(1)}, bf16[8,80,256]{2,1,0:T(8,128)(2,1)S(1)}) custom-call(s32[1]{0:T(128)} %bitcast.me_ref, bf16[4,2,80,256]{3,2,1,0:T(8,128)(2,1)S(1)} %stack.14.same_ref, bf16[4,2,80,256]{3,2,1,0:T(8,128)(2,1)S(1)} %collective-permute-done.8.other_ref, ...), custom_call_target="tpu_custom_call" | custom-call | bytes 15000000 | tf_op jit(solution)/shard_map/middle/pallas_call | solution.py:354
  31.6 0.2 collective-permute-start.9
  31.8 1.5 %collective-permute-done.9.recv_ref = bf16[8,80,256]{2,1,0:T(8,128)(2,1)S(1)} collective-permute-done((bf16[8,80,256]{2,1,0:T(8,128)(2,1)S(1)}, bf16[8,80,256]{2,1,0:T(8,128)(2,1)S(1)}, u32[]{:S(2)}, u32[]{:S(2)}) %collective-permute-start.9) | collective-permute-done | bytes 327712 | tf_op jit(solution)/shard_map/ppermute | solution.py:437
  33.3 0.1 core_sum.3
  33.3 1.7 %collective-permute-start.10 = (bf16[2,80,256]{2,1,0:T(8,128)(2,1)S(1)}, bf16[2,80,256]{2,1,0:T(8,128)(2,1)S(1)}, u32[]{:S(2)}, u32[]{:S(2)}) collective-permute-start(bf16[2,80,256]{2,1,0:T(8,128)(2,1)S(1)} %get-tuple-element.46), channel_id=1, source_target_pairs={{0,24},{4,28},{8,16},{12,20},{16,8},{20,12},{24,0},{28,4},{1,25},{... | collective-permute-start | bytes 245768 | tf_op jit(solution)/shard_map/ppermute | solution.py:461
  35.0 0.5 collective-permute-start.11
  35.5 1.3 %collective-permute-start.12 = (bf16[2,80,256]{2,1,0:T(8,128)(2,1)S(1)}, bf16[2,80,256]{2,1,0:T(8,128)(2,1)S(1)}, u32[]{:S(2)}, u32[]{:S(2)}) collective-permute-start(bf16[2,80,256]{2,1,0:T(8,128)(2,1)S(1)} %get-tuple-element.48), channel_id=1, source_target_pairs={{0,8},{4,12},{8,0},{12,4},{16,24},{20,28},{24,16},{28,20},{1,9},{5... | collective-permute-start | bytes 245768 | tf_op jit(solution)/shard_map/ppermute | solution.py:461
  36.9 2.0 %collective-permute-done.10.refs_0_ = bf16[2,80,256]{2,1,0:T(8,128)(2,1)S(1)} collective-permute-done((bf16[2,80,256]{2,1,0:T(8,128)(2,1)S(1)}, bf16[2,80,256]{2,1,0:T(8,128)(2,1)S(1)}, u32[]{:S(2)}, u32[]{:S(2)}) %collective-permute-start.10) | collective-permute-done | bytes 81952 | tf_op jit(solution)/shard_map/ppermute | solution.py:461
  38.9 1.6 %collective-permute-done.11.refs_1_ = bf16[2,80,256]{2,1,0:T(8,128)(2,1)S(1)} collective-permute-done((bf16[2,80,256]{2,1,0:T(8,128)(2,1)S(1)}, bf16[2,80,256]{2,1,0:T(8,128)(2,1)S(1)}, u32[]{:S(2)}, u32[]{:S(2)}) %collective-permute-start.11) | collective-permute-done | bytes 81952 | tf_op jit(solution)/shard_map/ppermute | solution.py:461
  40.5 0.0 collective-permute-done.12.refs_2_
  40.6 0.9 %collective-permute-start.13 = (bf16[2,32,256]{2,1,0:T(8,128)(2,1)S(1)}, bf16[2,32,256]{2,1,0:T(8,128)(2,1)S(1)}, u32[]{:S(2)}, u32[]{:S(2)}) collective-permute-start(bf16[2,32,256]{2,1,0:T(8,128)(2,1)S(1)} %get-tuple-element.50), channel_id=1, source_target_pairs={{5,4},{4,5},{2,1},{1,2},{7,6},{6,7},{0,8},{3,11},{13,12},{12,13},{... | collective-permute-start | bytes 98312 | tf_op jit(solution)/shard_map/ppermute | solution.py:469
  41.4 3.1 %collective-permute-done.13.edge_ref = bf16[2,32,256]{2,1,0:T(8,128)(2,1)S(1)} collective-permute-done((bf16[2,32,256]{2,1,0:T(8,128)(2,1)S(1)}, bf16[2,32,256]{2,1,0:T(8,128)(2,1)S(1)}, u32[]{:S(2)}, u32[]{:S(2)}) %collective-permute-start.13) | collective-permute-done | bytes 32800 | tf_op jit(solution)/shard_map/ppermute | solution.py:469
  44.5 0.3 ratio.3.refs_0_
  44.8 1.7 %collective-permute-start.16 = (bf16[2,80,256]{2,1,0:T(8,128)(2,1)S(1)}, bf16[2,80,256]{2,1,0:T(8,128)(2,1)S(1)}, u32[]{:S(2)}, u32[]{:S(2)}) collective-permute-start(bf16[2,80,256]{2,1,0:T(8,128)(2,1)S(1)} %ratio.3.refs_0_), channel_id=1, source_target_pairs={{0,24},{4,28},{8,16},{12,20},{16,8},{20,12},{24,0},{28,4},{1,25},{... | collective-permute-start | bytes 245768 | tf_op jit(solution)/shard_map/ppermute | solution.py:479
  46.5 0.6 %collective-permute-start.15 = (bf16[2,80,256]{2,1,0:T(8,128)(2,1)S(1)}, bf16[2,80,256]{2,1,0:T(8,128)(2,1)S(1)}, u32[]{:S(2)}, u32[]{:S(2)}) collective-permute-start(bf16[2,80,256]{2,1,0:T(8,128)(2,1)S(1)} %ratio.3.refs_0_), channel_id=1, source_target_pairs={{0,16},{4,20},{8,24},{12,28},{16,0},{20,4},{24,8},{28,12},{1,17},{... | collective-permute-start | bytes 245768 | tf_op jit(solution)/shard_map/ppermute | solution.py:479
  47.1 1.2 %collective-permute-start.14 = (bf16[2,80,256]{2,1,0:T(8,128)(2,1)S(1)}, bf16[2,80,256]{2,1,0:T(8,128)(2,1)S(1)}, u32[]{:S(2)}, u32[]{:S(2)}) collective-permute-start(bf16[2,80,256]{2,1,0:T(8,128)(2,1)S(1)} %ratio.3.refs_0_), channel_id=1, source_target_pairs={{0,8},{4,12},{8,0},{12,4},{16,24},{20,28},{24,16},{28,20},{1,9},{5... | collective-permute-start | bytes 245768 | tf_op jit(solution)/shard_map/ppermute | solution.py:479
  48.4 2.4 %collective-permute-done.16.refs_3_ = bf16[2,80,256]{2,1,0:T(8,128)(2,1)S(1)} collective-permute-done((bf16[2,80,256]{2,1,0:T(8,128)(2,1)S(1)}, bf16[2,80,256]{2,1,0:T(8,128)(2,1)S(1)}, u32[]{:S(2)}, u32[]{:S(2)}) %collective-permute-start.16) | collective-permute-done | bytes 81952 | tf_op jit(solution)/shard_map/ppermute | solution.py:479
  50.8 0.7 %collective-permute-done.15.refs_2_ = bf16[2,80,256]{2,1,0:T(8,128)(2,1)S(1)} collective-permute-done((bf16[2,80,256]{2,1,0:T(8,128)(2,1)S(1)}, bf16[2,80,256]{2,1,0:T(8,128)(2,1)S(1)}, u32[]{:S(2)}, u32[]{:S(2)}) %collective-permute-start.15) | collective-permute-done | bytes 81952 | tf_op jit(solution)/shard_map/ppermute | solution.py:479
  51.4 0.1 collective-permute-done.14.refs_1_
  51.6 0.1 collective-permute-start.17
  51.7 1.6 %collective-permute-done.17.other_ref = bf16[4,2,80,256]{3,2,1,0:T(8,128)(2,1)S(1)} collective-permute-done((bf16[4,2,80,256]{3,2,1,0:T(8,128)(2,1)S(1)}, bf16[4,2,80,256]{3,2,1,0:T(8,128)(2,1)S(1)}, u32[]{:S(2)}, u32[]{:S(2)}) %collective-permute-start.17) | collective-permute-done | bytes 327712 | tf_op jit(solution)/shard_map/ppermute | solution.py:492
  53.3 3.5 %last.1 = f32[4,120,1920]{2,1,0:T(8,128)} custom-call(s32[1]{0:T(128)} %bitcast.me_ref, bf16[4,2,80,256]{3,2,1,0:T(8,128)(2,1)S(1)} %stack.15.same_ref, bf16[4,2,80,256]{3,2,1,0:T(8,128)(2,1)S(1)} %collective-permute-done.17.other_ref, bf16[4,512,256]{2,1,0:T(8,128)(2,1)S(1)} %get-tuple-element.38.wb_ref, bf16[4,128,256]{2,1,0:T(8,128)(2,1)S(1)} %get-tuple-element.39.rt_ref, ...), custom_call_target="tpu_custom_call" | custom-call | bytes 15000000 | tf_op jit(solution)/shard_map/last/pallas_call | solution.py:354
  (5 shorter events, 0.2 us)
Async XLA Ops:
  3.5 1.8 %collective-permute-start = (bf16[8,80,256]{2,1,0:T(8,128)(2,1)S(1)}, bf16[8,80,256]{2,1,0:T(8,128)(2,1)S(1)}, u32[]{:S(2)}, u32[]{:S(2)}) collective-permute-start(bf16[8,80,256]{2,1,0:T(8,128)(2,1)S(1)} %get-tuple-element.29), channel_id=1, source_target_pairs={{0,4},{4,0},{8,12},{12,8},{16,20},{20,16},{24,28},{28,24},{1,5},{5... | collective-permute-start | bytes 983048 | tf_op jit(solution)/shard_map/ppermute | solution.py:437
  5.4 6.8 %collective-permute-start.1 = (bf16[2,80,256]{2,1,0:T(8,128)(2,1)S(1)}, bf16[2,80,256]{2,1,0:T(8,128)(2,1)S(1)}, u32[]{:S(2)}, u32[]{:S(2)}) collective-permute-start(bf16[2,80,256]{2,1,0:T(8,128)(2,1)S(1)} %get-tuple-element.32), channel_id=1, source_target_pairs={{0,24},{4,28},{8,16},{12,20},{16,8},{20,12},{24,0},{28,4},{1,25},{... | collective-permute-start | bytes 245768 | tf_op jit(solution)/shard_map/ppermute | solution.py:461
  9.3 4.5 %collective-permute-start.2 = (bf16[2,80,256]{2,1,0:T(8,128)(2,1)S(1)}, bf16[2,80,256]{2,1,0:T(8,128)(2,1)S(1)}, u32[]{:S(2)}, u32[]{:S(2)}) collective-permute-start(bf16[2,80,256]{2,1,0:T(8,128)(2,1)S(1)} %get-tuple-element.33), channel_id=1, source_target_pairs={{0,16},{4,20},{8,24},{12,28},{16,0},{20,4},{24,8},{28,12},{1,17},{... | collective-permute-start | bytes 245768 | tf_op jit(solution)/shard_map/ppermute | solution.py:461
  9.7 4.4 %collective-permute-start.3 = (bf16[2,80,256]{2,1,0:T(8,128)(2,1)S(1)}, bf16[2,80,256]{2,1,0:T(8,128)(2,1)S(1)}, u32[]{:S(2)}, u32[]{:S(2)}) collective-permute-start(bf16[2,80,256]{2,1,0:T(8,128)(2,1)S(1)} %get-tuple-element.34), channel_id=1, source_target_pairs={{0,8},{4,12},{8,0},{12,4},{16,24},{20,28},{24,16},{28,20},{1,9},{5... | collective-permute-start | bytes 245768 | tf_op jit(solution)/shard_map/ppermute | solution.py:461
  14.2 4.3 %collective-permute-start.4 = (bf16[2,64,256]{2,1,0:T(8,128)(2,1)S(1)}, bf16[2,64,256]{2,1,0:T(8,128)(2,1)S(1)}, u32[]{:S(2)}, u32[]{:S(2)}) collective-permute-start(bf16[2,64,256]{2,1,0:T(8,128)(2,1)S(1)} %get-tuple-element.36), channel_id=1, source_target_pairs={{5,4},{4,5},{2,1},{1,2},{7,6},{6,7},{0,8},{3,11},{13,12},{12,13},{... | collective-permute-start | bytes 196616 | tf_op jit(solution)/shard_map/ppermute | solution.py:469
  18.7 6.3 %collective-permute-start.7 = (bf16[2,80,256]{2,1,0:T(8,128)(2,1)S(1)}, bf16[2,80,256]{2,1,0:T(8,128)(2,1)S(1)}, u32[]{:S(2)}, u32[]{:S(2)}) collective-permute-start(bf16[2,80,256]{2,1,0:T(8,128)(2,1)S(1)} %ratio.2.after_ref.refs_0_), channel_id=1, source_target_pairs={{0,24},{4,28},{8,16},{12,20},{16,8},{20,12},{24,0},{28,4},{1,25},{... | collective-permute-start | bytes 245768 | tf_op jit(solution)/shard_map/ppermute | solution.py:479
  20.2 4.8 %collective-permute-start.6 = (bf16[2,80,256]{2,1,0:T(8,128)(2,1)S(1)}, bf16[2,80,256]{2,1,0:T(8,128)(2,1)S(1)}, u32[]{:S(2)}, u32[]{:S(2)}) collective-permute-start(bf16[2,80,256]{2,1,0:T(8,128)(2,1)S(1)} %ratio.2.after_ref.refs_0_), channel_id=1, source_target_pairs={{0,16},{4,20},{8,24},{12,28},{16,0},{20,4},{24,8},{28,12},{1,17},{... | collective-permute-start | bytes 245768 | tf_op jit(solution)/shard_map/ppermute | solution.py:479
  21.5 4.4 %collective-permute-start.5 = (bf16[2,80,256]{2,1,0:T(8,128)(2,1)S(1)}, bf16[2,80,256]{2,1,0:T(8,128)(2,1)S(1)}, u32[]{:S(2)}, u32[]{:S(2)}) collective-permute-start(bf16[2,80,256]{2,1,0:T(8,128)(2,1)S(1)} %ratio.2.after_ref.refs_0_), channel_id=1, source_target_pairs={{0,8},{4,12},{8,0},{12,4},{16,24},{20,28},{24,16},{28,20},{1,9},{5... | collective-permute-start | bytes 245768 | tf_op jit(solution)/shard_map/ppermute | solution.py:479
  26.0 1.7 %collective-permute-start.8 = (bf16[4,2,80,256]{3,2,1,0:T(8,128)(2,1)S(1)}, bf16[4,2,80,256]{3,2,1,0:T(8,128)(2,1)S(1)}, u32[]{:S(2)}, u32[]{:S(2)}) collective-permute-start(bf16[4,2,80,256]{3,2,1,0:T(8,128)(2,1)S(1)} %stack.14.same_ref), channel_id=1, source_target_pairs={{0,4},{4,0},{8,12},{12,8},{16,20},{20,16},{24,28},{28,24},{1,5},{5... | collective-permute-start | bytes 983048 | tf_op jit(solution)/shard_map/ppermute | solution.py:492
  31.6 1.7 %collective-permute-start.9 = (bf16[8,80,256]{2,1,0:T(8,128)(2,1)S(1)}, bf16[8,80,256]{2,1,0:T(8,128)(2,1)S(1)}, u32[]{:S(2)}, u32[]{:S(2)}) collective-permute-start(bf16[8,80,256]{2,1,0:T(8,128)(2,1)S(1)} %get-tuple-element.44), channel_id=1, source_target_pairs={{0,4},{4,0},{8,12},{12,8},{16,20},{20,16},{24,28},{28,24},{1,5},{5... | collective-permute-start | bytes 983048 | tf_op jit(solution)/shard_map/ppermute | solution.py:437
  33.3 5.6 %collective-permute-start.10 = (bf16[2,80,256]{2,1,0:T(8,128)(2,1)S(1)}, bf16[2,80,256]{2,1,0:T(8,128)(2,1)S(1)}, u32[]{:S(2)}, u32[]{:S(2)}) collective-permute-start(bf16[2,80,256]{2,1,0:T(8,128)(2,1)S(1)} %get-tuple-element.46), channel_id=1, source_target_pairs={{0,24},{4,28},{8,16},{12,20},{16,8},{20,12},{24,0},{28,4},{1,25},{... | collective-permute-start | bytes 245768 | tf_op jit(solution)/shard_map/ppermute | solution.py:461
  35.0 5.5 %collective-permute-start.11 = (bf16[2,80,256]{2,1,0:T(8,128)(2,1)S(1)}, bf16[2,80,256]{2,1,0:T(8,128)(2,1)S(1)}, u32[]{:S(2)}, u32[]{:S(2)}) collective-permute-start(bf16[2,80,256]{2,1,0:T(8,128)(2,1)S(1)} %get-tuple-element.47), channel_id=1, source_target_pairs={{0,16},{4,20},{8,24},{12,28},{16,0},{20,4},{24,8},{28,12},{1,17},{... | collective-permute-start | bytes 245768 | tf_op jit(solution)/shard_map/ppermute | solution.py:461
  35.5 5.0 %collective-permute-start.12 = (bf16[2,80,256]{2,1,0:T(8,128)(2,1)S(1)}, bf16[2,80,256]{2,1,0:T(8,128)(2,1)S(1)}, u32[]{:S(2)}, u32[]{:S(2)}) collective-permute-start(bf16[2,80,256]{2,1,0:T(8,128)(2,1)S(1)} %get-tuple-element.48), channel_id=1, source_target_pairs={{0,8},{4,12},{8,0},{12,4},{16,24},{20,28},{24,16},{28,20},{1,9},{5... | collective-permute-start | bytes 245768 | tf_op jit(solution)/shard_map/ppermute | solution.py:461
  40.6 4.0 %collective-permute-start.13 = (bf16[2,32,256]{2,1,0:T(8,128)(2,1)S(1)}, bf16[2,32,256]{2,1,0:T(8,128)(2,1)S(1)}, u32[]{:S(2)}, u32[]{:S(2)}) collective-permute-start(bf16[2,32,256]{2,1,0:T(8,128)(2,1)S(1)} %get-tuple-element.50), channel_id=1, source_target_pairs={{5,4},{4,5},{2,1},{1,2},{7,6},{6,7},{0,8},{3,11},{13,12},{12,13},{... | collective-permute-start | bytes 98312 | tf_op jit(solution)/shard_map/ppermute | solution.py:469
  44.8 5.9 %collective-permute-start.16 = (bf16[2,80,256]{2,1,0:T(8,128)(2,1)S(1)}, bf16[2,80,256]{2,1,0:T(8,128)(2,1)S(1)}, u32[]{:S(2)}, u32[]{:S(2)}) collective-permute-start(bf16[2,80,256]{2,1,0:T(8,128)(2,1)S(1)} %ratio.3.refs_0_), channel_id=1, source_target_pairs={{0,24},{4,28},{8,16},{12,20},{16,8},{20,12},{24,0},{28,4},{1,25},{... | collective-permute-start | bytes 245768 | tf_op jit(solution)/shard_map/ppermute | solution.py:479
  46.5 4.9 %collective-permute-start.15 = (bf16[2,80,256]{2,1,0:T(8,128)(2,1)S(1)}, bf16[2,80,256]{2,1,0:T(8,128)(2,1)S(1)}, u32[]{:S(2)}, u32[]{:S(2)}) collective-permute-start(bf16[2,80,256]{2,1,0:T(8,128)(2,1)S(1)} %ratio.3.refs_0_), channel_id=1, source_target_pairs={{0,16},{4,20},{8,24},{12,28},{16,0},{20,4},{24,8},{28,12},{1,17},{... | collective-permute-start | bytes 245768 | tf_op jit(solution)/shard_map/ppermute | solution.py:479
  47.1 4.4 %collective-permute-start.14 = (bf16[2,80,256]{2,1,0:T(8,128)(2,1)S(1)}, bf16[2,80,256]{2,1,0:T(8,128)(2,1)S(1)}, u32[]{:S(2)}, u32[]{:S(2)}) collective-permute-start(bf16[2,80,256]{2,1,0:T(8,128)(2,1)S(1)} %ratio.3.refs_0_), channel_id=1, source_target_pairs={{0,8},{4,12},{8,0},{12,4},{16,24},{20,28},{24,16},{28,20},{1,9},{5... | collective-permute-start | bytes 245768 | tf_op jit(solution)/shard_map/ppermute | solution.py:479
  51.6 1.7 %collective-permute-start.17 = (bf16[4,2,80,256]{3,2,1,0:T(8,128)(2,1)S(1)}, bf16[4,2,80,256]{3,2,1,0:T(8,128)(2,1)S(1)}, u32[]{:S(2)}, u32[]{:S(2)}) collective-permute-start(bf16[4,2,80,256]{3,2,1,0:T(8,128)(2,1)S(1)} %stack.15.same_ref), channel_id=1, source_target_pairs={{0,4},{4,0},{8,12},{12,8},{16,20},{20,16},{24,28},{28,24},{1,5},{5... | collective-permute-start | bytes 983048 | tf_op jit(solution)/shard_map/ppermute | solution.py:492

commit v4 on v3

--- a/solution.py
+++ b/solution.py
@@ -11,6 +11,8 @@
 ITERS = 2
 SIDE = 16
 LANES = 128
+HALF = LANES // 2
+GROUP = 2
 
 F32 = jnp.float32
 BF16 = jnp.bfloat16
@@ -31,12 +33,15 @@
         self.wl = round_up(self.w, LANES)
         self.span = self.w + 2 * SIDE
         self.kp = round_up(self.span, LANES)
-        self.kb = self.wl + 2 * LANES
+        self.kb = self.wl + LANES
+        self.group = 1 if devices % GROUP else GROUP
         self.rp = round_up(rows, LANES)
         self.e = rows + 2 * RMAX
         self.ep = round_up(self.e, 32)
         self.hr = self.ep // 2
+        self.hp = round_up(self.hr, LANES)
         self.el = round_up(self.ep, LANES)
+        assert self.el == 2 * self.hp
         assert 32 <= rows - self.hr and rows - self.hr + 32 <= self.hr and (rows - self.hr) % 8 == 0
         self.ar = round_up(max(self.span, self.wl) + pitch, pitch)
         self.starts = [LANES + b * self.w - SIDE for b in range(devices)]
@@ -78,10 +83,9 @@
     def zeros(count):
         return [jnp.zeros((count, sz.wl), F32)] if count else []
 
-    lead = sz.w - (sz.wl - LANES) - SIDE
+    lead = sz.w - (sz.wl - LANES) - 2 * SIDE
     parts = [matrix[SIDE : SIDE + sz.w]] + zeros(sz.wl - sz.w)
-    parts += [matrix[SIDE + sz.w :]] + zeros(LANES - SIDE)
-    parts += zeros(lead) + [matrix[0:SIDE]] + zeros(sz.wl - sz.w)
+    parts += [matrix[SIDE + sz.w :]] + zeros(lead) + [matrix[0:SIDE]] + zeros(sz.wl - sz.w)
     return jnp.concatenate(parts, axis=0).astype(BF16)
 
 
@@ -96,12 +100,36 @@
     return jnp.where(iota(wide.shape, 0) < sz.rows, wide, 0.0)
 
 
-def side_by_side(sz, ref, b, height):
-    at = (b + 1) * height
-    here = ref[at : at + height, :]
-    after = ref[at + height : at + 2 * height, 0:LANES]
-    before = ref[at - height : at, sz.wl - LANES :]
-    return jnp.concatenate([here, after, before], axis=1)
+class Windows:
+    def __init__(self, sz, height, main_ref, side_ref):
+        self.sz, self.height, self.main, self.side = sz, height, main_ref, side_ref
+
+    def clear_sides(self):
+        self.side[...] = jnp.zeros_like(self.side)
+
+    def put(self, b, row, x):
+        sz = self.sz
+
+        def rows(block):
+            at = block * self.height + row
+            if not isinstance(at, int):
+                at = pl.multiple_of(at, 16)
+            return pl.ds(at, x.shape[0])
+
+        self.main[rows(b), :] = x
+        self.side[rows(b), 0:HALF] = x[:, 0:HALF]
+        self.side[rows(b + 2), HALF:] = x[:, sz.wl - HALF :]
+
+    def products(self, matrix):
+        sz, height = self.sz, self.height
+        for first in range(0, sz.n, sz.group):
+            count = sz.group * height
+            main = self.main[first * height : first * height + count, :]
+            side = self.side[(first + 1) * height : (first + 1) * height + count, :]
+            window = jnp.concatenate([main, side], axis=1)
+            out = jnp.dot(window, matrix, preferred_element_type=F32).astype(BF16)
+            for k in range(sz.group):
+                yield first + k, out[k * height : (k + 1) * height, :]
 
 
 def rows_forward(sz, rc_ref, s_ref, keep_ref, send_ref):
@@ -112,13 +140,12 @@
         keep_ref[b] = out[sz.hr :, :]
 
 
-def backward(sz, ratio_ref, matrix, rt, g_ref):
+def backward(sz, z, ratio, matrix, rt, own_ref, g_ref):
+    for b, out in ratio.products(matrix):
+        g_ref[b, 0 : sz.hr, :] = out
     for b in range(sz.n):
-        window = side_by_side(sz, ratio_ref, b, sz.ep)
-        out = jnp.dot(window, matrix, preferred_element_type=F32)
-        g_ref[b, 0 : sz.ep, :] = out.astype(BF16)
-    for b in range(sz.n):
-        back = jnp.dot(rt, g_ref[b], preferred_element_type=F32)
+        rows = jnp.concatenate([own_ref[z, b], g_ref[b]], axis=0)
+        back = jnp.dot(rt, rows, preferred_element_type=F32)
         yield b, back[0 : sz.rows, :]
 
 
@@ -127,18 +154,13 @@
     return icn[kind : kind + 1, :]
 
 
-def place_ratio(sz, me, same_ref, other_ref, ratio_ref, g_ref):
-    empty = jnp.zeros((sz.ep, sz.wl), BF16)
-    ratio_ref[0 : sz.ep, :] = empty
-    ratio_ref[(sz.n + 1) * sz.ep :, :] = empty
-    g_ref[:, sz.ep :, :] = jnp.zeros((sz.n, sz.el - sz.ep, sz.wl), BF16)
-    part = lax.rem(me, 2)
+def place_ratio(sz, me, stack_ref, main_ref, side_ref):
+    ratio = Windows(sz, sz.hr, main_ref, side_ref)
+    ratio.clear_sides()
     for j in range(sz.half):
-        chip = (me // 2) ^ j
-        for ref, rows in ((same_ref, part), (other_ref, 1 - part)):
-            for k in range(2):
-                at = (2 * chip + k + 1) * sz.ep + rows * sz.hr
-                ratio_ref[pl.ds(pl.multiple_of(at, sz.hr), sz.hr), :] = ref[j, k]
+        for k in range(2):
+            ratio.put(2 * ((me // 2) ^ j) + k, 0, stack_ref[j, k])
+    return ratio
 
 
 def first_kernel(
@@ -185,7 +207,7 @@
 
 
 def table_kernel(
-    sz, strip_ref, radius_hbm, phase_hbm, row_hbm, col_hbm, after_ref,
+    sz, me_ref, strip_ref, radius_hbm, phase_hbm, row_hbm, col_hbm, after_ref,
     wf_ref, wb_ref, rt_ref, irn_ref, icn_ref,
     radius_ref, phase_ref, row_ref, col_ref, t_ref, a_ref, sems,
 ):
@@ -196,7 +218,7 @@
     for copy in small:
         copy.wait()
     kind, col = iota((8, sz.kb), 0), iota((8, sz.kb), 1)
-    after, before = (col >= sz.wl) & (col < sz.wl + LANES), col >= sz.wl + LANES
+    after, before = (col >= sz.wl) & (col < sz.wl + HALF), col >= sz.wl + HALF
     ones = jnp.where(((kind == 1) & before) | ((kind == 2) & after), 0.0, 1.0).astype(BF16)
     for z in range(sz.planes):
         reach = radius_ref[z]
@@ -207,7 +229,13 @@
         norm = jnp.dot(ones, matrix, preferred_element_type=F32)
         icn_ref[z] = jnp.where(norm > 0.0, 1.0 / norm, 0.0)
         rt = row_matrix(sz, z, reach, row_ref)
-        rt_ref[z] = rt.astype(BF16)
+        lane = iota(rt.shape, 1)
+        top = jnp.where(lane < sz.hr, rt, 0.0)
+        bottom = jnp.where((lane >= sz.hr) & (lane < sz.ep), rt, 0.0)
+        bottom = pltpu.roll(bottom, sz.hp - sz.hr, 1)
+        both = top + bottom
+        turned = pltpu.roll(both, sz.hp, 1)
+        rt_ref[z] = jnp.where(lax.rem(me_ref[0], 2) == 0, both, turned).astype(BF16)
         row = strip_ref[0] * sz.rows + iota(rt.shape, 1) - RMAX
         norm = jnp.sum(jnp.where((row >= 0) & (row < sz.total), rt, 0.0), axis=1, keepdims=True)
         irn_ref[z] = jnp.where(norm > 0.0, 1.0 / norm, 0.0)
@@ -254,7 +282,8 @@
 
 
 def ratio_kernel(
-    sz, me_ref, strip_ref, sum_ref, meas_ref, edge_ref, first_edge_ref, ratio_ref, s_ref, m_ref
+    sz, me_ref, strip_ref, after_ref, sum_ref, meas_ref, edge_ref, first_edge_ref,
+    ratio_ref, s_ref, m_ref,
 ):
     part = lax.rem(me_ref[0], 2)
     s_ref[...] = sum_ref[...]
@@ -283,61 +312,57 @@
     ratio_ref[...] = jnp.where(inside, m_ref[...] / s_ref[...], 0.0).astype(BF16)
 
 
-def stack_kernel(sz, after_ref, *refs):
+def stack_kernel(sz, *refs):
     for j, ref in enumerate(refs[:-1]):
         refs[-1][j] = ref[...]
 
 
+def ahead_kernel(sz, me_ref, same_ref, wb_ref, own_ref, ratio_ref, ratio_side_ref):
+    ratio = place_ratio(sz, me_ref[0], same_ref, ratio_ref, ratio_side_ref)
+    own_ref[:, :, sz.hr :, :] = jnp.zeros((sz.planes, sz.n, sz.hp - sz.hr, sz.wl), BF16)
+    for z in range(sz.planes):
+        for b, out in ratio.products(wb_ref[z]):
+            own_ref[z, b, 0 : sz.hr, :] = out
+
+
 def middle_kernel(
-    sz, me_ref, same_ref, other_ref, wf_ref, wb_ref, rt_ref, irn_ref, icn_ref, rc_ref, vol_ref,
-    new_ref, keep_ref, send_ref, ratio_ref, g_ref, x_ref, s_ref,
+    sz, me_ref, own_ref, other_ref, wf_ref, wb_ref, rt_ref, irn_ref, icn_ref, rc_ref, vol_ref,
+    new_ref, keep_ref, send_ref,
+    ratio_ref, ratio_side_ref, g_ref, x_ref, x_side_ref, s_ref,
 ):
-    empty = jnp.zeros((sz.rp, sz.wl), BF16)
-    x_ref[0 : sz.rp, :] = empty
-    x_ref[(sz.n + 1) * sz.rp :, :] = empty
-    place_ratio(sz, me_ref[0], same_ref, other_ref, ratio_ref, g_ref)
+    ratio = place_ratio(sz, me_ref[0], other_ref, ratio_ref, ratio_side_ref)
+    g_ref[:, sz.hr :, :] = jnp.zeros((sz.n, sz.hp - sz.hr, sz.wl), BF16)
+    estimate = Windows(sz, sz.rp, x_ref, x_side_ref)
+    estimate.clear_sides()
     lead = jnp.zeros((sz.rp - sz.rows, sz.wl), F32)
-
-    def step(z, carry):
+    for z in range(sz.planes):
         icn, irn = icn_ref[z], irn_ref[z][0 : sz.rows]
-        for b, back in backward(sz, ratio_ref, wb_ref[z], rt_ref[z], g_ref):
+        for b, back in backward(sz, z, ratio, wb_ref[z], rt_ref[z], own_ref, g_ref):
             new = vol_ref[z, b] * back * (irn * block_norm(sz, b, icn))
             new_ref[z, b] = new
-            x_ref[(b + 1) * sz.rp : (b + 2) * sz.rp, :] = jnp.concatenate([new, lead]).astype(BF16)
-        matrix = wf_ref[z]
-        at = pl.ds(pl.multiple_of(z * sz.rp, sz.rp), sz.rp)
-        for b in range(sz.n):
-            window = side_by_side(sz, x_ref, b, sz.rp)
-            out = jnp.dot(window, matrix, preferred_element_type=F32)
-            s_ref[b, at, :] = out.astype(BF16)
-        return carry
-
+            estimate.put(b, 0, jnp.concatenate([new, lead]).astype(BF16))
+        for b, out in estimate.products(wf_ref[z]):
+            s_ref[b, z * sz.rp : (z + 1) * sz.rp, :] = out
+    rows_forward(sz, rc_ref, s_ref, keep_ref, send_ref)
+
+
+def last_kernel(
+    sz, me_ref, own_ref, other_ref, wb_ref, rt_ref, irn_ref, icn_ref, vol_ref,
+    out_hbm, ratio_ref, ratio_side_ref, g_ref, out_ref, sems,
+):
+    ratio = place_ratio(sz, me_ref[0], other_ref, ratio_ref, ratio_side_ref)
+    g_ref[:, sz.hr :, :] = jnp.zeros((sz.n, sz.hp - sz.hr, sz.wl), BF16)
+    copies = [
+        pltpu.make_async_copy(out_ref.at[z], out_hbm.at[z], sems.at[z]) for z in range(sz.planes)
+    ]
     for z in range(sz.planes):
-        step(z, 0)
-    rows_forward(sz, rc_ref, s_ref, keep_ref, send_ref)
-
-
-def last_kernel(
-    sz, me_ref, same_ref, other_ref, wb_ref, rt_ref, irn_ref, icn_ref, vol_ref,
-    out_hbm, ratio_ref, g_ref, out_ref, sems,
-):
-    place_ratio(sz, me_ref[0], same_ref, other_ref, ratio_ref, g_ref)
-
-    def copy(z):
-        return pltpu.make_async_copy(out_ref.at[z], out_hbm.at[z], sems.at[z])
-
-    def step(z, carry):
         icn, irn = icn_ref[z], irn_ref[z][0 : sz.rows]
-        for b, back in backward(sz, ratio_ref, wb_ref[z], rt_ref[z], g_ref):
+        for b, back in backward(sz, z, ratio, wb_ref[z], rt_ref[z], own_ref, g_ref):
             new = vol_ref[z, b] * back * (irn * block_norm(sz, b, icn))
             out_ref[z, :, b * sz.w : (b + 1) * sz.w] = new[:, 0 : sz.w]
-        copy(z).start()
-        return carry
-
-    for z in range(sz.planes):
-        step(z, 0)
-    for z in range(sz.planes):
-        copy(z).wait()
+        copies[z].start()
+    for copy in copies:
+        copy.wait()
 
 
 SMEM = pl.BlockSpec(memory_space=pltpu.SMEM)
@@ -410,9 +435,14 @@
         pltpu.VMEM((sz.ar, sz.kp), F32),
     ]
     s_scratch = pltpu.VMEM((n, planes * sz.rp, sz.wl), BF16)
-    ratio_scratch = [
-        pltpu.VMEM(((n + 2) * sz.ep, sz.wl), BF16),
-        pltpu.VMEM((n, sz.el, sz.wl), BF16),
+    place_scratch = [
+        pltpu.VMEM((n * sz.hr, sz.wl), BF16),
+        pltpu.VMEM(((n + 2) * sz.hr, LANES), BF16),
+    ]
+    ratio_scratch = place_scratch + [pltpu.VMEM((n, sz.hp, sz.wl), BF16)]
+    x_scratch = [
+        pltpu.VMEM((n * sz.rp, sz.wl), BF16),
+        pltpu.VMEM(((n + 2) * sz.rp, LANES), BF16),
     ]
     vol_scratch = pltpu.VMEM(volume.shape, F32)
 
@@ -445,7 +475,7 @@
         if tables is None:
             wf, *tables = call(
                 table_kernel, sz, "tables",
-                [SMEM] + [HBM] * 4 + [ANY],
+                [SMEM] * 2 + [HBM] * 4 + [ANY],
                 [VMEM] * 5,
                 [
                     shape((planes, sz.kb, sz.wl), BF16),
@@ -455,7 +485,7 @@
                     shape((planes, 8, sz.wl), F32),
                 ],
                 tap_scratch + row_scratch + [pltpu.SemaphoreType.DMA((4,))],
-                (strip_arg, *tap_args, own),
+                (me_arg, strip_arg, *tap_args, own),
                 8, 2,
             )
         recvs = [lax.ppermute(part, "depth", pairs) for part, pairs in zip(sends, to_chip)][::-1]
@@ -468,36 +498,42 @@
         )
         edge = lax.ppermute(edge, ("depth", "strip"), to_strip)
         first_edge = edge if iteration == 0 else first_edge
-        ratio = call(
-            ratio_kernel, sz, "ratio",
-            [SMEM] * 2 + [VMEM] * 4,
-            VMEM,
-            flat,
-            [pltpu.VMEM(flat32.shape, F32)] * 2,
-            (me_arg, strip_arg, total, meas, edge, first_edge), 4,
-        )
-        chips = [lax.ppermute(ratio, "depth", pairs) for pairs in to_chip]
         if iteration == 0:
             current = call(
                 block_kernel, sz, "blocks",
                 [HBM, ANY], VMEM, blocked,
                 [vol_scratch, pltpu.SemaphoreType.DMA((planes,))],
-                (volume, ratio), 12, 3,
+                (volume, total), 12, 3,
             )
+        ratio = call(
+            ratio_kernel, sz, "ratio",
+            [SMEM] * 2 + [ANY] + [VMEM] * 4,
+            VMEM,
+            flat,
+            [pltpu.VMEM(flat32.shape, F32)] * 2,
+            (me_arg, strip_arg, current, total, meas, edge, first_edge), 4,
+        )
+        chips = [lax.ppermute(ratio, "depth", pairs) for pairs in to_chip]
         same = call(
             stack_kernel, sz, "stack",
-            [ANY] + [VMEM] * sz.half, VMEM, shape((sz.half,) + flat.shape, BF16),
-            [], (current, ratio, *chips), 4,
+            [VMEM] * sz.half, VMEM, shape((sz.half,) + flat.shape, BF16),
+            [], (ratio, *chips), 4,
         )
         other = lax.ppermute(same, "depth", to_core)
+        own = call(
+            ahead_kernel, sz, "ahead",
+            [SMEM] + [VMEM] * 2, VMEM,
+            shape((planes, n, sz.hp, sz.wl), BF16),
+            place_scratch, (me_arg, same, tables[0]), 8,
+        )
         if iteration < ITERS - 1:
             current, keep, send = call(
                 middle_kernel, sz, "middle",
                 [SMEM] + [VMEM] * 9,
                 [VMEM] * 3,
                 [blocked, *halves],
-                ratio_scratch + [pltpu.VMEM(((n + 2) * sz.rp, sz.wl), BF16), s_scratch],
-                (me_arg, same, other, wf, *tables, rc, current),
+                ratio_scratch + x_scratch + [s_scratch],
+                (me_arg, own, other, wf, *tables, rc, current),
                 16, 5,
             )
         else:
@@ -507,7 +543,7 @@
                 HBM,
                 shape(volume.shape, F32),
                 ratio_scratch + [vol_scratch, pltpu.SemaphoreType.DMA((planes,))],
-                (me_arg, same, other, *tables, current),
+                (me_arg, own, other, *tables, current),
                 16, 5,
             )
     return current

time: 57.2 us -> 56 us (0.979)
  waiting for transfers between devices: 20.7 us -> 18.7 us
  Pallas kernels: 16.6 us -> 17.3 us
    ppermute x6, waiting for transfers between devices: 4.16 us -> 7.02 us  [local(): chips = [lax.ppermute(ratio, 'depth', pairs) for pairs in to_chip]]
    ppermute x2, waiting for transfers between devices: 6.05 us -> 3.21 us  [local(): edge = lax.ppermute(edge, ('depth', 'strip'), to_strip)]
    ppermute x2, waiting for transfers between devices: 3.23 us -> 1.39 us  [local(): other = lax.ppermute(same, 'depth', to_core)]
    pallas_call x13 -> x15, Pallas kernels: 16.6 us -> 17.3 us  [call(): pl.pallas_call(functools.partial(kernel, sz), in_specs=in_specs, out_spec...]
  transfers between devices with their start and end apart: 18 -> 18, of which waited for: 14 -> 16; matrix products, arithmetic and copies ran while one was open for 2% -> 2% of each run, Pallas kernels for 9% -> 13%
where the time goes in v4:
time: 56 us; the launch traced here: 55.8 us
  waiting for transfers between devices  18.7 us (33%)
  starting transfers between devices  18.4 us (33%)
  Pallas kernels  17.3 us (31%)
  local copies, waits for them, and re-layouts  1.13 us (2%)
    pallas_call x15, Pallas kernels, call(): pl.pallas_call(functools.partial(kernel, sz), in_specs=in_specs, out_spec...  17.3 us
    ppermute x6, starting transfers between devices, local(): lax.ppermute(part, 'depth', pairs)  8.08 us
    ppermute x6, starting transfers between devices, local(): chips = [lax.ppermute(ratio, 'depth', pairs) for pairs in to_chip]  7.11 us
    ppermute x6, waiting for transfers between devices, local(): chips = [lax.ppermute(ratio, 'depth', pairs) for pairs in to_chip]  7.02 us
    ppermute x6, waiting for transfers between devices, local(): lax.ppermute(part, 'depth', pairs)  5.46 us
    ppermute x2, waiting for transfers between devices, local(): edge = lax.ppermute(edge, ('depth', 'strip'), to_strip)  3.21 us
    ppermute x2, starting transfers between devices, local(): edge = lax.ppermute(edge, ('depth', 'strip'), to_strip)  2.32 us
    ppermute x2, waiting for transfers between devices, local(): recv = lax.ppermute(send, 'depth', to_core)  1.61 us
  transfers between devices with their start and end apart: 18, of which 16 were waited for; matrix products, arithmetic and copies ran while one was open for 2% of the time, Pallas kernels for 13%

profile of v4, /device:TPU:0, one launch (start us, length us, event | category | flops | bytes accessed | tf_op | source)
XLA Modules:
  0.0 55.8 jit_solution(2399414638791214283)
XLA Ops:
  0.0 3.5 %first.1 = (bf16[160,512]{1,0:T(8,128)(2,1)S(1)}, f32[8,80,256]{2,1,0:T(8,128)S(1)}, bf16[8,80,256]{2,1,0:T(8,128)(2,1)S(1)}) custom-call(s32[1]{0:T(128)} %bitcast.me_ref, s32[4]{0:T(128)} %radius_hbm.3, s32[4,15]{1,0:T(4,128)} %phase_hbm.3, f32[4,31]{1,0:T(4,128)} %row_hbm.3, f32[15,4,31]{2,1,0:T(4,128)} %bitcast.7, f32[4,120,1920]{2,1,0:T(8,128)} %vol_hbm.3), custom_call_target="tpu_custom_call" | custom-call | bytes 12000000 | tf_op jit(solution)/shard_map/first/pallas_call | solution.py:379
  3.5 0.5 collective-permute-start
  4.0 1.1 %dynamic-slice_bitcast_fusion.1 = (f32[1,120,240]{2,1,0:T(8,128)S(1)}, f32[1,120,240]{2,1,0:T(8,128)S(1)}) fusion(f32[120,1920]{1,0:T(8,128)} %param.7, s32[]{:T(128)S(6)} %select_n.16, s32[]{:T(128)S(6)} %add.12), kind=kLoop, calls=%fused_computation.3 | loop fusion | bytes 460808 | tf_op jit(solution)/shard_map/stack | solution.py:415
  5.2 0.1 collective-permute-done.recv_ref
  5.3 0.1 core_sum.2
  5.4 3.9 %collective-permute-start.1 = (bf16[2,80,256]{2,1,0:T(8,128)(2,1)S(1)}, bf16[2,80,256]{2,1,0:T(8,128)(2,1)S(1)}, u32[]{:S(2)}, u32[]{:S(2)}) collective-permute-start(bf16[2,80,256]{2,1,0:T(8,128)(2,1)S(1)} %get-tuple-element.32), channel_id=1, source_target_pairs={{0,24},{4,28},{8,16},{12,20},{16,8},{20,12},{24,0},{28,4},{1,25},{... | collective-permute-start | bytes 245768 | tf_op jit(solution)/shard_map/ppermute | solution.py:491
  9.2 0.5 collective-permute-start.2
  9.7 0.1 collective-permute-start.3
  9.9 2.4 %tables.1 = (bf16[4,384,256]{2,1,0:T(8,128)(2,1)S(1)}, bf16[4,384,256]{2,1,0:T(8,128)(2,1)S(1)}, bf16[4,128,256]{2,1,0:T(8,128)(2,1)S(1)}, f32[4,128,1]{2,1,0:T(8,128)S(1)}, f32[4,8,256]{2,1,0:T(8,128)S(1)}) custom-call(s32[1]{0:T(128)} %bitcast.me_ref, s32[1]{0:T(128)} %bitcast.1.strip_ref, s32[4]{0:T(128)} %radius_hbm.3, s32[4,15]{1,0:T(4,128)} %phase_hbm.3, ...), custom_call_target="tpu_custom_call" | custom-call | bytes 6000000 | tf_op jit(solution)/shard_map/tables/pallas_call | solution.py:379
  12.4 0.0 collective-permute-done.1.refs_0_
  12.4 1.4 %collective-permute-done.2.refs_1_ = bf16[2,80,256]{2,1,0:T(8,128)(2,1)S(1)} collective-permute-done((bf16[2,80,256]{2,1,0:T(8,128)(2,1)S(1)}, bf16[2,80,256]{2,1,0:T(8,128)(2,1)S(1)}, u32[]{:S(2)}, u32[]{:S(2)}) %collective-permute-start.2) | collective-permute-done | bytes 81952 | tf_op jit(solution)/shard_map/ppermute | solution.py:491
  13.7 0.4 collective-permute-done.3.refs_2_
  14.2 1.4 %collective-permute-start.4 = (bf16[2,64,256]{2,1,0:T(8,128)(2,1)S(1)}, bf16[2,64,256]{2,1,0:T(8,128)(2,1)S(1)}, u32[]{:S(2)}, u32[]{:S(2)}) collective-permute-start(bf16[2,64,256]{2,1,0:T(8,128)(2,1)S(1)} %get-tuple-element.36), channel_id=1, source_target_pairs={{5,4},{4,5},{2,1},{1,2},{7,6},{6,7},{0,8},{3,11},{13,12},{12,13},{... | collective-permute-start | bytes 196616 | tf_op jit(solution)/shard_map/ppermute | solution.py:499
  15.6 2.8 %blocks.1.after_ref.vol_ref = f32[4,8,120,256]{3,2,1,0:T(8,128)S(1)} custom-call(f32[4,120,1920]{2,1,0:T(8,128)} %vol_hbm.3, f32[2,80,256]{2,1,0:T(8,128)S(1)} %get-tuple-element.35.after_ref.sum_ref), custom_call_target="tpu_custom_call" | custom-call | bytes 9000000 | tf_op jit(solution)/shard_map/blocks/pallas_call | solution.py:379
  18.4 0.1 collective-permute-done.4.edge_ref.first_edge_ref
  18.6 0.1 ratio.2.refs_0_
  18.7 1.6 %collective-permute-start.7 = (bf16[2,80,256]{2,1,0:T(8,128)(2,1)S(1)}, bf16[2,80,256]{2,1,0:T(8,128)(2,1)S(1)}, u32[]{:S(2)}, u32[]{:S(2)}) collective-permute-start(bf16[2,80,256]{2,1,0:T(8,128)(2,1)S(1)} %ratio.2.refs_0_), channel_id=1, source_target_pairs={{0,24},{4,28},{8,16},{12,20},{16,8},{20,12},{24,0},{28,4},{1,25},{... | collective-permute-start | bytes 245768 | tf_op jit(solution)/shard_map/ppermute | solution.py:516
  20.2 1.3 %collective-permute-start.6 = (bf16[2,80,256]{2,1,0:T(8,128)(2,1)S(1)}, bf16[2,80,256]{2,1,0:T(8,128)(2,1)S(1)}, u32[]{:S(2)}, u32[]{:S(2)}) collective-permute-start(bf16[2,80,256]{2,1,0:T(8,128)(2,1)S(1)} %ratio.2.refs_0_), channel_id=1, source_target_pairs={{0,16},{4,20},{8,24},{12,28},{16,0},{20,4},{24,8},{28,12},{1,17},{... | collective-permute-start | bytes 245768 | tf_op jit(solution)/shard_map/ppermute | solution.py:516
  21.5 0.7 %collective-permute-start.5 = (bf16[2,80,256]{2,1,0:T(8,128)(2,1)S(1)}, bf16[2,80,256]{2,1,0:T(8,128)(2,1)S(1)}, u32[]{:S(2)}, u32[]{:S(2)}) collective-permute-start(bf16[2,80,256]{2,1,0:T(8,128)(2,1)S(1)} %ratio.2.refs_0_), channel_id=1, source_target_pairs={{0,8},{4,12},{8,0},{12,4},{16,24},{20,28},{24,16},{28,20},{1,9},{5... | collective-permute-start | bytes 245768 | tf_op jit(solution)/shard_map/ppermute | solution.py:516
  22.2 2.7 %collective-permute-done.7.refs_3_ = bf16[2,80,256]{2,1,0:T(8,128)(2,1)S(1)} collective-permute-done((bf16[2,80,256]{2,1,0:T(8,128)(2,1)S(1)}, bf16[2,80,256]{2,1,0:T(8,128)(2,1)S(1)}, u32[]{:S(2)}, u32[]{:S(2)}) %collective-permute-start.7) | collective-permute-done | bytes 81952 | tf_op jit(solution)/shard_map/ppermute | solution.py:516
  24.9 0.3 collective-permute-done.6.refs_2_
  25.2 0.7 %collective-permute-done.5.refs_1_ = bf16[2,80,256]{2,1,0:T(8,128)(2,1)S(1)} collective-permute-done((bf16[2,80,256]{2,1,0:T(8,128)(2,1)S(1)}, bf16[2,80,256]{2,1,0:T(8,128)(2,1)S(1)}, u32[]{:S(2)}, u32[]{:S(2)}) %collective-permute-start.5) | collective-permute-done | bytes 81952 | tf_op jit(solution)/shard_map/ppermute | solution.py:516
  26.0 0.1 collective-permute-start.8
  26.1 0.9 %ahead.2.own_ref = bf16[4,8,128,256]{3,2,1,0:T(8,128)(2,1)S(1)} custom-call(s32[1]{0:T(128)} %bitcast.me_ref, bf16[4,2,80,256]{3,2,1,0:T(8,128)(2,1)S(1)} %stack.14.same_ref, bf16[4,384,256]{2,1,0:T(8,128)(2,1)S(1)} %get-tuple-element.37.wb_ref), custom_call_target="tpu_custom_call" | custom-call | bytes 3000000 | tf_op jit(solution)/shard_map/ahead/pallas_call | solution.py:379
  27.0 0.7 %collective-permute-done.8.other_ref = bf16[4,2,80,256]{3,2,1,0:T(8,128)(2,1)S(1)} collective-permute-done((bf16[4,2,80,256]{3,2,1,0:T(8,128)(2,1)S(1)}, bf16[4,2,80,256]{3,2,1,0:T(8,128)(2,1)S(1)}, u32[]{:S(2)}, u32[]{:S(2)}) %collective-permute-start.8) | collective-permute-done | bytes 327712 | tf_op jit(solution)/shard_map/ppermute | solution.py:522
  27.7 3.4 %middle.1 = (f32[4,8,120,256]{3,2,1,0:T(8,128)S(1)}, f32[8,80,256]{2,1,0:T(8,128)S(1)}, bf16[8,80,256]{2,1,0:T(8,128)(2,1)S(1)}) custom-call(s32[1]{0:T(128)} %bitcast.me_ref, bf16[4,8,128,256]{3,2,1,0:T(8,128)(2,1)S(1)} %ahead.2.own_ref, bf16[4,2,80,256]{3,2,1,0:T(8,128)(2,1)S(1)} %collective-permute-done.8.other_ref, ...), custom_call_target="tpu_custom_call" | custom-call | bytes 15000000 | tf_op jit(solution)/shard_map/middle/pallas_call | solution.py:379
  31.0 0.2 collective-permute-start.9
  31.2 1.5 %collective-permute-done.9.recv_ref = bf16[8,80,256]{2,1,0:T(8,128)(2,1)S(1)} collective-permute-done((bf16[8,80,256]{2,1,0:T(8,128)(2,1)S(1)}, bf16[8,80,256]{2,1,0:T(8,128)(2,1)S(1)}, u32[]{:S(2)}, u32[]{:S(2)}) %collective-permute-start.9) | collective-permute-done | bytes 327712 | tf_op jit(solution)/shard_map/ppermute | solution.py:467
  32.7 0.1 core_sum.3
  32.8 1.7 %collective-permute-start.10 = (bf16[2,80,256]{2,1,0:T(8,128)(2,1)S(1)}, bf16[2,80,256]{2,1,0:T(8,128)(2,1)S(1)}, u32[]{:S(2)}, u32[]{:S(2)}) collective-permute-start(bf16[2,80,256]{2,1,0:T(8,128)(2,1)S(1)} %get-tuple-element.46), channel_id=1, source_target_pairs={{0,24},{4,28},{8,16},{12,20},{16,8},{20,12},{24,0},{28,4},{1,25},{... | collective-permute-start | bytes 245768 | tf_op jit(solution)/shard_map/ppermute | solution.py:491
  34.5 0.7 %collective-permute-start.11 = (bf16[2,80,256]{2,1,0:T(8,128)(2,1)S(1)}, bf16[2,80,256]{2,1,0:T(8,128)(2,1)S(1)}, u32[]{:S(2)}, u32[]{:S(2)}) collective-permute-start(bf16[2,80,256]{2,1,0:T(8,128)(2,1)S(1)} %get-tuple-element.47), channel_id=1, source_target_pairs={{0,16},{4,20},{8,24},{12,28},{16,0},{20,4},{24,8},{28,12},{1,17},{... | collective-permute-start | bytes 245768 | tf_op jit(solution)/shard_map/ppermute | solution.py:491
  35.2 1.2 %collective-permute-start.12 = (bf16[2,80,256]{2,1,0:T(8,128)(2,1)S(1)}, bf16[2,80,256]{2,1,0:T(8,128)(2,1)S(1)}, u32[]{:S(2)}, u32[]{:S(2)}) collective-permute-start(bf16[2,80,256]{2,1,0:T(8,128)(2,1)S(1)} %get-tuple-element.48), channel_id=1, source_target_pairs={{0,8},{4,12},{8,0},{12,4},{16,24},{20,28},{24,16},{28,20},{1,9},{5... | collective-permute-start | bytes 245768 | tf_op jit(solution)/shard_map/ppermute | solution.py:491
  36.3 2.0 %collective-permute-done.10.refs_0_ = bf16[2,80,256]{2,1,0:T(8,128)(2,1)S(1)} collective-permute-done((bf16[2,80,256]{2,1,0:T(8,128)(2,1)S(1)}, bf16[2,80,256]{2,1,0:T(8,128)(2,1)S(1)}, u32[]{:S(2)}, u32[]{:S(2)}) %collective-permute-start.10) | collective-permute-done | bytes 81952 | tf_op jit(solution)/shard_map/ppermute | solution.py:491
  38.4 1.6 %collective-permute-done.11.refs_1_ = bf16[2,80,256]{2,1,0:T(8,128)(2,1)S(1)} collective-permute-done((bf16[2,80,256]{2,1,0:T(8,128)(2,1)S(1)}, bf16[2,80,256]{2,1,0:T(8,128)(2,1)S(1)}, u32[]{:S(2)}, u32[]{:S(2)}) %collective-permute-start.11) | collective-permute-done | bytes 81952 | tf_op jit(solution)/shard_map/ppermute | solution.py:491
  40.0 0.0 collective-permute-done.12.refs_2_
  40.0 0.9 %collective-permute-start.13 = (bf16[2,32,256]{2,1,0:T(8,128)(2,1)S(1)}, bf16[2,32,256]{2,1,0:T(8,128)(2,1)S(1)}, u32[]{:S(2)}, u32[]{:S(2)}) collective-permute-start(bf16[2,32,256]{2,1,0:T(8,128)(2,1)S(1)} %get-tuple-element.50), channel_id=1, source_target_pairs={{5,4},{4,5},{2,1},{1,2},{7,6},{6,7},{0,8},{3,11},{13,12},{12,13},{... | collective-permute-start | bytes 98312 | tf_op jit(solution)/shard_map/ppermute | solution.py:499
  41.0 3.1 %collective-permute-done.13.edge_ref = bf16[2,32,256]{2,1,0:T(8,128)(2,1)S(1)} collective-permute-done((bf16[2,32,256]{2,1,0:T(8,128)(2,1)S(1)}, bf16[2,32,256]{2,1,0:T(8,128)(2,1)S(1)}, u32[]{:S(2)}, u32[]{:S(2)}) %collective-permute-start.13) | collective-permute-done | bytes 32800 | tf_op jit(solution)/shard_map/ppermute | solution.py:499
  44.0 0.3 ratio.3.refs_0_
  44.3 1.7 %collective-permute-start.16 = (bf16[2,80,256]{2,1,0:T(8,128)(2,1)S(1)}, bf16[2,80,256]{2,1,0:T(8,128)(2,1)S(1)}, u32[]{:S(2)}, u32[]{:S(2)}) collective-permute-start(bf16[2,80,256]{2,1,0:T(8,128)(2,1)S(1)} %ratio.3.refs_0_), channel_id=1, source_target_pairs={{0,24},{4,28},{8,16},{12,20},{16,8},{20,12},{24,0},{28,4},{1,25},{... | collective-permute-start | bytes 245768 | tf_op jit(solution)/shard_map/ppermute | solution.py:516
  46.0 0.7 %collective-permute-start.15 = (bf16[2,80,256]{2,1,0:T(8,128)(2,1)S(1)}, bf16[2,80,256]{2,1,0:T(8,128)(2,1)S(1)}, u32[]{:S(2)}, u32[]{:S(2)}) collective-permute-start(bf16[2,80,256]{2,1,0:T(8,128)(2,1)S(1)} %ratio.3.refs_0_), channel_id=1, source_target_pairs={{0,16},{4,20},{8,24},{12,28},{16,0},{20,4},{24,8},{28,12},{1,17},{... | collective-permute-start | bytes 245768 | tf_op jit(solution)/shard_map/ppermute | solution.py:516
  46.7 1.2 %collective-permute-start.14 = (bf16[2,80,256]{2,1,0:T(8,128)(2,1)S(1)}, bf16[2,80,256]{2,1,0:T(8,128)(2,1)S(1)}, u32[]{:S(2)}, u32[]{:S(2)}) collective-permute-start(bf16[2,80,256]{2,1,0:T(8,128)(2,1)S(1)} %ratio.3.refs_0_), channel_id=1, source_target_pairs={{0,8},{4,12},{8,0},{12,4},{16,24},{20,28},{24,16},{28,20},{1,9},{5... | collective-permute-start | bytes 245768 | tf_op jit(solution)/shard_map/ppermute | solution.py:516
  47.9 2.4 %collective-permute-done.16.refs_3_ = bf16[2,80,256]{2,1,0:T(8,128)(2,1)S(1)} collective-permute-done((bf16[2,80,256]{2,1,0:T(8,128)(2,1)S(1)}, bf16[2,80,256]{2,1,0:T(8,128)(2,1)S(1)}, u32[]{:S(2)}, u32[]{:S(2)}) %collective-permute-start.16) | collective-permute-done | bytes 81952 | tf_op jit(solution)/shard_map/ppermute | solution.py:516
  50.2 0.7 %collective-permute-done.15.refs_2_ = bf16[2,80,256]{2,1,0:T(8,128)(2,1)S(1)} collective-permute-done((bf16[2,80,256]{2,1,0:T(8,128)(2,1)S(1)}, bf16[2,80,256]{2,1,0:T(8,128)(2,1)S(1)}, u32[]{:S(2)}, u32[]{:S(2)}) %collective-permute-start.15) | collective-permute-done | bytes 81952 | tf_op jit(solution)/shard_map/ppermute | solution.py:516
  50.9 0.2 collective-permute-done.14.refs_1_
  51.1 0.1 collective-permute-start.17
  51.2 0.9 %ahead.3.own_ref = bf16[4,8,128,256]{3,2,1,0:T(8,128)(2,1)S(1)} custom-call(s32[1]{0:T(128)} %bitcast.me_ref, bf16[4,2,80,256]{3,2,1,0:T(8,128)(2,1)S(1)} %stack.15.same_ref, bf16[4,384,256]{2,1,0:T(8,128)(2,1)S(1)} %get-tuple-element.37.wb_ref), custom_call_target="tpu_custom_call" | custom-call | bytes 3000000 | tf_op jit(solution)/shard_map/ahead/pallas_call | solution.py:379
  52.1 0.7 %collective-permute-done.17.other_ref = bf16[4,2,80,256]{3,2,1,0:T(8,128)(2,1)S(1)} collective-permute-done((bf16[4,2,80,256]{3,2,1,0:T(8,128)(2,1)S(1)}, bf16[4,2,80,256]{3,2,1,0:T(8,128)(2,1)S(1)}, u32[]{:S(2)}, u32[]{:S(2)}) %collective-permute-start.17) | collective-permute-done | bytes 327712 | tf_op jit(solution)/shard_map/ppermute | solution.py:522
  52.8 2.8 %last.1 = f32[4,120,1920]{2,1,0:T(8,128)} custom-call(s32[1]{0:T(128)} %bitcast.me_ref, bf16[4,8,128,256]{3,2,1,0:T(8,128)(2,1)S(1)} %ahead.3.own_ref, bf16[4,2,80,256]{3,2,1,0:T(8,128)(2,1)S(1)} %collective-permute-done.17.other_ref, bf16[4,384,256]{2,1,0:T(8,128)(2,1)S(1)} %get-tuple-element.37.wb_ref, bf16[4,128,256]{2,1,0:T(8,128)(2,1)S(1)} %get-tuple-element.39.rt_ref, ...), custom_call_target="tpu_custom_call" | custom-call | bytes 15000000 | tf_op jit(solution)/shard_map/last/pallas_call | solution.py:379
  (5 shorter events, 0.2 us)
Async XLA Ops:
  3.5 1.8 %collective-permute-start = (bf16[8,80,256]{2,1,0:T(8,128)(2,1)S(1)}, bf16[8,80,256]{2,1,0:T(8,128)(2,1)S(1)}, u32[]{:S(2)}, u32[]{:S(2)}) collective-permute-start(bf16[8,80,256]{2,1,0:T(8,128)(2,1)S(1)} %get-tuple-element.29), channel_id=1, source_target_pairs={{0,4},{4,0},{8,12},{12,8},{16,20},{20,16},{24,28},{28,24},{1,5},{5... | collective-permute-start | bytes 983048 | tf_op jit(solution)/shard_map/ppermute | solution.py:467
  5.4 7.0 %collective-permute-start.1 = (bf16[2,80,256]{2,1,0:T(8,128)(2,1)S(1)}, bf16[2,80,256]{2,1,0:T(8,128)(2,1)S(1)}, u32[]{:S(2)}, u32[]{:S(2)}) collective-permute-start(bf16[2,80,256]{2,1,0:T(8,128)(2,1)S(1)} %get-tuple-element.32), channel_id=1, source_target_pairs={{0,24},{4,28},{8,16},{12,20},{16,8},{20,12},{24,0},{28,4},{1,25},{... | collective-permute-start | bytes 245768 | tf_op jit(solution)/shard_map/ppermute | solution.py:491
  9.2 4.5 %collective-permute-start.2 = (bf16[2,80,256]{2,1,0:T(8,128)(2,1)S(1)}, bf16[2,80,256]{2,1,0:T(8,128)(2,1)S(1)}, u32[]{:S(2)}, u32[]{:S(2)}) collective-permute-start(bf16[2,80,256]{2,1,0:T(8,128)(2,1)S(1)} %get-tuple-element.33), channel_id=1, source_target_pairs={{0,16},{4,20},{8,24},{12,28},{16,0},{20,4},{24,8},{28,12},{1,17},{... | collective-permute-start | bytes 245768 | tf_op jit(solution)/shard_map/ppermute | solution.py:491
  9.7 4.4 %collective-permute-start.3 = (bf16[2,80,256]{2,1,0:T(8,128)(2,1)S(1)}, bf16[2,80,256]{2,1,0:T(8,128)(2,1)S(1)}, u32[]{:S(2)}, u32[]{:S(2)}) collective-permute-start(bf16[2,80,256]{2,1,0:T(8,128)(2,1)S(1)} %get-tuple-element.34), channel_id=1, source_target_pairs={{0,8},{4,12},{8,0},{12,4},{16,24},{20,28},{24,16},{28,20},{1,9},{5... | collective-permute-start | bytes 245768 | tf_op jit(solution)/shard_map/ppermute | solution.py:491
  14.2 4.3 %collective-permute-start.4 = (bf16[2,64,256]{2,1,0:T(8,128)(2,1)S(1)}, bf16[2,64,256]{2,1,0:T(8,128)(2,1)S(1)}, u32[]{:S(2)}, u32[]{:S(2)}) collective-permute-start(bf16[2,64,256]{2,1,0:T(8,128)(2,1)S(1)} %get-tuple-element.36), channel_id=1, source_target_pairs={{5,4},{4,5},{2,1},{1,2},{7,6},{6,7},{0,8},{3,11},{13,12},{12,13},{... | collective-permute-start | bytes 196616 | tf_op jit(solution)/shard_map/ppermute | solution.py:499
  18.7 6.3 %collective-permute-start.7 = (bf16[2,80,256]{2,1,0:T(8,128)(2,1)S(1)}, bf16[2,80,256]{2,1,0:T(8,128)(2,1)S(1)}, u32[]{:S(2)}, u32[]{:S(2)}) collective-permute-start(bf16[2,80,256]{2,1,0:T(8,128)(2,1)S(1)} %ratio.2.refs_0_), channel_id=1, source_target_pairs={{0,24},{4,28},{8,16},{12,20},{16,8},{20,12},{24,0},{28,4},{1,25},{... | collective-permute-start | bytes 245768 | tf_op jit(solution)/shard_map/ppermute | solution.py:516
  20.2 5.0 %collective-permute-start.6 = (bf16[2,80,256]{2,1,0:T(8,128)(2,1)S(1)}, bf16[2,80,256]{2,1,0:T(8,128)(2,1)S(1)}, u32[]{:S(2)}, u32[]{:S(2)}) collective-permute-start(bf16[2,80,256]{2,1,0:T(8,128)(2,1)S(1)} %ratio.2.refs_0_), channel_id=1, source_target_pairs={{0,16},{4,20},{8,24},{12,28},{16,0},{20,4},{24,8},{28,12},{1,17},{... | collective-permute-start | bytes 245768 | tf_op jit(solution)/shard_map/ppermute | solution.py:516
  21.5 4.4 %collective-permute-start.5 = (bf16[2,80,256]{2,1,0:T(8,128)(2,1)S(1)}, bf16[2,80,256]{2,1,0:T(8,128)(2,1)S(1)}, u32[]{:S(2)}, u32[]{:S(2)}) collective-permute-start(bf16[2,80,256]{2,1,0:T(8,128)(2,1)S(1)} %ratio.2.refs_0_), channel_id=1, source_target_pairs={{0,8},{4,12},{8,0},{12,4},{16,24},{20,28},{24,16},{28,20},{1,9},{5... | collective-permute-start | bytes 245768 | tf_op jit(solution)/shard_map/ppermute | solution.py:516
  26.0 1.7 %collective-permute-start.8 = (bf16[4,2,80,256]{3,2,1,0:T(8,128)(2,1)S(1)}, bf16[4,2,80,256]{3,2,1,0:T(8,128)(2,1)S(1)}, u32[]{:S(2)}, u32[]{:S(2)}) collective-permute-start(bf16[4,2,80,256]{3,2,1,0:T(8,128)(2,1)S(1)} %stack.14.same_ref), channel_id=1, source_target_pairs={{0,4},{4,0},{8,12},{12,8},{16,20},{20,16},{24,28},{28,24},{1,5},{5... | collective-permute-start | bytes 983048 | tf_op jit(solution)/shard_map/ppermute | solution.py:522
  31.0 1.7 %collective-permute-start.9 = (bf16[8,80,256]{2,1,0:T(8,128)(2,1)S(1)}, bf16[8,80,256]{2,1,0:T(8,128)(2,1)S(1)}, u32[]{:S(2)}, u32[]{:S(2)}) collective-permute-start(bf16[8,80,256]{2,1,0:T(8,128)(2,1)S(1)} %get-tuple-element.44), channel_id=1, source_target_pairs={{0,4},{4,0},{8,12},{12,8},{16,20},{20,16},{24,28},{28,24},{1,5},{5... | collective-permute-start | bytes 983048 | tf_op jit(solution)/shard_map/ppermute | solution.py:467
  32.8 5.6 %collective-permute-start.10 = (bf16[2,80,256]{2,1,0:T(8,128)(2,1)S(1)}, bf16[2,80,256]{2,1,0:T(8,128)(2,1)S(1)}, u32[]{:S(2)}, u32[]{:S(2)}) collective-permute-start(bf16[2,80,256]{2,1,0:T(8,128)(2,1)S(1)} %get-tuple-element.46), channel_id=1, source_target_pairs={{0,24},{4,28},{8,16},{12,20},{16,8},{20,12},{24,0},{28,4},{1,25},{... | collective-permute-start | bytes 245768 | tf_op jit(solution)/shard_map/ppermute | solution.py:491
  34.5 5.5 %collective-permute-start.11 = (bf16[2,80,256]{2,1,0:T(8,128)(2,1)S(1)}, bf16[2,80,256]{2,1,0:T(8,128)(2,1)S(1)}, u32[]{:S(2)}, u32[]{:S(2)}) collective-permute-start(bf16[2,80,256]{2,1,0:T(8,128)(2,1)S(1)} %get-tuple-element.47), channel_id=1, source_target_pairs={{0,16},{4,20},{8,24},{12,28},{16,0},{20,4},{24,8},{28,12},{1,17},{... | collective-permute-start | bytes 245768 | tf_op jit(solution)/shard_map/ppermute | solution.py:491
  35.2 4.8 %collective-permute-start.12 = (bf16[2,80,256]{2,1,0:T(8,128)(2,1)S(1)}, bf16[2,80,256]{2,1,0:T(8,128)(2,1)S(1)}, u32[]{:S(2)}, u32[]{:S(2)}) collective-permute-start(bf16[2,80,256]{2,1,0:T(8,128)(2,1)S(1)} %get-tuple-element.48), channel_id=1, source_target_pairs={{0,8},{4,12},{8,0},{12,4},{16,24},{20,28},{24,16},{28,20},{1,9},{5... | collective-permute-start | bytes 245768 | tf_op jit(solution)/shard_map/ppermute | solution.py:491
  40.0 4.0 %collective-permute-start.13 = (bf16[2,32,256]{2,1,0:T(8,128)(2,1)S(1)}, bf16[2,32,256]{2,1,0:T(8,128)(2,1)S(1)}, u32[]{:S(2)}, u32[]{:S(2)}) collective-permute-start(bf16[2,32,256]{2,1,0:T(8,128)(2,1)S(1)} %get-tuple-element.50), channel_id=1, source_target_pairs={{5,4},{4,5},{2,1},{1,2},{7,6},{6,7},{0,8},{3,11},{13,12},{12,13},{... | collective-permute-start | bytes 98312 | tf_op jit(solution)/shard_map/ppermute | solution.py:499
  44.3 5.9 %collective-permute-start.16 = (bf16[2,80,256]{2,1,0:T(8,128)(2,1)S(1)}, bf16[2,80,256]{2,1,0:T(8,128)(2,1)S(1)}, u32[]{:S(2)}, u32[]{:S(2)}) collective-permute-start(bf16[2,80,256]{2,1,0:T(8,128)(2,1)S(1)} %ratio.3.refs_0_), channel_id=1, source_target_pairs={{0,24},{4,28},{8,16},{12,20},{16,8},{20,12},{24,0},{28,4},{1,25},{... | collective-permute-start | bytes 245768 | tf_op jit(solution)/shard_map/ppermute | solution.py:516
  46.0 4.9 %collective-permute-start.15 = (bf16[2,80,256]{2,1,0:T(8,128)(2,1)S(1)}, bf16[2,80,256]{2,1,0:T(8,128)(2,1)S(1)}, u32[]{:S(2)}, u32[]{:S(2)}) collective-permute-start(bf16[2,80,256]{2,1,0:T(8,128)(2,1)S(1)} %ratio.3.refs_0_), channel_id=1, source_target_pairs={{0,16},{4,20},{8,24},{12,28},{16,0},{20,4},{24,8},{28,12},{1,17},{... | collective-permute-start | bytes 245768 | tf_op jit(solution)/shard_map/ppermute | solution.py:516
  46.7 4.4 %collective-permute-start.14 = (bf16[2,80,256]{2,1,0:T(8,128)(2,1)S(1)}, bf16[2,80,256]{2,1,0:T(8,128)(2,1)S(1)}, u32[]{:S(2)}, u32[]{:S(2)}) collective-permute-start(bf16[2,80,256]{2,1,0:T(8,128)(2,1)S(1)} %ratio.3.refs_0_), channel_id=1, source_target_pairs={{0,8},{4,12},{8,0},{12,4},{16,24},{20,28},{24,16},{28,20},{1,9},{5... | collective-permute-start | bytes 245768 | tf_op jit(solution)/shard_map/ppermute | solution.py:516
  51.1 1.7 %collective-permute-start.17 = (bf16[4,2,80,256]{3,2,1,0:T(8,128)(2,1)S(1)}, bf16[4,2,80,256]{3,2,1,0:T(8,128)(2,1)S(1)}, u32[]{:S(2)}, u32[]{:S(2)}) collective-permute-start(bf16[4,2,80,256]{3,2,1,0:T(8,128)(2,1)S(1)} %stack.15.same_ref), channel_id=1, source_target_pairs={{0,4},{4,0},{8,12},{12,8},{16,20},{20,16},{24,28},{28,24},{1,5},{5... | collective-permute-start | bytes 983048 | tf_op jit(solution)/shard_map/ppermute | solution.py:522

commit v5 on v4

--- a/solution.py
+++ b/solution.py
@@ -12,7 +12,6 @@
 SIDE = 16
 LANES = 128
 HALF = LANES // 2
-GROUP = 2
 
 F32 = jnp.float32
 BF16 = jnp.bfloat16
@@ -34,7 +33,8 @@
         self.span = self.w + 2 * SIDE
         self.kp = round_up(self.span, LANES)
         self.kb = self.wl + LANES
-        self.group = 1 if devices % GROUP else GROUP
+        self.tiles = self.wl // LANES
+        assert self.tiles <= 2 and planes % 2 == 0
         self.rp = round_up(rows, LANES)
         self.e = rows + 2 * RMAX
         self.ep = round_up(self.e, 32)
@@ -89,6 +89,22 @@
     return jnp.concatenate(parts, axis=0).astype(BF16)
 
 
+def by_tile(sz, matrix):
+    def zeros(count):
+        return [jnp.zeros((count, sz.wl), F32)] if count else []
+
+    here = min(sz.w, LANES)
+    lead = sz.w - (sz.wl - LANES) - 2 * SIDE
+    first = [matrix[SIDE : SIDE + here]] + zeros(LANES - here)
+    first += [matrix[SIDE + here : SIDE + here + SIDE]] + zeros(lead)
+    first += [matrix[0:SIDE]] + zeros(sz.wl - sz.w)
+    parts = [jnp.concatenate(first, axis=0)[:, 0:LANES]]
+    if sz.tiles == 2:
+        second = [matrix[SIDE : 2 * SIDE + sz.w]] + zeros(sz.wl - sz.w - SIDE)
+        parts.append(jnp.concatenate(second, axis=0)[:, LANES:])
+    return [part.astype(BF16) for part in parts]
+
+
 def row_matrix(sz, z, reach, row_ref):
     taps = row_ref.shape[1]
     lane = iota((1, sz.el), 1)
@@ -101,7 +117,8 @@
 
 
 class Windows:
-    def __init__(self, sz, height, main_ref, side_ref):
+    def __init__(self, sz, height, main_ref, side_ref, group):
+        self.group = group
         self.sz, self.height, self.main, self.side = sz, height, main_ref, side_ref
 
     def clear_sides(self):
@@ -122,14 +139,53 @@
 
     def products(self, matrix):
         sz, height = self.sz, self.height
-        for first in range(0, sz.n, sz.group):
-            count = sz.group * height
+        for first in range(0, sz.n, self.group):
+            count = self.group * height
             main = self.main[first * height : first * height + count, :]
             side = self.side[(first + 1) * height : (first + 1) * height + count, :]
             window = jnp.concatenate([main, side], axis=1)
             out = jnp.dot(window, matrix, preferred_element_type=F32).astype(BF16)
-            for k in range(sz.group):
+            for k in range(self.group):
                 yield first + k, out[k * height : (k + 1) * height, :]
+
+
+class PairWindows:
+    def __init__(self, sz, main_ref, side_ref):
+        self.sz, self.main, self.side = sz, main_ref, side_ref
+
+    def clear(self):
+        sz = self.sz
+        self.main[sz.n * sz.hr :, :] = jnp.zeros((sz.hr, sz.wl), BF16)
+        self.side[...] = jnp.zeros_like(self.side)
+
+    def put(self, b, x):
+        sz = self.sz
+
+        def rows(block):
+            return pl.ds(pl.multiple_of(block * sz.hr, 16), sz.hr)
+
+        self.main[rows(b + 1), 0 : sz.w] = x[:, 0 : sz.w]
+        if sz.tiles == 2:
+            self.main[rows(b), sz.w : sz.w + SIDE] = x[:, 0:SIDE]
+            self.side[rows(b + 1), 0:HALF] = x[:, LANES : LANES + HALF]
+        else:
+            self.side[rows(b), 0:HALF] = x[:, 0:HALF]
+        self.side[rows(b + 2), HALF:] = x[:, sz.wl - HALF :]
+
+    def products(self, pair_ref, group):
+        sz = self.sz
+        for first in range(0, sz.n, group):
+            rows = slice((first + 1) * sz.hr, (first + 1 + group) * sz.hr)
+            for tile in range(sz.tiles):
+                if tile == 0:
+                    window = jnp.concatenate([self.main[rows, 0:LANES], self.side[rows, :]], axis=1)
+                else:
+                    window = self.main[rows, :]
+                out = jnp.dot(window, pair_ref[tile], preferred_element_type=F32).astype(BF16)
+                for k in range(group):
+                    for plane in range(2):
+                        lanes = slice(plane * LANES, (plane + 1) * LANES)
+                        yield first + k, plane, tile, out[k * sz.hr : (k + 1) * sz.hr, lanes]
 
 
 def rows_forward(sz, rc_ref, s_ref, keep_ref, send_ref):
@@ -140,13 +196,15 @@
         keep_ref[b] = out[sz.hr :, :]
 
 
-def backward(sz, z, ratio, matrix, rt, own_ref, g_ref):
-    for b, out in ratio.products(matrix):
-        g_ref[b, 0 : sz.hr, :] = out
-    for b in range(sz.n):
-        rows = jnp.concatenate([own_ref[z, b], g_ref[b]], axis=0)
-        back = jnp.dot(rt, rows, preferred_element_type=F32)
-        yield b, back[0 : sz.rows, :]
+def backward(sz, pair, ratio, wb_ref, rt_ref, own_ref, g_ref):
+    for b, plane, tile, out in ratio.products(wb_ref.at[pair], 2):
+        g_ref[plane, b, 0 : sz.hr, tile * LANES : (tile + 1) * LANES] = out
+    for plane in range(2):
+        z = 2 * pair + plane
+        for b in range(sz.n):
+            rows = jnp.concatenate([own_ref[z, b], g_ref[plane, b]], axis=0)
+            back = jnp.dot(rt_ref[z], rows, preferred_element_type=F32)
+            yield z, b, back[0 : sz.rows, :]
 
 
 def block_norm(sz, b, icn):
@@ -155,11 +213,11 @@
 
 
 def place_ratio(sz, me, stack_ref, main_ref, side_ref):
-    ratio = Windows(sz, sz.hr, main_ref, side_ref)
-    ratio.clear_sides()
+    ratio = PairWindows(sz, main_ref, side_ref)
+    ratio.clear()
     for j in range(sz.half):
         for k in range(2):
-            ratio.put(2 * ((me // 2) ^ j) + k, 0, stack_ref[j, k])
+            ratio.put(2 * ((me // 2) ^ j) + k, stack_ref[j, k])
     return ratio
 
 
@@ -217,16 +275,23 @@
         copy.start()
     for copy in small:
         copy.wait()
-    kind, col = iota((8, sz.kb), 0), iota((8, sz.kb), 1)
-    after, before = (col >= sz.wl) & (col < sz.wl + HALF), col >= sz.wl + HALF
-    ones = jnp.where(((kind == 1) & before) | ((kind == 2) & after), 0.0, 1.0).astype(BF16)
+    kind, col = iota((8, 2 * LANES), 0), iota((8, 2 * LANES), 1)
+    missing = [(kind == 1) & (col >= LANES + HALF)]
+    if sz.tiles == 2:
+        missing.append((kind == 2) & (col >= sz.w))
+    else:
+        missing[0] |= (kind == 2) & (col >= LANES) & (col < LANES + HALF)
+    ones = [jnp.where(part, 0.0, 1.0).astype(BF16) for part in missing]
     for z in range(sz.planes):
         reach = radius_ref[z]
         phase_rows(sz, z, phase_ref, col_ref, t_ref, a_ref)
         wf_ref[z] = by_block(sz, spread_matrix(sz, reach, a_ref))
-        matrix = by_block(sz, gather_matrix(sz, reach, a_ref))
-        wb_ref[z] = matrix
-        norm = jnp.dot(ones, matrix, preferred_element_type=F32)
+        parts = by_tile(sz, gather_matrix(sz, reach, a_ref))
+        for tile, part in enumerate(parts):
+            lanes = slice(z % 2 * LANES, (z % 2 + 1) * LANES)
+            wb_ref[z // 2, tile, :, lanes] = part
+        norm = [jnp.dot(a, b, preferred_element_type=F32) for a, b in zip(ones, parts)]
+        norm = jnp.concatenate(norm, axis=1)
         icn_ref[z] = jnp.where(norm > 0.0, 1.0 / norm, 0.0)
         rt = row_matrix(sz, z, reach, row_ref)
         lane = iota(rt.shape, 1)
@@ -241,9 +306,10 @@
         irn_ref[z] = jnp.where(norm > 0.0, 1.0 / norm, 0.0)
 
 
-def block_kernel(sz, vol_hbm, after_ref, blocks_ref, vol_ref, sems):
+def block_kernel(sz, vol_hbm, after_ref, blocks_ref, vol_ref, sems, planes):
     copies = [
-        pltpu.make_async_copy(vol_hbm.at[z], vol_ref.at[z], sems.at[z]) for z in range(sz.planes)
+        pltpu.make_async_copy(vol_hbm.at[z], vol_ref.at[i], sems.at[i])
+        for i, z in enumerate(planes)
     ]
     for copy in copies:
         copy.start()
@@ -312,37 +378,43 @@
     ratio_ref[...] = jnp.where(inside, m_ref[...] / s_ref[...], 0.0).astype(BF16)
 
 
-def stack_kernel(sz, *refs):
-    for j, ref in enumerate(refs[:-1]):
+def stack_kernel(sz, after_ref, *refs, order):
+    for j, ref in zip(order, refs[:-1]):
         refs[-1][j] = ref[...]
 
 
 def ahead_kernel(sz, me_ref, same_ref, wb_ref, own_ref, ratio_ref, ratio_side_ref):
     ratio = place_ratio(sz, me_ref[0], same_ref, ratio_ref, ratio_side_ref)
     own_ref[:, :, sz.hr :, :] = jnp.zeros((sz.planes, sz.n, sz.hp - sz.hr, sz.wl), BF16)
-    for z in range(sz.planes):
-        for b, out in ratio.products(wb_ref[z]):
-            own_ref[z, b, 0 : sz.hr, :] = out
+    for pair in range(sz.planes // 2):
+        for b, plane, tile, out in ratio.products(wb_ref.at[pair], 2):
+            lanes = slice(tile * LANES, (tile + 1) * LANES)
+            own_ref[2 * pair + plane, b, 0 : sz.hr, lanes] = out
 
 
 def middle_kernel(
-    sz, me_ref, own_ref, other_ref, wf_ref, wb_ref, rt_ref, irn_ref, icn_ref, rc_ref, vol_ref,
+    sz, me_ref, own_ref, other_ref, wf_ref, wb_ref, rt_ref, irn_ref, icn_ref, rc_ref, before_ref, after_ref,
     new_ref, keep_ref, send_ref,
     ratio_ref, ratio_side_ref, g_ref, x_ref, x_side_ref, s_ref,
 ):
     ratio = place_ratio(sz, me_ref[0], other_ref, ratio_ref, ratio_side_ref)
-    g_ref[:, sz.hr :, :] = jnp.zeros((sz.n, sz.hp - sz.hr, sz.wl), BF16)
-    estimate = Windows(sz, sz.rp, x_ref, x_side_ref)
+    g_ref[:, :, sz.hr :, :] = jnp.zeros((2, sz.n, sz.hp - sz.hr, sz.wl), BF16)
+    estimate = Windows(sz, sz.rp, x_ref, x_side_ref, 4)
     estimate.clear_sides()
     lead = jnp.zeros((sz.rp - sz.rows, sz.wl), F32)
-    for z in range(sz.planes):
-        icn, irn = icn_ref[z], irn_ref[z][0 : sz.rows]
-        for b, back in backward(sz, z, ratio, wb_ref[z], rt_ref[z], own_ref, g_ref):
-            new = vol_ref[z, b] * back * (irn * block_norm(sz, b, icn))
+    split = before_ref.shape[0]
+    for pair in range(sz.planes // 2):
+        for z, b, back in backward(sz, pair, ratio, wb_ref, rt_ref, own_ref, g_ref):
+            old = before_ref[z, b] if z < split else after_ref[z - split, b]
+            if b == 0:
+                icn, irn = icn_ref[z], irn_ref[z][0 : sz.rows]
+            norm = irn * block_norm(sz, b, icn)
+            new = old * back * norm
             new_ref[z, b] = new
             estimate.put(b, 0, jnp.concatenate([new, lead]).astype(BF16))
-        for b, out in estimate.products(wf_ref[z]):
-            s_ref[b, z * sz.rp : (z + 1) * sz.rp, :] = out
+            if b == sz.n - 1:
+                for k, out in estimate.products(wf_ref[z]):
+                    s_ref[k, z * sz.rp : (z + 1) * sz.rp, :] = out
     rows_forward(sz, rc_ref, s_ref, keep_ref, send_ref)
 
 
@@ -351,18 +423,30 @@
     out_hbm, ratio_ref, ratio_side_ref, g_ref, out_ref, sems,
 ):
     ratio = place_ratio(sz, me_ref[0], other_ref, ratio_ref, ratio_side_ref)
-    g_ref[:, sz.hr :, :] = jnp.zeros((sz.n, sz.hp - sz.hr, sz.wl), BF16)
+    g_ref[:, :, sz.hr :, :] = jnp.zeros((2, sz.n, sz.hp - sz.hr, sz.wl), BF16)
+    middle = sz.cols // 2 // LANES * LANES
+    lanes = (slice(0, middle), slice(middle, sz.cols))
     copies = [
-        pltpu.make_async_copy(out_ref.at[z], out_hbm.at[z], sems.at[z]) for z in range(sz.planes)
+        [
+            pltpu.make_async_copy(out_ref.at[z, :, k], out_hbm.at[z, :, k], sems.at[z, i])
+            for i, k in enumerate(lanes)
+        ]
+        for z in range(sz.planes)
     ]
-    for z in range(sz.planes):
-        icn, irn = icn_ref[z], irn_ref[z][0 : sz.rows]
-        for b, back in backward(sz, z, ratio, wb_ref[z], rt_ref[z], own_ref, g_ref):
-            new = vol_ref[z, b] * back * (irn * block_norm(sz, b, icn))
+    for pair in range(sz.planes // 2):
+        for z, b, back in backward(sz, pair, ratio, wb_ref, rt_ref, own_ref, g_ref):
+            if b == 0:
+                icn, irn = icn_ref[z], irn_ref[z][0 : sz.rows]
+            norm = irn * block_norm(sz, b, icn)
+            new = vol_ref[z, b] * back * norm
             out_ref[z, :, b * sz.w : (b + 1) * sz.w] = new[:, 0 : sz.w]
-        copies[z].start()
-    for copy in copies:
-        copy.wait()
+            if b == sz.n // 2 - 1:
+                copies[z][0].start()
+            if b == sz.n - 1:
+                copies[z][1].start()
+    for plane in copies:
+        for copy in plane:
+            copy.wait()
 
 
 SMEM = pl.BlockSpec(memory_space=pltpu.SMEM)
@@ -401,6 +485,8 @@
     strip_arg = strip.reshape(1).astype(jnp.int32)
     to_core = [(i, i ^ 1) for i in range(n)]
     to_chip = [[(i, i ^ (2 * j)) for i in range(n)] for j in range(1, sz.half)]
+    order_rs = range(sz.half - 1)[::-1]
+    order_ag = range(sz.half - 1)
     to_strip = []
     for chip in range(sz.half):
         for lower in range(1, strips):
@@ -436,10 +522,10 @@
     ]
     s_scratch = pltpu.VMEM((n, planes * sz.rp, sz.wl), BF16)
     place_scratch = [
-        pltpu.VMEM((n * sz.hr, sz.wl), BF16),
+        pltpu.VMEM(((n + 1) * sz.hr, sz.wl), BF16),
         pltpu.VMEM(((n + 2) * sz.hr, LANES), BF16),
     ]
-    ratio_scratch = place_scratch + [pltpu.VMEM((n, sz.hp, sz.wl), BF16)]
+    ratio_scratch = place_scratch + [pltpu.VMEM((2, n, sz.hp, sz.wl), BF16)]
     x_scratch = [
         pltpu.VMEM((n * sz.rp, sz.wl), BF16),
         pltpu.VMEM(((n + 2) * sz.rp, LANES), BF16),
@@ -461,6 +547,17 @@
         (me_arg, *tap_args, volume),
         24, 4,
     )
+
+    def block_planes(which, after):
+        return call(
+            functools.partial(block_kernel, planes=tuple(which)), sz, "blocks",
+            [HBM, ANY], VMEM, shape((len(which), n, rows, sz.wl), F32),
+            [
+                pltpu.VMEM((len(which), rows, cols), F32),
+                pltpu.SemaphoreType.DMA((len(which),)),
+            ],
+            (volume, after), 12, 2,
+        )
 
     tables, current = None, None
     for iteration in range(ITERS):
@@ -479,7 +576,7 @@
                 [VMEM] * 5,
                 [
                     shape((planes, sz.kb, sz.wl), BF16),
-                    shape((planes, sz.kb, sz.wl), BF16),
+                    shape((planes // 2, sz.tiles, 2 * LANES, 2 * LANES), BF16),
                     shape((planes, sz.rp, sz.el), BF16),
                     shape((planes, sz.rp, 1), F32),
                     shape((planes, 8, sz.wl), F32),
@@ -488,7 +585,7 @@
                 (me_arg, strip_arg, *tap_args, own),
                 8, 2,
             )
-        recvs = [lax.ppermute(part, "depth", pairs) for part, pairs in zip(sends, to_chip)][::-1]
+        recvs = [lax.ppermute(sends[j], "depth", to_chip[j]) for j in order_rs]
         total, edge = call(
             functools.partial(chip_sum_kernel, first=iteration == 0), sz, "chip_sum",
             [SMEM, ANY] + [VMEM] * (2 + len(recvs)),
@@ -499,25 +596,22 @@
         edge = lax.ppermute(edge, ("depth", "strip"), to_strip)
         first_edge = edge if iteration == 0 else first_edge
         if iteration == 0:
-            current = call(
-                block_kernel, sz, "blocks",
-                [HBM, ANY], VMEM, blocked,
-                [vol_scratch, pltpu.SemaphoreType.DMA((planes,))],
-                (volume, total), 12, 3,
-            )
+            before = block_planes(range(planes // 2), total)
         ratio = call(
             ratio_kernel, sz, "ratio",
             [SMEM] * 2 + [ANY] + [VMEM] * 4,
             VMEM,
             flat,
             [pltpu.VMEM(flat32.shape, F32)] * 2,
-            (me_arg, strip_arg, current, total, meas, edge, first_edge), 4,
+            (me_arg, strip_arg, before, total, meas, edge, first_edge), 4,
         )
-        chips = [lax.ppermute(ratio, "depth", pairs) for pairs in to_chip]
+        chips = [lax.ppermute(ratio, "depth", to_chip[j]) for j in order_ag]
+        if iteration == 0:
+            after = block_planes(range(planes // 2, planes), ratio)
         same = call(
-            stack_kernel, sz, "stack",
-            [VMEM] * sz.half, VMEM, shape((sz.half,) + flat.shape, BF16),
-            [], (ratio, *chips), 4,
+            functools.partial(stack_kernel, order=(0, *[j + 1 for j in order_ag])), sz, "stack",
+            [ANY] + [VMEM] * sz.half, VMEM, shape((sz.half,) + flat.shape, BF16),
+            [], (after, ratio, *chips), 4,
         )
         other = lax.ppermute(same, "depth", to_core)
         own = call(
@@ -529,11 +623,11 @@
         if iteration < ITERS - 1:
             current, keep, send = call(
                 middle_kernel, sz, "middle",
-                [SMEM] + [VMEM] * 9,
+                [SMEM] + [VMEM] * 10,
                 [VMEM] * 3,
                 [blocked, *halves],
                 ratio_scratch + x_scratch + [s_scratch],
-                (me_arg, own, other, wf, *tables, rc, current),
+                (me_arg, own, other, wf, *tables, rc, before, after),
                 16, 5,
             )
         else:
@@ -542,7 +636,7 @@
                 [SMEM] + [VMEM] * 7,
                 HBM,
                 shape(volume.shape, F32),
-                ratio_scratch + [vol_scratch, pltpu.SemaphoreType.DMA((planes,))],
+                ratio_scratch + [vol_scratch, pltpu.SemaphoreType.DMA((planes, 2))],
                 (me_arg, own, other, *tables, current),
                 16, 5,
             )

time: 56 us -> 55.6 us (level)
  waiting for transfers between devices: 18.7 us -> 18 us
    ppermute x12, waiting for transfers between devices: 12.5 us -> 10.5 us  [the longest x6 5.5 us: local(): recvs = [lax.ppermute(sends[j], 'depth', to_chip[j]) for j in order_rs]]
    ppermute x2, waiting for transfers between devices: 3.21 us -> 4.07 us  [local(): edge = lax.ppermute(edge, ('depth', 'strip'), to_strip)]
    pallas_call x15 -> x16, Pallas kernels: 17.3 us -> 17.6 us  [call(): pl.pallas_call(functools.partial(kernel, sz), in_specs=in_specs, out_spec...]
  transfers between devices with their start and end apart: 18 -> 18, of which waited for: 16 -> 15; matrix products, arithmetic and copies ran while one was open for 2% -> 2% of each run, Pallas kernels for 13% -> 14%
where the time goes in v5:
time: 55.6 us; the launch traced here: 55.4 us
  starting transfers between devices  18.3 us (33%)
  waiting for transfers between devices  18 us (32%)
  Pallas kernels  17.6 us (32%)
  local copies, waits for them, and re-layouts  1.13 us (2%)
    pallas_call x16, Pallas kernels, call(): pl.pallas_call(functools.partial(kernel, sz), in_specs=in_specs, out_spec...  17.6 us
    ppermute x6, starting transfers between devices, local(): recvs = [lax.ppermute(sends[j], 'depth', to_chip[j]) for j in order_rs]  8.08 us
    ppermute x6, starting transfers between devices, local(): chips = [lax.ppermute(ratio, 'depth', to_chip[j]) for j in order_ag]  7.11 us
    ppermute x6, waiting for transfers between devices, local(): recvs = [lax.ppermute(sends[j], 'depth', to_chip[j]) for j in order_rs]  5.5 us
    ppermute x6, waiting for transfers between devices, local(): chips = [lax.ppermute(ratio, 'depth', to_chip[j]) for j in order_ag]  4.96 us
    ppermute x2, waiting for transfers between devices, local(): edge = lax.ppermute(edge, ('depth', 'strip'), to_strip)  4.07 us
    ppermute x2, starting transfers between devices, local(): edge = lax.ppermute(edge, ('depth', 'strip'), to_strip)  2.25 us
    ppermute x2, waiting for transfers between devices, local(): other = lax.ppermute(same, 'depth', to_core)  1.86 us
  transfers between devices with their start and end apart: 18, of which 15 were waited for; matrix products, arithmetic and copies ran while one was open for 2% of the time, Pallas kernels for 14%

profile of v5, /device:TPU:0, one launch (start us, length us, event | category | flops | bytes accessed | tf_op | source)
XLA Modules:
  0.0 55.4 jit_solution(449337846055849601)
XLA Ops:
  0.0 3.5 %first.1 = (bf16[160,512]{1,0:T(8,128)(2,1)S(1)}, f32[8,80,256]{2,1,0:T(8,128)S(1)}, bf16[8,80,256]{2,1,0:T(8,128)(2,1)S(1)}) custom-call(s32[1]{0:T(128)} %bitcast.me_ref, s32[4]{0:T(128)} %radius_hbm.3, s32[4,15]{1,0:T(4,128)} %phase_hbm.3, f32[4,31]{1,0:T(4,128)} %row_hbm.3, f32[15,4,31]{2,1,0:T(4,128)} %bitcast.7, f32[4,120,1920]{2,1,0:T(8,128)} %vol_hbm.5), custom_call_target="tpu_custom_call" | custom-call | bytes 12000000 | tf_op jit(solution)/shard_map/first/pallas_call | solution.py:463
  3.5 0.5 collective-permute-start
  4.1 1.1 %dynamic-slice_bitcast_fusion.1 = (f32[1,120,240]{2,1,0:T(8,128)S(1)}, f32[1,120,240]{2,1,0:T(8,128)S(1)}) fusion(f32[120,1920]{1,0:T(8,128)} %param.7, s32[]{:T(128)S(6)} %select_n.16, s32[]{:T(128)S(6)} %add.12), kind=kLoop, calls=%fused_computation.3 | loop fusion | bytes 460808 | tf_op jit(solution)/shard_map/stack | solution.py:501
  5.2 0.1 collective-permute-done.recv_ref
  5.3 0.1 core_sum.2
  5.4 3.9 %collective-permute-start.1 = (bf16[2,80,256]{2,1,0:T(8,128)(2,1)S(1)}, bf16[2,80,256]{2,1,0:T(8,128)(2,1)S(1)}, u32[]{:S(2)}, u32[]{:S(2)}) collective-permute-start(bf16[2,80,256]{2,1,0:T(8,128)(2,1)S(1)} %get-tuple-element.32), channel_id=1, source_target_pairs={{0,24},{4,28},{8,16},{12,20},{16,8},{20,12},{24,0},{28,4},{1,25},{... | collective-permute-start | bytes 245768 | tf_op jit(solution)/shard_map/ppermute | solution.py:588
  9.3 0.5 collective-permute-start.2
  9.8 0.1 collective-permute-start.3
  9.9 2.4 %tables.1 = (bf16[4,384,256]{2,1,0:T(8,128)(2,1)S(1)}, bf16[2,2,256,256]{3,2,1,0:T(8,128)(2,1)S(1)}, bf16[4,128,256]{2,1,0:T(8,128)(2,1)S(1)}, f32[4,128,1]{2,1,0:T(8,128)S(1)}, f32[4,8,256]{2,1,0:T(8,128)S(1)}) custom-call(s32[1]{0:T(128)} %bitcast.me_ref, s32[1]{0:T(128)} %bitcast.1.strip_ref, s32[4]{0:T(128)} %radius_hbm.3, s32[4,15]{1,0:T(4,128)} %phase_hbm.3, ...), custom_call_target="tpu_custom_call" | custom-call | bytes 6000000 | tf_op jit(solution)/shard_map/tables/pallas_call | solution.py:463
  12.3 0.0 collective-permute-done.1.refs_0_
  12.3 1.4 %collective-permute-done.2.refs_1_ = bf16[2,80,256]{2,1,0:T(8,128)(2,1)S(1)} collective-permute-done((bf16[2,80,256]{2,1,0:T(8,128)(2,1)S(1)}, bf16[2,80,256]{2,1,0:T(8,128)(2,1)S(1)}, u32[]{:S(2)}, u32[]{:S(2)}) %collective-permute-start.2) | collective-permute-done | bytes 81952 | tf_op jit(solution)/shard_map/ppermute | solution.py:588
  13.8 0.4 collective-permute-done.3.refs_2_
  14.2 1.4 %collective-permute-start.4 = (bf16[2,64,256]{2,1,0:T(8,128)(2,1)S(1)}, bf16[2,64,256]{2,1,0:T(8,128)(2,1)S(1)}, u32[]{:S(2)}, u32[]{:S(2)}) collective-permute-start(bf16[2,64,256]{2,1,0:T(8,128)(2,1)S(1)} %get-tuple-element.36), channel_id=1, source_target_pairs={{5,4},{4,5},{2,1},{1,2},{7,6},{6,7},{0,8},{3,11},{13,12},{12,13},{... | collective-permute-start | bytes 196616 | tf_op jit(solution)/shard_map/ppermute | solution.py:596
  15.6 2.0 %blocks.2.after_ref.before_ref = f32[2,8,120,256]{3,2,1,0:T(8,128)S(1)} custom-call(f32[4,120,1920]{2,1,0:T(8,128)} %vol_hbm.5, f32[2,80,256]{2,1,0:T(8,128)S(1)} %get-tuple-element.35.after_ref.sum_ref), custom_call_target="tpu_custom_call" | custom-call | bytes 6000000 | tf_op jit(solution)/shard_map/blocks/pallas_call | solution.py:463
  17.6 0.9 %collective-permute-done.4.edge_ref.first_edge_ref = bf16[2,64,256]{2,1,0:T(8,128)(2,1)S(1)} collective-permute-done((bf16[2,64,256]{2,1,0:T(8,128)(2,1)S(1)}, bf16[2,64,256]{2,1,0:T(8,128)(2,1)S(1)}, u32[]{:S(2)}, u32[]{:S(2)}) %collective-permute-start.4) | collective-permute-done | bytes 65568 | tf_op jit(solution)/shard_map/ppermute | solution.py:596
  18.6 0.1 ratio.2.after_ref.refs_0_
  18.7 1.5 %collective-permute-start.7 = (bf16[2,80,256]{2,1,0:T(8,128)(2,1)S(1)}, bf16[2,80,256]{2,1,0:T(8,128)(2,1)S(1)}, u32[]{:S(2)}, u32[]{:S(2)}) collective-permute-start(bf16[2,80,256]{2,1,0:T(8,128)(2,1)S(1)} %ratio.2.after_ref.refs_0_), channel_id=1, source_target_pairs={{0,24},{4,28},{8,16},{12,20},{16,8},{20,12},{24,0},{28,4},{1,25},{... | collective-permute-start | bytes 245768 | tf_op jit(solution)/shard_map/ppermute | solution.py:608
  20.2 1.3 %collective-permute-start.6 = (bf16[2,80,256]{2,1,0:T(8,128)(2,1)S(1)}, bf16[2,80,256]{2,1,0:T(8,128)(2,1)S(1)}, u32[]{:S(2)}, u32[]{:S(2)}) collective-permute-start(bf16[2,80,256]{2,1,0:T(8,128)(2,1)S(1)} %ratio.2.after_ref.refs_0_), channel_id=1, source_target_pairs={{0,16},{4,20},{8,24},{12,28},{16,0},{20,4},{24,8},{28,12},{1,17},{... | collective-permute-start | bytes 245768 | tf_op jit(solution)/shard_map/ppermute | solution.py:608
  21.5 0.7 %collective-permute-start.5 = (bf16[2,80,256]{2,1,0:T(8,128)(2,1)S(1)}, bf16[2,80,256]{2,1,0:T(8,128)(2,1)S(1)}, u32[]{:S(2)}, u32[]{:S(2)}) collective-permute-start(bf16[2,80,256]{2,1,0:T(8,128)(2,1)S(1)} %ratio.2.after_ref.refs_0_), channel_id=1, source_target_pairs={{0,8},{4,12},{8,0},{12,4},{16,24},{20,28},{24,16},{28,20},{1,9},{5... | collective-permute-start | bytes 245768 | tf_op jit(solution)/shard_map/ppermute | solution.py:608
  22.2 2.0 %blocks.3.after_ref = f32[2,8,120,256]{3,2,1,0:T(8,128)S(1)} custom-call(f32[4,120,1920]{2,1,0:T(8,128)} %vol_hbm.5, bf16[2,80,256]{2,1,0:T(8,128)(2,1)S(1)} %ratio.2.after_ref.refs_0_), custom_call_target="tpu_custom_call" | custom-call | bytes 6000000 | tf_op jit(solution)/shard_map/blocks/pallas_call | solution.py:463
  24.2 0.0 collective-permute-done.7.refs_3_
  24.2 0.7 %collective-permute-done.6.refs_2_ = bf16[2,80,256]{2,1,0:T(8,128)(2,1)S(1)} collective-permute-done((bf16[2,80,256]{2,1,0:T(8,128)(2,1)S(1)}, bf16[2,80,256]{2,1,0:T(8,128)(2,1)S(1)}, u32[]{:S(2)}, u32[]{:S(2)}) %collective-permute-start.6) | collective-permute-done | bytes 81952 | tf_op jit(solution)/shard_map/ppermute | solution.py:608
  24.9 1.0 %collective-permute-done.5.refs_1_ = bf16[2,80,256]{2,1,0:T(8,128)(2,1)S(1)} collective-permute-done((bf16[2,80,256]{2,1,0:T(8,128)(2,1)S(1)}, bf16[2,80,256]{2,1,0:T(8,128)(2,1)S(1)}, u32[]{:S(2)}, u32[]{:S(2)}) %collective-permute-start.5) | collective-permute-done | bytes 81952 | tf_op jit(solution)/shard_map/ppermute | solution.py:608
  26.0 0.1 collective-permute-start.8
  26.1 0.7 %ahead.2.own_ref = bf16[4,8,128,256]{3,2,1,0:T(8,128)(2,1)S(1)} custom-call(s32[1]{0:T(128)} %bitcast.me_ref, bf16[4,2,80,256]{3,2,1,0:T(8,128)(2,1)S(1)} %stack.14.same_ref, bf16[2,2,256,256]{3,2,1,0:T(8,128)(2,1)S(1)} %get-tuple-element.37.wb_ref), custom_call_target="tpu_custom_call" | custom-call | bytes 3000000 | tf_op jit(solution)/shard_map/ahead/pallas_call | solution.py:463
  26.8 0.9 %collective-permute-done.8.other_ref = bf16[4,2,80,256]{3,2,1,0:T(8,128)(2,1)S(1)} collective-permute-done((bf16[4,2,80,256]{3,2,1,0:T(8,128)(2,1)S(1)}, bf16[4,2,80,256]{3,2,1,0:T(8,128)(2,1)S(1)}, u32[]{:S(2)}, u32[]{:S(2)}) %collective-permute-start.8) | collective-permute-done | bytes 327712 | tf_op jit(solution)/shard_map/ppermute | solution.py:616
  27.7 3.0 %middle.1 = (f32[4,8,120,256]{3,2,1,0:T(8,128)S(1)}, f32[8,80,256]{2,1,0:T(8,128)S(1)}, bf16[8,80,256]{2,1,0:T(8,128)(2,1)S(1)}) custom-call(s32[1]{0:T(128)} %bitcast.me_ref, bf16[4,8,128,256]{3,2,1,0:T(8,128)(2,1)S(1)} %ahead.2.own_ref, bf16[4,2,80,256]{3,2,1,0:T(8,128)(2,1)S(1)} %collective-permute-done.8.other_ref, ...), custom_call_target="tpu_custom_call" | custom-call | bytes 15000000 | tf_op jit(solution)/shard_map/middle/pallas_call | solution.py:463
  30.7 0.2 collective-permute-start.9
  30.9 1.5 %collective-permute-done.9.recv_ref = bf16[8,80,256]{2,1,0:T(8,128)(2,1)S(1)} collective-permute-done((bf16[8,80,256]{2,1,0:T(8,128)(2,1)S(1)}, bf16[8,80,256]{2,1,0:T(8,128)(2,1)S(1)}, u32[]{:S(2)}, u32[]{:S(2)}) %collective-permute-start.9) | collective-permute-done | bytes 327712 | tf_op jit(solution)/shard_map/ppermute | solution.py:564
  32.4 0.1 core_sum.3
  32.5 1.7 %collective-permute-start.10 = (bf16[2,80,256]{2,1,0:T(8,128)(2,1)S(1)}, bf16[2,80,256]{2,1,0:T(8,128)(2,1)S(1)}, u32[]{:S(2)}, u32[]{:S(2)}) collective-permute-start(bf16[2,80,256]{2,1,0:T(8,128)(2,1)S(1)} %get-tuple-element.45), channel_id=1, source_target_pairs={{0,24},{4,28},{8,16},{12,20},{16,8},{20,12},{24,0},{28,4},{1,25},{... | collective-permute-start | bytes 245768 | tf_op jit(solution)/shard_map/ppermute | solution.py:588
  34.2 0.5 collective-permute-start.11
  34.7 1.3 %collective-permute-start.12 = (bf16[2,80,256]{2,1,0:T(8,128)(2,1)S(1)}, bf16[2,80,256]{2,1,0:T(8,128)(2,1)S(1)}, u32[]{:S(2)}, u32[]{:S(2)}) collective-permute-start(bf16[2,80,256]{2,1,0:T(8,128)(2,1)S(1)} %get-tuple-element.47), channel_id=1, source_target_pairs={{0,8},{4,12},{8,0},{12,4},{16,24},{20,28},{24,16},{28,20},{1,9},{5... | collective-permute-start | bytes 245768 | tf_op jit(solution)/shard_map/ppermute | solution.py:588
  36.0 2.0 %collective-permute-done.10.refs_0_ = bf16[2,80,256]{2,1,0:T(8,128)(2,1)S(1)} collective-permute-done((bf16[2,80,256]{2,1,0:T(8,128)(2,1)S(1)}, bf16[2,80,256]{2,1,0:T(8,128)(2,1)S(1)}, u32[]{:S(2)}, u32[]{:S(2)}) %collective-permute-start.10) | collective-permute-done | bytes 81952 | tf_op jit(solution)/shard_map/ppermute | solution.py:588
  38.0 1.6 %collective-permute-done.11.refs_1_ = bf16[2,80,256]{2,1,0:T(8,128)(2,1)S(1)} collective-permute-done((bf16[2,80,256]{2,1,0:T(8,128)(2,1)S(1)}, bf16[2,80,256]{2,1,0:T(8,128)(2,1)S(1)}, u32[]{:S(2)}, u32[]{:S(2)}) %collective-permute-start.11) | collective-permute-done | bytes 81952 | tf_op jit(solution)/shard_map/ppermute | solution.py:588
  39.7 0.0 collective-permute-done.12.refs_2_
  39.7 0.9 %collective-permute-start.13 = (bf16[2,32,256]{2,1,0:T(8,128)(2,1)S(1)}, bf16[2,32,256]{2,1,0:T(8,128)(2,1)S(1)}, u32[]{:S(2)}, u32[]{:S(2)}) collective-permute-start(bf16[2,32,256]{2,1,0:T(8,128)(2,1)S(1)} %get-tuple-element.49), channel_id=1, source_target_pairs={{5,4},{4,5},{2,1},{1,2},{7,6},{6,7},{0,8},{3,11},{13,12},{12,13},{... | collective-permute-start | bytes 98312 | tf_op jit(solution)/shard_map/ppermute | solution.py:596
  40.6 3.1 %collective-permute-done.13.edge_ref = bf16[2,32,256]{2,1,0:T(8,128)(2,1)S(1)} collective-permute-done((bf16[2,32,256]{2,1,0:T(8,128)(2,1)S(1)}, bf16[2,32,256]{2,1,0:T(8,128)(2,1)S(1)}, u32[]{:S(2)}, u32[]{:S(2)}) %collective-permute-start.13) | collective-permute-done | bytes 32800 | tf_op jit(solution)/shard_map/ppermute | solution.py:596
  43.7 0.3 ratio.3.refs_0_
  44.0 1.7 %collective-permute-start.16 = (bf16[2,80,256]{2,1,0:T(8,128)(2,1)S(1)}, bf16[2,80,256]{2,1,0:T(8,128)(2,1)S(1)}, u32[]{:S(2)}, u32[]{:S(2)}) collective-permute-start(bf16[2,80,256]{2,1,0:T(8,128)(2,1)S(1)} %ratio.3.refs_0_), channel_id=1, source_target_pairs={{0,24},{4,28},{8,16},{12,20},{16,8},{20,12},{24,0},{28,4},{1,25},{... | collective-permute-start | bytes 245768 | tf_op jit(solution)/shard_map/ppermute | solution.py:608
  45.7 0.6 %collective-permute-start.15 = (bf16[2,80,256]{2,1,0:T(8,128)(2,1)S(1)}, bf16[2,80,256]{2,1,0:T(8,128)(2,1)S(1)}, u32[]{:S(2)}, u32[]{:S(2)}) collective-permute-start(bf16[2,80,256]{2,1,0:T(8,128)(2,1)S(1)} %ratio.3.refs_0_), channel_id=1, source_target_pairs={{0,16},{4,20},{8,24},{12,28},{16,0},{20,4},{24,8},{28,12},{1,17},{... | collective-permute-start | bytes 245768 | tf_op jit(solution)/shard_map/ppermute | solution.py:608
  46.3 1.2 %collective-permute-start.14 = (bf16[2,80,256]{2,1,0:T(8,128)(2,1)S(1)}, bf16[2,80,256]{2,1,0:T(8,128)(2,1)S(1)}, u32[]{:S(2)}, u32[]{:S(2)}) collective-permute-start(bf16[2,80,256]{2,1,0:T(8,128)(2,1)S(1)} %ratio.3.refs_0_), channel_id=1, source_target_pairs={{0,8},{4,12},{8,0},{12,4},{16,24},{20,28},{24,16},{28,20},{1,9},{5... | collective-permute-start | bytes 245768 | tf_op jit(solution)/shard_map/ppermute | solution.py:608
  47.5 2.4 %collective-permute-done.16.refs_3_ = bf16[2,80,256]{2,1,0:T(8,128)(2,1)S(1)} collective-permute-done((bf16[2,80,256]{2,1,0:T(8,128)(2,1)S(1)}, bf16[2,80,256]{2,1,0:T(8,128)(2,1)S(1)}, u32[]{:S(2)}, u32[]{:S(2)}) %collective-permute-start.16) | collective-permute-done | bytes 81952 | tf_op jit(solution)/shard_map/ppermute | solution.py:608
  49.9 0.7 %collective-permute-done.15.refs_2_ = bf16[2,80,256]{2,1,0:T(8,128)(2,1)S(1)} collective-permute-done((bf16[2,80,256]{2,1,0:T(8,128)(2,1)S(1)}, bf16[2,80,256]{2,1,0:T(8,128)(2,1)S(1)}, u32[]{:S(2)}, u32[]{:S(2)}) %collective-permute-start.15) | collective-permute-done | bytes 81952 | tf_op jit(solution)/shard_map/ppermute | solution.py:608
  50.6 0.1 collective-permute-done.14.refs_1_
  50.8 0.1 collective-permute-start.17
  50.8 0.7 %ahead.3.own_ref = bf16[4,8,128,256]{3,2,1,0:T(8,128)(2,1)S(1)} custom-call(s32[1]{0:T(128)} %bitcast.me_ref, bf16[4,2,80,256]{3,2,1,0:T(8,128)(2,1)S(1)} %stack.15.same_ref, bf16[2,2,256,256]{3,2,1,0:T(8,128)(2,1)S(1)} %get-tuple-element.37.wb_ref), custom_call_target="tpu_custom_call" | custom-call | bytes 3000000 | tf_op jit(solution)/shard_map/ahead/pallas_call | solution.py:463
  51.5 0.9 %collective-permute-done.17.other_ref = bf16[4,2,80,256]{3,2,1,0:T(8,128)(2,1)S(1)} collective-permute-done((bf16[4,2,80,256]{3,2,1,0:T(8,128)(2,1)S(1)}, bf16[4,2,80,256]{3,2,1,0:T(8,128)(2,1)S(1)}, u32[]{:S(2)}, u32[]{:S(2)}) %collective-permute-start.17) | collective-permute-done | bytes 327712 | tf_op jit(solution)/shard_map/ppermute | solution.py:616
  52.5 2.7 %last.1 = f32[4,120,1920]{2,1,0:T(8,128)} custom-call(s32[1]{0:T(128)} %bitcast.me_ref, bf16[4,8,128,256]{3,2,1,0:T(8,128)(2,1)S(1)} %ahead.3.own_ref, bf16[4,2,80,256]{3,2,1,0:T(8,128)(2,1)S(1)} %collective-permute-done.17.other_ref, bf16[2,2,256,256]{3,2,1,0:T(8,128)(2,1)S(1)} %get-tuple-element.37.wb_ref, ...), custom_call_target="tpu_custom_call" | custom-call | bytes 15000000 | tf_op jit(solution)/shard_map/last/pallas_call | solution.py:463
  (5 shorter events, 0.2 us)
Async XLA Ops:
  3.5 1.8 %collective-permute-start = (bf16[8,80,256]{2,1,0:T(8,128)(2,1)S(1)}, bf16[8,80,256]{2,1,0:T(8,128)(2,1)S(1)}, u32[]{:S(2)}, u32[]{:S(2)}) collective-permute-start(bf16[8,80,256]{2,1,0:T(8,128)(2,1)S(1)} %get-tuple-element.29), channel_id=1, source_target_pairs={{0,4},{4,0},{8,12},{12,8},{16,20},{20,16},{24,28},{28,24},{1,5},{5... | collective-permute-start | bytes 983048 | tf_op jit(solution)/shard_map/ppermute | solution.py:564
  5.4 7.0 %collective-permute-start.1 = (bf16[2,80,256]{2,1,0:T(8,128)(2,1)S(1)}, bf16[2,80,256]{2,1,0:T(8,128)(2,1)S(1)}, u32[]{:S(2)}, u32[]{:S(2)}) collective-permute-start(bf16[2,80,256]{2,1,0:T(8,128)(2,1)S(1)} %get-tuple-element.32), channel_id=1, source_target_pairs={{0,24},{4,28},{8,16},{12,20},{16,8},{20,12},{24,0},{28,4},{1,25},{... | collective-permute-start | bytes 245768 | tf_op jit(solution)/shard_map/ppermute | solution.py:588
  9.3 4.5 %collective-permute-start.2 = (bf16[2,80,256]{2,1,0:T(8,128)(2,1)S(1)}, bf16[2,80,256]{2,1,0:T(8,128)(2,1)S(1)}, u32[]{:S(2)}, u32[]{:S(2)}) collective-permute-start(bf16[2,80,256]{2,1,0:T(8,128)(2,1)S(1)} %get-tuple-element.33), channel_id=1, source_target_pairs={{0,16},{4,20},{8,24},{12,28},{16,0},{20,4},{24,8},{28,12},{1,17},{... | collective-permute-start | bytes 245768 | tf_op jit(solution)/shard_map/ppermute | solution.py:588
  9.8 4.4 %collective-permute-start.3 = (bf16[2,80,256]{2,1,0:T(8,128)(2,1)S(1)}, bf16[2,80,256]{2,1,0:T(8,128)(2,1)S(1)}, u32[]{:S(2)}, u32[]{:S(2)}) collective-permute-start(bf16[2,80,256]{2,1,0:T(8,128)(2,1)S(1)} %get-tuple-element.34), channel_id=1, source_target_pairs={{0,8},{4,12},{8,0},{12,4},{16,24},{20,28},{24,16},{28,20},{1,9},{5... | collective-permute-start | bytes 245768 | tf_op jit(solution)/shard_map/ppermute | solution.py:588
  14.2 4.3 %collective-permute-start.4 = (bf16[2,64,256]{2,1,0:T(8,128)(2,1)S(1)}, bf16[2,64,256]{2,1,0:T(8,128)(2,1)S(1)}, u32[]{:S(2)}, u32[]{:S(2)}) collective-permute-start(bf16[2,64,256]{2,1,0:T(8,128)(2,1)S(1)} %get-tuple-element.36), channel_id=1, source_target_pairs={{5,4},{4,5},{2,1},{1,2},{7,6},{6,7},{0,8},{3,11},{13,12},{12,13},{... | collective-permute-start | bytes 196616 | tf_op jit(solution)/shard_map/ppermute | solution.py:596
  18.7 5.5 %collective-permute-start.7 = (bf16[2,80,256]{2,1,0:T(8,128)(2,1)S(1)}, bf16[2,80,256]{2,1,0:T(8,128)(2,1)S(1)}, u32[]{:S(2)}, u32[]{:S(2)}) collective-permute-start(bf16[2,80,256]{2,1,0:T(8,128)(2,1)S(1)} %ratio.2.after_ref.refs_0_), channel_id=1, source_target_pairs={{0,24},{4,28},{8,16},{12,20},{16,8},{20,12},{24,0},{28,4},{1,25},{... | collective-permute-start | bytes 245768 | tf_op jit(solution)/shard_map/ppermute | solution.py:608
  20.2 4.7 %collective-permute-start.6 = (bf16[2,80,256]{2,1,0:T(8,128)(2,1)S(1)}, bf16[2,80,256]{2,1,0:T(8,128)(2,1)S(1)}, u32[]{:S(2)}, u32[]{:S(2)}) collective-permute-start(bf16[2,80,256]{2,1,0:T(8,128)(2,1)S(1)} %ratio.2.after_ref.refs_0_), channel_id=1, source_target_pairs={{0,16},{4,20},{8,24},{12,28},{16,0},{20,4},{24,8},{28,12},{1,17},{... | collective-permute-start | bytes 245768 | tf_op jit(solution)/shard_map/ppermute | solution.py:608
  21.5 4.4 %collective-permute-start.5 = (bf16[2,80,256]{2,1,0:T(8,128)(2,1)S(1)}, bf16[2,80,256]{2,1,0:T(8,128)(2,1)S(1)}, u32[]{:S(2)}, u32[]{:S(2)}) collective-permute-start(bf16[2,80,256]{2,1,0:T(8,128)(2,1)S(1)} %ratio.2.after_ref.refs_0_), channel_id=1, source_target_pairs={{0,8},{4,12},{8,0},{12,4},{16,24},{20,28},{24,16},{28,20},{1,9},{5... | collective-permute-start | bytes 245768 | tf_op jit(solution)/shard_map/ppermute | solution.py:608
  26.0 1.7 %collective-permute-start.8 = (bf16[4,2,80,256]{3,2,1,0:T(8,128)(2,1)S(1)}, bf16[4,2,80,256]{3,2,1,0:T(8,128)(2,1)S(1)}, u32[]{:S(2)}, u32[]{:S(2)}) collective-permute-start(bf16[4,2,80,256]{3,2,1,0:T(8,128)(2,1)S(1)} %stack.14.same_ref), channel_id=1, source_target_pairs={{0,4},{4,0},{8,12},{12,8},{16,20},{20,16},{24,28},{28,24},{1,5},{5... | collective-permute-start | bytes 983048 | tf_op jit(solution)/shard_map/ppermute | solution.py:616
  30.7 1.7 %collective-permute-start.9 = (bf16[8,80,256]{2,1,0:T(8,128)(2,1)S(1)}, bf16[8,80,256]{2,1,0:T(8,128)(2,1)S(1)}, u32[]{:S(2)}, u32[]{:S(2)}) collective-permute-start(bf16[8,80,256]{2,1,0:T(8,128)(2,1)S(1)} %get-tuple-element.43), channel_id=1, source_target_pairs={{0,4},{4,0},{8,12},{12,8},{16,20},{20,16},{24,28},{28,24},{1,5},{5... | collective-permute-start | bytes 983048 | tf_op jit(solution)/shard_map/ppermute | solution.py:564
  32.5 5.6 %collective-permute-start.10 = (bf16[2,80,256]{2,1,0:T(8,128)(2,1)S(1)}, bf16[2,80,256]{2,1,0:T(8,128)(2,1)S(1)}, u32[]{:S(2)}, u32[]{:S(2)}) collective-permute-start(bf16[2,80,256]{2,1,0:T(8,128)(2,1)S(1)} %get-tuple-element.45), channel_id=1, source_target_pairs={{0,24},{4,28},{8,16},{12,20},{16,8},{20,12},{24,0},{28,4},{1,25},{... | collective-permute-start | bytes 245768 | tf_op jit(solution)/shard_map/ppermute | solution.py:588
  34.2 5.5 %collective-permute-start.11 = (bf16[2,80,256]{2,1,0:T(8,128)(2,1)S(1)}, bf16[2,80,256]{2,1,0:T(8,128)(2,1)S(1)}, u32[]{:S(2)}, u32[]{:S(2)}) collective-permute-start(bf16[2,80,256]{2,1,0:T(8,128)(2,1)S(1)} %get-tuple-element.46), channel_id=1, source_target_pairs={{0,16},{4,20},{8,24},{12,28},{16,0},{20,4},{24,8},{28,12},{1,17},{... | collective-permute-start | bytes 245768 | tf_op jit(solution)/shard_map/ppermute | solution.py:588
  34.7 5.0 %collective-permute-start.12 = (bf16[2,80,256]{2,1,0:T(8,128)(2,1)S(1)}, bf16[2,80,256]{2,1,0:T(8,128)(2,1)S(1)}, u32[]{:S(2)}, u32[]{:S(2)}) collective-permute-start(bf16[2,80,256]{2,1,0:T(8,128)(2,1)S(1)} %get-tuple-element.47), channel_id=1, source_target_pairs={{0,8},{4,12},{8,0},{12,4},{16,24},{20,28},{24,16},{28,20},{1,9},{5... | collective-permute-start | bytes 245768 | tf_op jit(solution)/shard_map/ppermute | solution.py:588
  39.7 4.0 %collective-permute-start.13 = (bf16[2,32,256]{2,1,0:T(8,128)(2,1)S(1)}, bf16[2,32,256]{2,1,0:T(8,128)(2,1)S(1)}, u32[]{:S(2)}, u32[]{:S(2)}) collective-permute-start(bf16[2,32,256]{2,1,0:T(8,128)(2,1)S(1)} %get-tuple-element.49), channel_id=1, source_target_pairs={{5,4},{4,5},{2,1},{1,2},{7,6},{6,7},{0,8},{3,11},{13,12},{12,13},{... | collective-permute-start | bytes 98312 | tf_op jit(solution)/shard_map/ppermute | solution.py:596
  44.0 5.9 %collective-permute-start.16 = (bf16[2,80,256]{2,1,0:T(8,128)(2,1)S(1)}, bf16[2,80,256]{2,1,0:T(8,128)(2,1)S(1)}, u32[]{:S(2)}, u32[]{:S(2)}) collective-permute-start(bf16[2,80,256]{2,1,0:T(8,128)(2,1)S(1)} %ratio.3.refs_0_), channel_id=1, source_target_pairs={{0,24},{4,28},{8,16},{12,20},{16,8},{20,12},{24,0},{28,4},{1,25},{... | collective-permute-start | bytes 245768 | tf_op jit(solution)/shard_map/ppermute | solution.py:608
  45.7 4.9 %collective-permute-start.15 = (bf16[2,80,256]{2,1,0:T(8,128)(2,1)S(1)}, bf16[2,80,256]{2,1,0:T(8,128)(2,1)S(1)}, u32[]{:S(2)}, u32[]{:S(2)}) collective-permute-start(bf16[2,80,256]{2,1,0:T(8,128)(2,1)S(1)} %ratio.3.refs_0_), channel_id=1, source_target_pairs={{0,16},{4,20},{8,24},{12,28},{16,0},{20,4},{24,8},{28,12},{1,17},{... | collective-permute-start | bytes 245768 | tf_op jit(solution)/shard_map/ppermute | solution.py:608
  46.3 4.4 %collective-permute-start.14 = (bf16[2,80,256]{2,1,0:T(8,128)(2,1)S(1)}, bf16[2,80,256]{2,1,0:T(8,128)(2,1)S(1)}, u32[]{:S(2)}, u32[]{:S(2)}) collective-permute-start(bf16[2,80,256]{2,1,0:T(8,128)(2,1)S(1)} %ratio.3.refs_0_), channel_id=1, source_target_pairs={{0,8},{4,12},{8,0},{12,4},{16,24},{20,28},{24,16},{28,20},{1,9},{5... | collective-permute-start | bytes 245768 | tf_op jit(solution)/shard_map/ppermute | solution.py:608
  50.8 1.7 %collective-permute-start.17 = (bf16[4,2,80,256]{3,2,1,0:T(8,128)(2,1)S(1)}, bf16[4,2,80,256]{3,2,1,0:T(8,128)(2,1)S(1)}, u32[]{:S(2)}, u32[]{:S(2)}) collective-permute-start(bf16[4,2,80,256]{3,2,1,0:T(8,128)(2,1)S(1)} %stack.15.same_ref), channel_id=1, source_target_pairs={{0,4},{4,0},{8,12},{12,8},{16,20},{20,16},{24,28},{28,24},{1,5},{5... | collective-permute-start | bytes 983048 | tf_op jit(solution)/shard_map/ppermute | solution.py:616

commit v6 on v5

--- a/solution.py
+++ b/solution.py
@@ -34,7 +34,7 @@
         self.kp = round_up(self.span, LANES)
         self.kb = self.wl + LANES
         self.tiles = self.wl // LANES
-        assert self.tiles <= 2 and planes % 2 == 0
+        assert self.tiles <= 2 and planes % 2 == 0 and self.wl > self.w
         self.rp = round_up(rows, LANES)
         self.e = rows + 2 * RMAX
         self.ep = round_up(self.e, 32)
@@ -188,11 +188,24 @@
                         yield first + k, plane, tile, out[k * sz.hr : (k + 1) * sz.hr, lanes]
 
 
+def pack(sz, x):
+    valid = iota(x.shape, x.ndim - 1) < sz.w
+    least = jnp.min(jnp.where(valid, x, jnp.inf), axis=-1, keepdims=True)
+    base = (2.0 * least).astype(BF16).astype(F32)
+    return jnp.where(valid, x - base, base).astype(BF16)
+
+
+def unpack(sz, y):
+    y = y.astype(F32)
+    valid = iota(y.shape, y.ndim - 1) < sz.w
+    return jnp.where(valid, y + y[..., sz.w : sz.w + 1], 0.0)
+
+
 def rows_forward(sz, rc_ref, s_ref, keep_ref, send_ref):
     coef = rc_ref[...]
     for b in range(sz.n):
         out = jnp.dot(coef, s_ref[b], preferred_element_type=F32)
-        send_ref[b] = out[0 : sz.hr, :].astype(BF16)
+        send_ref[b] = pack(sz, out[0 : sz.hr, :])
         keep_ref[b] = out[sz.hr :, :]
 
 
@@ -326,14 +339,15 @@
     mine = me_ref[0] // 2
     for j, ref in enumerate((own_ref, *out_refs)):
         blocks = pl.ds(2 * (mine ^ j), 2)
-        ref[...] = (keep_ref[blocks] + recv_ref[blocks].astype(F32)).astype(ref.dtype)
+        total = keep_ref[blocks] + unpack(sz, recv_ref[blocks])
+        ref[...] = total if j == 0 else pack(sz, total)
 
 
 def chip_sum_kernel(sz, me_ref, after_ref, own_ref, meas_ref, *refs, first):
     recv_refs, (sum_ref, edge_ref) = refs[:-2], refs[-2:]
     total = own_ref[...]
     for ref in recv_refs:
-        total = total + ref[...].astype(F32)
+        total = total + unpack(sz, ref[...])
     sum_ref[...] = total
     edges = []
     for at, row in ((0, 0), (sz.rows - sz.hr, sz.rows - SIDE)):

time: 55.6 us -> 56.5 us (1.016)
  Pallas kernels: 17.6 us -> 18.5 us
    pallas_call x16, Pallas kernels: 17.6 us -> 18.5 us  [call(): pl.pallas_call(functools.partial(kernel, sz), in_specs=in_specs, out_spec...]
where the time goes in v6:
time: 56.5 us; the launch traced here: 56.2 us
  Pallas kernels  18.5 us (33%)
  starting transfers between devices  18.3 us (32%)
  waiting for transfers between devices  18 us (32%)
  local copies, waits for them, and re-layouts  1.13 us (2%)
    pallas_call x16, Pallas kernels, call(): pl.pallas_call(functools.partial(kernel, sz), in_specs=in_specs, out_spec...  18.5 us
    ppermute x6, starting transfers between devices, local(): recvs = [lax.ppermute(sends[j], 'depth', to_chip[j]) for j in order_rs]  8.08 us
    ppermute x6, starting transfers between devices, local(): chips = [lax.ppermute(ratio, 'depth', to_chip[j]) for j in order_ag]  7.11 us
    ppermute x6, waiting for transfers between devices, local(): recvs = [lax.ppermute(sends[j], 'depth', to_chip[j]) for j in order_rs]  5.51 us
    ppermute x6, waiting for transfers between devices, local(): chips = [lax.ppermute(ratio, 'depth', to_chip[j]) for j in order_ag]  4.94 us
    ppermute x2, waiting for transfers between devices, local(): edge = lax.ppermute(edge, ('depth', 'strip'), to_strip)  4.08 us
    ppermute x2, starting transfers between devices, local(): edge = lax.ppermute(edge, ('depth', 'strip'), to_strip)  2.24 us
    ppermute x2, waiting for transfers between devices, local(): other = lax.ppermute(same, 'depth', to_core)  1.87 us
  transfers between devices with their start and end apart: 18, of which 15 were waited for; matrix products, arithmetic and copies ran while one was open for 2% of the time, Pallas kernels for 14%

profile of v6, /device:TPU:0, one launch (start us, length us, event | category | flops | bytes accessed | tf_op | source)
XLA Modules:
  0.0 56.2 jit_solution(6695036143391115721)
XLA Ops:
  0.0 3.6 %first.1 = (bf16[160,512]{1,0:T(8,128)(2,1)S(1)}, f32[8,80,256]{2,1,0:T(8,128)S(1)}, bf16[8,80,256]{2,1,0:T(8,128)(2,1)S(1)}) custom-call(s32[1]{0:T(128)} %bitcast.me_ref, s32[4]{0:T(128)} %radius_hbm.3, s32[4,15]{1,0:T(4,128)} %phase_hbm.3, f32[4,31]{1,0:T(4,128)} %row_hbm.3, f32[15,4,31]{2,1,0:T(4,128)} %bitcast.7, f32[4,120,1920]{2,1,0:T(8,128)} %vol_hbm.5), custom_call_target="tpu_custom_call" | custom-call | bytes 12000000 | tf_op jit(solution)/shard_map/first/pallas_call | solution.py:477
  3.6 0.5 collective-permute-start
  4.1 1.1 %dynamic-slice_bitcast_fusion.1 = (f32[1,120,240]{2,1,0:T(8,128)S(1)}, f32[1,120,240]{2,1,0:T(8,128)S(1)}) fusion(f32[120,1920]{1,0:T(8,128)} %param.7, s32[]{:T(128)S(6)} %select_n.16, s32[]{:T(128)S(6)} %add.12), kind=kLoop, calls=%fused_computation.3 | loop fusion | bytes 460808 | tf_op jit(solution)/shard_map/stack | solution.py:515
  5.3 0.1 collective-permute-done.recv_ref
  5.4 0.3 core_sum.2
  5.7 3.9 %collective-permute-start.1 = (bf16[2,80,256]{2,1,0:T(8,128)(2,1)S(1)}, bf16[2,80,256]{2,1,0:T(8,128)(2,1)S(1)}, u32[]{:S(2)}, u32[]{:S(2)}) collective-permute-start(bf16[2,80,256]{2,1,0:T(8,128)(2,1)S(1)} %get-tuple-element.32), channel_id=1, source_target_pairs={{0,24},{4,28},{8,16},{12,20},{16,8},{20,12},{24,0},{28,4},{1,25},{... | collective-permute-start | bytes 245768 | tf_op jit(solution)/shard_map/ppermute | solution.py:602
  9.6 0.5 collective-permute-start.2
  10.1 0.1 collective-permute-start.3
  10.3 2.4 %tables.1 = (bf16[4,384,256]{2,1,0:T(8,128)(2,1)S(1)}, bf16[2,2,256,256]{3,2,1,0:T(8,128)(2,1)S(1)}, bf16[4,128,256]{2,1,0:T(8,128)(2,1)S(1)}, f32[4,128,1]{2,1,0:T(8,128)S(1)}, f32[4,8,256]{2,1,0:T(8,128)S(1)}) custom-call(s32[1]{0:T(128)} %bitcast.me_ref, s32[1]{0:T(128)} %bitcast.1.strip_ref, s32[4]{0:T(128)} %radius_hbm.3, s32[4,15]{1,0:T(4,128)} %phase_hbm.3, ...), custom_call_target="tpu_custom_call" | custom-call | bytes 6000000 | tf_op jit(solution)/shard_map/tables/pallas_call | solution.py:477
  12.7 0.0 collective-permute-done.1.refs_0_
  12.7 1.4 %collective-permute-done.2.refs_1_ = bf16[2,80,256]{2,1,0:T(8,128)(2,1)S(1)} collective-permute-done((bf16[2,80,256]{2,1,0:T(8,128)(2,1)S(1)}, bf16[2,80,256]{2,1,0:T(8,128)(2,1)S(1)}, u32[]{:S(2)}, u32[]{:S(2)}) %collective-permute-start.2) | collective-permute-done | bytes 81952 | tf_op jit(solution)/shard_map/ppermute | solution.py:602
  14.1 0.4 collective-permute-done.3.refs_2_
  14.5 0.1 chip_sum.2
  14.7 1.4 %collective-permute-start.4 = (bf16[2,64,256]{2,1,0:T(8,128)(2,1)S(1)}, bf16[2,64,256]{2,1,0:T(8,128)(2,1)S(1)}, u32[]{:S(2)}, u32[]{:S(2)}) collective-permute-start(bf16[2,64,256]{2,1,0:T(8,128)(2,1)S(1)} %get-tuple-element.36), channel_id=1, source_target_pairs={{5,4},{4,5},{2,1},{1,2},{7,6},{6,7},{0,8},{3,11},{13,12},{12,13},{... | collective-permute-start | bytes 196616 | tf_op jit(solution)/shard_map/ppermute | solution.py:610
  16.1 2.0 %blocks.2.after_ref.before_ref = f32[2,8,120,256]{3,2,1,0:T(8,128)S(1)} custom-call(f32[4,120,1920]{2,1,0:T(8,128)} %vol_hbm.5, f32[2,80,256]{2,1,0:T(8,128)S(1)} %get-tuple-element.35.after_ref.sum_ref), custom_call_target="tpu_custom_call" | custom-call | bytes 6000000 | tf_op jit(solution)/shard_map/blocks/pallas_call | solution.py:477
  18.1 1.0 %collective-permute-done.4.edge_ref.first_edge_ref = bf16[2,64,256]{2,1,0:T(8,128)(2,1)S(1)} collective-permute-done((bf16[2,64,256]{2,1,0:T(8,128)(2,1)S(1)}, bf16[2,64,256]{2,1,0:T(8,128)(2,1)S(1)}, u32[]{:S(2)}, u32[]{:S(2)}) %collective-permute-start.4) | collective-permute-done | bytes 65568 | tf_op jit(solution)/shard_map/ppermute | solution.py:610
  19.0 0.1 ratio.2.after_ref.refs_0_
  19.1 1.5 %collective-permute-start.7 = (bf16[2,80,256]{2,1,0:T(8,128)(2,1)S(1)}, bf16[2,80,256]{2,1,0:T(8,128)(2,1)S(1)}, u32[]{:S(2)}, u32[]{:S(2)}) collective-permute-start(bf16[2,80,256]{2,1,0:T(8,128)(2,1)S(1)} %ratio.2.after_ref.refs_0_), channel_id=1, source_target_pairs={{0,24},{4,28},{8,16},{12,20},{16,8},{20,12},{24,0},{28,4},{1,25},{... | collective-permute-start | bytes 245768 | tf_op jit(solution)/shard_map/ppermute | solution.py:622
  20.7 1.3 %collective-permute-start.6 = (bf16[2,80,256]{2,1,0:T(8,128)(2,1)S(1)}, bf16[2,80,256]{2,1,0:T(8,128)(2,1)S(1)}, u32[]{:S(2)}, u32[]{:S(2)}) collective-permute-start(bf16[2,80,256]{2,1,0:T(8,128)(2,1)S(1)} %ratio.2.after_ref.refs_0_), channel_id=1, source_target_pairs={{0,16},{4,20},{8,24},{12,28},{16,0},{20,4},{24,8},{28,12},{1,17},{... | collective-permute-start | bytes 245768 | tf_op jit(solution)/shard_map/ppermute | solution.py:622
  22.0 0.7 %collective-permute-start.5 = (bf16[2,80,256]{2,1,0:T(8,128)(2,1)S(1)}, bf16[2,80,256]{2,1,0:T(8,128)(2,1)S(1)}, u32[]{:S(2)}, u32[]{:S(2)}) collective-permute-start(bf16[2,80,256]{2,1,0:T(8,128)(2,1)S(1)} %ratio.2.after_ref.refs_0_), channel_id=1, source_target_pairs={{0,8},{4,12},{8,0},{12,4},{16,24},{20,28},{24,16},{28,20},{1,9},{5... | collective-permute-start | bytes 245768 | tf_op jit(solution)/shard_map/ppermute | solution.py:622
  22.7 2.0 %blocks.3.after_ref = f32[2,8,120,256]{3,2,1,0:T(8,128)S(1)} custom-call(f32[4,120,1920]{2,1,0:T(8,128)} %vol_hbm.5, bf16[2,80,256]{2,1,0:T(8,128)(2,1)S(1)} %ratio.2.after_ref.refs_0_), custom_call_target="tpu_custom_call" | custom-call | bytes 6000000 | tf_op jit(solution)/shard_map/blocks/pallas_call | solution.py:477
  24.6 0.0 collective-permute-done.7.refs_3_
  24.7 0.7 %collective-permute-done.6.refs_2_ = bf16[2,80,256]{2,1,0:T(8,128)(2,1)S(1)} collective-permute-done((bf16[2,80,256]{2,1,0:T(8,128)(2,1)S(1)}, bf16[2,80,256]{2,1,0:T(8,128)(2,1)S(1)}, u32[]{:S(2)}, u32[]{:S(2)}) %collective-permute-start.6) | collective-permute-done | bytes 81952 | tf_op jit(solution)/shard_map/ppermute | solution.py:622
  25.4 1.0 %collective-permute-done.5.refs_1_ = bf16[2,80,256]{2,1,0:T(8,128)(2,1)S(1)} collective-permute-done((bf16[2,80,256]{2,1,0:T(8,128)(2,1)S(1)}, bf16[2,80,256]{2,1,0:T(8,128)(2,1)S(1)}, u32[]{:S(2)}, u32[]{:S(2)}) %collective-permute-start.5) | collective-permute-done | bytes 81952 | tf_op jit(solution)/shard_map/ppermute | solution.py:622
  26.4 0.1 collective-permute-start.8
  26.5 0.7 %ahead.2.own_ref = bf16[4,8,128,256]{3,2,1,0:T(8,128)(2,1)S(1)} custom-call(s32[1]{0:T(128)} %bitcast.me_ref, bf16[4,2,80,256]{3,2,1,0:T(8,128)(2,1)S(1)} %stack.14.same_ref, bf16[2,2,256,256]{3,2,1,0:T(8,128)(2,1)S(1)} %get-tuple-element.37.wb_ref), custom_call_target="tpu_custom_call" | custom-call | bytes 3000000 | tf_op jit(solution)/shard_map/ahead/pallas_call | solution.py:477
  27.2 0.9 %collective-permute-done.8.other_ref = bf16[4,2,80,256]{3,2,1,0:T(8,128)(2,1)S(1)} collective-permute-done((bf16[4,2,80,256]{3,2,1,0:T(8,128)(2,1)S(1)}, bf16[4,2,80,256]{3,2,1,0:T(8,128)(2,1)S(1)}, u32[]{:S(2)}, u32[]{:S(2)}) %collective-permute-start.8) | collective-permute-done | bytes 327712 | tf_op jit(solution)/shard_map/ppermute | solution.py:630
  28.1 3.1 %middle.1 = (f32[4,8,120,256]{3,2,1,0:T(8,128)S(1)}, f32[8,80,256]{2,1,0:T(8,128)S(1)}, bf16[8,80,256]{2,1,0:T(8,128)(2,1)S(1)}) custom-call(s32[1]{0:T(128)} %bitcast.me_ref, bf16[4,8,128,256]{3,2,1,0:T(8,128)(2,1)S(1)} %ahead.2.own_ref, bf16[4,2,80,256]{3,2,1,0:T(8,128)(2,1)S(1)} %collective-permute-done.8.other_ref, ...), custom_call_target="tpu_custom_call" | custom-call | bytes 15000000 | tf_op jit(solution)/shard_map/middle/pallas_call | solution.py:477
  31.2 0.2 collective-permute-start.9
  31.4 1.5 %collective-permute-done.9.recv_ref = bf16[8,80,256]{2,1,0:T(8,128)(2,1)S(1)} collective-permute-done((bf16[8,80,256]{2,1,0:T(8,128)(2,1)S(1)}, bf16[8,80,256]{2,1,0:T(8,128)(2,1)S(1)}, u32[]{:S(2)}, u32[]{:S(2)}) %collective-permute-start.9) | collective-permute-done | bytes 327712 | tf_op jit(solution)/shard_map/ppermute | solution.py:578
  32.9 0.3 core_sum.3
  33.3 1.7 %collective-permute-start.10 = (bf16[2,80,256]{2,1,0:T(8,128)(2,1)S(1)}, bf16[2,80,256]{2,1,0:T(8,128)(2,1)S(1)}, u32[]{:S(2)}, u32[]{:S(2)}) collective-permute-start(bf16[2,80,256]{2,1,0:T(8,128)(2,1)S(1)} %get-tuple-element.45), channel_id=1, source_target_pairs={{0,24},{4,28},{8,16},{12,20},{16,8},{20,12},{24,0},{28,4},{1,25},{... | collective-permute-start | bytes 245768 | tf_op jit(solution)/shard_map/ppermute | solution.py:602
  35.0 0.5 collective-permute-start.11
  35.5 1.3 %collective-permute-start.12 = (bf16[2,80,256]{2,1,0:T(8,128)(2,1)S(1)}, bf16[2,80,256]{2,1,0:T(8,128)(2,1)S(1)}, u32[]{:S(2)}, u32[]{:S(2)}) collective-permute-start(bf16[2,80,256]{2,1,0:T(8,128)(2,1)S(1)} %get-tuple-element.47), channel_id=1, source_target_pairs={{0,8},{4,12},{8,0},{12,4},{16,24},{20,28},{24,16},{28,20},{1,9},{5... | collective-permute-start | bytes 245768 | tf_op jit(solution)/shard_map/ppermute | solution.py:602
  36.8 2.0 %collective-permute-done.10.refs_0_ = bf16[2,80,256]{2,1,0:T(8,128)(2,1)S(1)} collective-permute-done((bf16[2,80,256]{2,1,0:T(8,128)(2,1)S(1)}, bf16[2,80,256]{2,1,0:T(8,128)(2,1)S(1)}, u32[]{:S(2)}, u32[]{:S(2)}) %collective-permute-start.10) | collective-permute-done | bytes 81952 | tf_op jit(solution)/shard_map/ppermute | solution.py:602
  38.8 1.6 %collective-permute-done.11.refs_1_ = bf16[2,80,256]{2,1,0:T(8,128)(2,1)S(1)} collective-permute-done((bf16[2,80,256]{2,1,0:T(8,128)(2,1)S(1)}, bf16[2,80,256]{2,1,0:T(8,128)(2,1)S(1)}, u32[]{:S(2)}, u32[]{:S(2)}) %collective-permute-start.11) | collective-permute-done | bytes 81952 | tf_op jit(solution)/shard_map/ppermute | solution.py:602
  40.5 0.0 collective-permute-done.12.refs_2_
  40.5 0.1 chip_sum.3
  40.6 0.9 %collective-permute-start.13 = (bf16[2,32,256]{2,1,0:T(8,128)(2,1)S(1)}, bf16[2,32,256]{2,1,0:T(8,128)(2,1)S(1)}, u32[]{:S(2)}, u32[]{:S(2)}) collective-permute-start(bf16[2,32,256]{2,1,0:T(8,128)(2,1)S(1)} %get-tuple-element.49), channel_id=1, source_target_pairs={{5,4},{4,5},{2,1},{1,2},{7,6},{6,7},{0,8},{3,11},{13,12},{12,13},{... | collective-permute-start | bytes 98312 | tf_op jit(solution)/shard_map/ppermute | solution.py:610
  41.5 3.1 %collective-permute-done.13.edge_ref = bf16[2,32,256]{2,1,0:T(8,128)(2,1)S(1)} collective-permute-done((bf16[2,32,256]{2,1,0:T(8,128)(2,1)S(1)}, bf16[2,32,256]{2,1,0:T(8,128)(2,1)S(1)}, u32[]{:S(2)}, u32[]{:S(2)}) %collective-permute-start.13) | collective-permute-done | bytes 32800 | tf_op jit(solution)/shard_map/ppermute | solution.py:610
  44.6 0.3 ratio.3.refs_0_
  44.9 1.7 %collective-permute-start.16 = (bf16[2,80,256]{2,1,0:T(8,128)(2,1)S(1)}, bf16[2,80,256]{2,1,0:T(8,128)(2,1)S(1)}, u32[]{:S(2)}, u32[]{:S(2)}) collective-permute-start(bf16[2,80,256]{2,1,0:T(8,128)(2,1)S(1)} %ratio.3.refs_0_), channel_id=1, source_target_pairs={{0,24},{4,28},{8,16},{12,20},{16,8},{20,12},{24,0},{28,4},{1,25},{... | collective-permute-start | bytes 245768 | tf_op jit(solution)/shard_map/ppermute | solution.py:622
  46.6 0.6 %collective-permute-start.15 = (bf16[2,80,256]{2,1,0:T(8,128)(2,1)S(1)}, bf16[2,80,256]{2,1,0:T(8,128)(2,1)S(1)}, u32[]{:S(2)}, u32[]{:S(2)}) collective-permute-start(bf16[2,80,256]{2,1,0:T(8,128)(2,1)S(1)} %ratio.3.refs_0_), channel_id=1, source_target_pairs={{0,16},{4,20},{8,24},{12,28},{16,0},{20,4},{24,8},{28,12},{1,17},{... | collective-permute-start | bytes 245768 | tf_op jit(solution)/shard_map/ppermute | solution.py:622
  47.2 1.2 %collective-permute-start.14 = (bf16[2,80,256]{2,1,0:T(8,128)(2,1)S(1)}, bf16[2,80,256]{2,1,0:T(8,128)(2,1)S(1)}, u32[]{:S(2)}, u32[]{:S(2)}) collective-permute-start(bf16[2,80,256]{2,1,0:T(8,128)(2,1)S(1)} %ratio.3.refs_0_), channel_id=1, source_target_pairs={{0,8},{4,12},{8,0},{12,4},{16,24},{20,28},{24,16},{28,20},{1,9},{5... | collective-permute-start | bytes 245768 | tf_op jit(solution)/shard_map/ppermute | solution.py:622
  48.4 2.4 %collective-permute-done.16.refs_3_ = bf16[2,80,256]{2,1,0:T(8,128)(2,1)S(1)} collective-permute-done((bf16[2,80,256]{2,1,0:T(8,128)(2,1)S(1)}, bf16[2,80,256]{2,1,0:T(8,128)(2,1)S(1)}, u32[]{:S(2)}, u32[]{:S(2)}) %collective-permute-start.16) | collective-permute-done | bytes 81952 | tf_op jit(solution)/shard_map/ppermute | solution.py:622
  50.8 0.7 %collective-permute-done.15.refs_2_ = bf16[2,80,256]{2,1,0:T(8,128)(2,1)S(1)} collective-permute-done((bf16[2,80,256]{2,1,0:T(8,128)(2,1)S(1)}, bf16[2,80,256]{2,1,0:T(8,128)(2,1)S(1)}, u32[]{:S(2)}, u32[]{:S(2)}) %collective-permute-start.15) | collective-permute-done | bytes 81952 | tf_op jit(solution)/shard_map/ppermute | solution.py:622
  51.5 0.1 collective-permute-done.14.refs_1_
  51.7 0.1 collective-permute-start.17
  51.7 0.7 %ahead.3.own_ref = bf16[4,8,128,256]{3,2,1,0:T(8,128)(2,1)S(1)} custom-call(s32[1]{0:T(128)} %bitcast.me_ref, bf16[4,2,80,256]{3,2,1,0:T(8,128)(2,1)S(1)} %stack.15.same_ref, bf16[2,2,256,256]{3,2,1,0:T(8,128)(2,1)S(1)} %get-tuple-element.37.wb_ref), custom_call_target="tpu_custom_call" | custom-call | bytes 3000000 | tf_op jit(solution)/shard_map/ahead/pallas_call | solution.py:477
  52.4 0.9 %collective-permute-done.17.other_ref = bf16[4,2,80,256]{3,2,1,0:T(8,128)(2,1)S(1)} collective-permute-done((bf16[4,2,80,256]{3,2,1,0:T(8,128)(2,1)S(1)}, bf16[4,2,80,256]{3,2,1,0:T(8,128)(2,1)S(1)}, u32[]{:S(2)}, u32[]{:S(2)}) %collective-permute-start.17) | collective-permute-done | bytes 327712 | tf_op jit(solution)/shard_map/ppermute | solution.py:630
  53.4 2.7 %last.1 = f32[4,120,1920]{2,1,0:T(8,128)} custom-call(s32[1]{0:T(128)} %bitcast.me_ref, bf16[4,8,128,256]{3,2,1,0:T(8,128)(2,1)S(1)} %ahead.3.own_ref, bf16[4,2,80,256]{3,2,1,0:T(8,128)(2,1)S(1)} %collective-permute-done.17.other_ref, bf16[2,2,256,256]{3,2,1,0:T(8,128)(2,1)S(1)} %get-tuple-element.37.wb_ref, ...), custom_call_target="tpu_custom_call" | custom-call | bytes 15000000 | tf_op jit(solution)/shard_map/last/pallas_call | solution.py:477
  (3 shorter events, 0.1 us)
Async XLA Ops:
  3.6 1.8 %collective-permute-start = (bf16[8,80,256]{2,1,0:T(8,128)(2,1)S(1)}, bf16[8,80,256]{2,1,0:T(8,128)(2,1)S(1)}, u32[]{:S(2)}, u32[]{:S(2)}) collective-permute-start(bf16[8,80,256]{2,1,0:T(8,128)(2,1)S(1)} %get-tuple-element.29), channel_id=1, source_target_pairs={{0,4},{4,0},{8,12},{12,8},{16,20},{20,16},{24,28},{28,24},{1,5},{5... | collective-permute-start | bytes 983048 | tf_op jit(solution)/shard_map/ppermute | solution.py:578
  5.7 7.0 %collective-permute-start.1 = (bf16[2,80,256]{2,1,0:T(8,128)(2,1)S(1)}, bf16[2,80,256]{2,1,0:T(8,128)(2,1)S(1)}, u32[]{:S(2)}, u32[]{:S(2)}) collective-permute-start(bf16[2,80,256]{2,1,0:T(8,128)(2,1)S(1)} %get-tuple-element.32), channel_id=1, source_target_pairs={{0,24},{4,28},{8,16},{12,20},{16,8},{20,12},{24,0},{28,4},{1,25},{... | collective-permute-start | bytes 245768 | tf_op jit(solution)/shard_map/ppermute | solution.py:602
  9.6 4.5 %collective-permute-start.2 = (bf16[2,80,256]{2,1,0:T(8,128)(2,1)S(1)}, bf16[2,80,256]{2,1,0:T(8,128)(2,1)S(1)}, u32[]{:S(2)}, u32[]{:S(2)}) collective-permute-start(bf16[2,80,256]{2,1,0:T(8,128)(2,1)S(1)} %get-tuple-element.33), channel_id=1, source_target_pairs={{0,16},{4,20},{8,24},{12,28},{16,0},{20,4},{24,8},{28,12},{1,17},{... | collective-permute-start | bytes 245768 | tf_op jit(solution)/shard_map/ppermute | solution.py:602
  10.1 4.4 %collective-permute-start.3 = (bf16[2,80,256]{2,1,0:T(8,128)(2,1)S(1)}, bf16[2,80,256]{2,1,0:T(8,128)(2,1)S(1)}, u32[]{:S(2)}, u32[]{:S(2)}) collective-permute-start(bf16[2,80,256]{2,1,0:T(8,128)(2,1)S(1)} %get-tuple-element.34), channel_id=1, source_target_pairs={{0,8},{4,12},{8,0},{12,4},{16,24},{20,28},{24,16},{28,20},{1,9},{5... | collective-permute-start | bytes 245768 | tf_op jit(solution)/shard_map/ppermute | solution.py:602
  14.7 4.3 %collective-permute-start.4 = (bf16[2,64,256]{2,1,0:T(8,128)(2,1)S(1)}, bf16[2,64,256]{2,1,0:T(8,128)(2,1)S(1)}, u32[]{:S(2)}, u32[]{:S(2)}) collective-permute-start(bf16[2,64,256]{2,1,0:T(8,128)(2,1)S(1)} %get-tuple-element.36), channel_id=1, source_target_pairs={{5,4},{4,5},{2,1},{1,2},{7,6},{6,7},{0,8},{3,11},{13,12},{12,13},{... | collective-permute-start | bytes 196616 | tf_op jit(solution)/shard_map/ppermute | solution.py:610
  19.1 5.5 %collective-permute-start.7 = (bf16[2,80,256]{2,1,0:T(8,128)(2,1)S(1)}, bf16[2,80,256]{2,1,0:T(8,128)(2,1)S(1)}, u32[]{:S(2)}, u32[]{:S(2)}) collective-permute-start(bf16[2,80,256]{2,1,0:T(8,128)(2,1)S(1)} %ratio.2.after_ref.refs_0_), channel_id=1, source_target_pairs={{0,24},{4,28},{8,16},{12,20},{16,8},{20,12},{24,0},{28,4},{1,25},{... | collective-permute-start | bytes 245768 | tf_op jit(solution)/shard_map/ppermute | solution.py:622
  20.7 4.7 %collective-permute-start.6 = (bf16[2,80,256]{2,1,0:T(8,128)(2,1)S(1)}, bf16[2,80,256]{2,1,0:T(8,128)(2,1)S(1)}, u32[]{:S(2)}, u32[]{:S(2)}) collective-permute-start(bf16[2,80,256]{2,1,0:T(8,128)(2,1)S(1)} %ratio.2.after_ref.refs_0_), channel_id=1, source_target_pairs={{0,16},{4,20},{8,24},{12,28},{16,0},{20,4},{24,8},{28,12},{1,17},{... | collective-permute-start | bytes 245768 | tf_op jit(solution)/shard_map/ppermute | solution.py:622
  22.0 4.4 %collective-permute-start.5 = (bf16[2,80,256]{2,1,0:T(8,128)(2,1)S(1)}, bf16[2,80,256]{2,1,0:T(8,128)(2,1)S(1)}, u32[]{:S(2)}, u32[]{:S(2)}) collective-permute-start(bf16[2,80,256]{2,1,0:T(8,128)(2,1)S(1)} %ratio.2.after_ref.refs_0_), channel_id=1, source_target_pairs={{0,8},{4,12},{8,0},{12,4},{16,24},{20,28},{24,16},{28,20},{1,9},{5... | collective-permute-start | bytes 245768 | tf_op jit(solution)/shard_map/ppermute | solution.py:622
  26.4 1.7 %collective-permute-start.8 = (bf16[4,2,80,256]{3,2,1,0:T(8,128)(2,1)S(1)}, bf16[4,2,80,256]{3,2,1,0:T(8,128)(2,1)S(1)}, u32[]{:S(2)}, u32[]{:S(2)}) collective-permute-start(bf16[4,2,80,256]{3,2,1,0:T(8,128)(2,1)S(1)} %stack.14.same_ref), channel_id=1, source_target_pairs={{0,4},{4,0},{8,12},{12,8},{16,20},{20,16},{24,28},{28,24},{1,5},{5... | collective-permute-start | bytes 983048 | tf_op jit(solution)/shard_map/ppermute | solution.py:630
  31.2 1.7 %collective-permute-start.9 = (bf16[8,80,256]{2,1,0:T(8,128)(2,1)S(1)}, bf16[8,80,256]{2,1,0:T(8,128)(2,1)S(1)}, u32[]{:S(2)}, u32[]{:S(2)}) collective-permute-start(bf16[8,80,256]{2,1,0:T(8,128)(2,1)S(1)} %get-tuple-element.43), channel_id=1, source_target_pairs={{0,4},{4,0},{8,12},{12,8},{16,20},{20,16},{24,28},{28,24},{1,5},{5... | collective-permute-start | bytes 983048 | tf_op jit(solution)/shard_map/ppermute | solution.py:578
  33.3 5.6 %collective-permute-start.10 = (bf16[2,80,256]{2,1,0:T(8,128)(2,1)S(1)}, bf16[2,80,256]{2,1,0:T(8,128)(2,1)S(1)}, u32[]{:S(2)}, u32[]{:S(2)}) collective-permute-start(bf16[2,80,256]{2,1,0:T(8,128)(2,1)S(1)} %get-tuple-element.45), channel_id=1, source_target_pairs={{0,24},{4,28},{8,16},{12,20},{16,8},{20,12},{24,0},{28,4},{1,25},{... | collective-permute-start | bytes 245768 | tf_op jit(solution)/shard_map/ppermute | solution.py:602
  35.0 5.5 %collective-permute-start.11 = (bf16[2,80,256]{2,1,0:T(8,128)(2,1)S(1)}, bf16[2,80,256]{2,1,0:T(8,128)(2,1)S(1)}, u32[]{:S(2)}, u32[]{:S(2)}) collective-permute-start(bf16[2,80,256]{2,1,0:T(8,128)(2,1)S(1)} %get-tuple-element.46), channel_id=1, source_target_pairs={{0,16},{4,20},{8,24},{12,28},{16,0},{20,4},{24,8},{28,12},{1,17},{... | collective-permute-start | bytes 245768 | tf_op jit(solution)/shard_map/ppermute | solution.py:602
  35.5 5.0 %collective-permute-start.12 = (bf16[2,80,256]{2,1,0:T(8,128)(2,1)S(1)}, bf16[2,80,256]{2,1,0:T(8,128)(2,1)S(1)}, u32[]{:S(2)}, u32[]{:S(2)}) collective-permute-start(bf16[2,80,256]{2,1,0:T(8,128)(2,1)S(1)} %get-tuple-element.47), channel_id=1, source_target_pairs={{0,8},{4,12},{8,0},{12,4},{16,24},{20,28},{24,16},{28,20},{1,9},{5... | collective-permute-start | bytes 245768 | tf_op jit(solution)/shard_map/ppermute | solution.py:602
  40.6 4.0 %collective-permute-start.13 = (bf16[2,32,256]{2,1,0:T(8,128)(2,1)S(1)}, bf16[2,32,256]{2,1,0:T(8,128)(2,1)S(1)}, u32[]{:S(2)}, u32[]{:S(2)}) collective-permute-start(bf16[2,32,256]{2,1,0:T(8,128)(2,1)S(1)} %get-tuple-element.49), channel_id=1, source_target_pairs={{5,4},{4,5},{2,1},{1,2},{7,6},{6,7},{0,8},{3,11},{13,12},{12,13},{... | collective-permute-start | bytes 98312 | tf_op jit(solution)/shard_map/ppermute | solution.py:610
  44.9 6.0 %collective-permute-start.16 = (bf16[2,80,256]{2,1,0:T(8,128)(2,1)S(1)}, bf16[2,80,256]{2,1,0:T(8,128)(2,1)S(1)}, u32[]{:S(2)}, u32[]{:S(2)}) collective-permute-start(bf16[2,80,256]{2,1,0:T(8,128)(2,1)S(1)} %ratio.3.refs_0_), channel_id=1, source_target_pairs={{0,24},{4,28},{8,16},{12,20},{16,8},{20,12},{24,0},{28,4},{1,25},{... | collective-permute-start | bytes 245768 | tf_op jit(solution)/shard_map/ppermute | solution.py:622
  46.6 4.9 %collective-permute-start.15 = (bf16[2,80,256]{2,1,0:T(8,128)(2,1)S(1)}, bf16[2,80,256]{2,1,0:T(8,128)(2,1)S(1)}, u32[]{:S(2)}, u32[]{:S(2)}) collective-permute-start(bf16[2,80,256]{2,1,0:T(8,128)(2,1)S(1)} %ratio.3.refs_0_), channel_id=1, source_target_pairs={{0,16},{4,20},{8,24},{12,28},{16,0},{20,4},{24,8},{28,12},{1,17},{... | collective-permute-start | bytes 245768 | tf_op jit(solution)/shard_map/ppermute | solution.py:622
  47.2 4.4 %collective-permute-start.14 = (bf16[2,80,256]{2,1,0:T(8,128)(2,1)S(1)}, bf16[2,80,256]{2,1,0:T(8,128)(2,1)S(1)}, u32[]{:S(2)}, u32[]{:S(2)}) collective-permute-start(bf16[2,80,256]{2,1,0:T(8,128)(2,1)S(1)} %ratio.3.refs_0_), channel_id=1, source_target_pairs={{0,8},{4,12},{8,0},{12,4},{16,24},{20,28},{24,16},{28,20},{1,9},{5... | collective-permute-start | bytes 245768 | tf_op jit(solution)/shard_map/ppermute | solution.py:622
  51.7 1.7 %collective-permute-start.17 = (bf16[4,2,80,256]{3,2,1,0:T(8,128)(2,1)S(1)}, bf16[4,2,80,256]{3,2,1,0:T(8,128)(2,1)S(1)}, u32[]{:S(2)}, u32[]{:S(2)}) collective-permute-start(bf16[4,2,80,256]{3,2,1,0:T(8,128)(2,1)S(1)} %stack.15.same_ref), channel_id=1, source_target_pairs={{0,4},{4,0},{8,12},{12,8},{16,20},{20,16},{24,28},{28,24},{1,5},{5... | collective-permute-start | bytes 983048 | tf_op jit(solution)/shard_map/ppermute | solution.py:630

commit v7 on v6

--- a/solution.py
+++ b/solution.py
@@ -205,7 +205,7 @@
     coef = rc_ref[...]
     for b in range(sz.n):
         out = jnp.dot(coef, s_ref[b], preferred_element_type=F32)
-        send_ref[b] = pack(sz, out[0 : sz.hr, :])
+        send_ref[b] = out[0 : sz.hr, :].astype(BF16)
         keep_ref[b] = out[sz.hr :, :]
 
 
@@ -339,7 +339,7 @@
     mine = me_ref[0] // 2
     for j, ref in enumerate((own_ref, *out_refs)):
         blocks = pl.ds(2 * (mine ^ j), 2)
-        total = keep_ref[blocks] + unpack(sz, recv_ref[blocks])
+        total = keep_ref[blocks] + recv_ref[blocks].astype(F32)
         ref[...] = total if j == 0 else pack(sz, total)
 
 

time: 56.5 us -> 56 us (level)
  no operation moved by 1% of the time
where the time goes in v7:
time: 56 us; the launch traced here: 55.8 us
  starting transfers between devices  18.3 us (33%)
  Pallas kernels  18 us (32%)
  waiting for transfers between devices  18 us (32%)
  local copies, waits for them, and re-layouts  1.13 us (2%)
    pallas_call x16, Pallas kernels, call(): pl.pallas_call(functools.partial(kernel, sz), in_specs=in_specs, out_spec...  18 us
    ppermute x6, starting transfers between devices, local(): recvs = [lax.ppermute(sends[j], 'depth', to_chip[j]) for j in order_rs]  8.09 us
    ppermute x6, starting transfers between devices, local(): chips = [lax.ppermute(ratio, 'depth', to_chip[j]) for j in order_ag]  7.11 us
    ppermute x6, waiting for transfers between devices, local(): recvs = [lax.ppermute(sends[j], 'depth', to_chip[j]) for j in order_rs]  5.52 us
    ppermute x6, waiting for transfers between devices, local(): chips = [lax.ppermute(ratio, 'depth', to_chip[j]) for j in order_ag]  4.94 us
    ppermute x2, waiting for transfers between devices, local(): edge = lax.ppermute(edge, ('depth', 'strip'), to_strip)  4.09 us
    ppermute x2, starting transfers between devices, local(): edge = lax.ppermute(edge, ('depth', 'strip'), to_strip)  2.23 us
    ppermute x2, waiting for transfers between devices, local(): other = lax.ppermute(same, 'depth', to_core)  1.85 us
  transfers between devices with their start and end apart: 18, of which 15 were waited for; matrix products, arithmetic and copies ran while one was open for 2% of the time, Pallas kernels for 14%

profile of v7, /device:TPU:0, one launch (start us, length us, event | category | flops | bytes accessed | tf_op | source)
XLA Modules:
  0.0 55.8 jit_solution(4120372782782086078)
XLA Ops:
  0.0 3.5 %first.1 = (bf16[160,512]{1,0:T(8,128)(2,1)S(1)}, f32[8,80,256]{2,1,0:T(8,128)S(1)}, bf16[8,80,256]{2,1,0:T(8,128)(2,1)S(1)}) custom-call(s32[1]{0:T(128)} %bitcast.me_ref, s32[4]{0:T(128)} %radius_hbm.3, s32[4,15]{1,0:T(4,128)} %phase_hbm.3, f32[4,31]{1,0:T(4,128)} %row_hbm.3, f32[15,4,31]{2,1,0:T(4,128)} %bitcast.7, f32[4,120,1920]{2,1,0:T(8,128)} %vol_hbm.5), custom_call_target="tpu_custom_call" | custom-call | bytes 12000000 | tf_op jit(solution)/shard_map/first/pallas_call | solution.py:477
  3.5 0.5 collective-permute-start
  4.0 1.1 %dynamic-slice_bitcast_fusion.1 = (f32[1,120,240]{2,1,0:T(8,128)S(1)}, f32[1,120,240]{2,1,0:T(8,128)S(1)}) fusion(f32[120,1920]{1,0:T(8,128)} %param.7, s32[]{:T(128)S(6)} %select_n.16, s32[]{:T(128)S(6)} %add.12), kind=kLoop, calls=%fused_computation.3 | loop fusion | bytes 460808 | tf_op jit(solution)/shard_map/stack | solution.py:515
  5.2 0.1 collective-permute-done.recv_ref
  5.3 0.2 core_sum.2
  5.5 3.9 %collective-permute-start.1 = (bf16[2,80,256]{2,1,0:T(8,128)(2,1)S(1)}, bf16[2,80,256]{2,1,0:T(8,128)(2,1)S(1)}, u32[]{:S(2)}, u32[]{:S(2)}) collective-permute-start(bf16[2,80,256]{2,1,0:T(8,128)(2,1)S(1)} %get-tuple-element.32), channel_id=1, source_target_pairs={{0,24},{4,28},{8,16},{12,20},{16,8},{20,12},{24,0},{28,4},{1,25},{... | collective-permute-start | bytes 245768 | tf_op jit(solution)/shard_map/ppermute | solution.py:602
  9.4 0.5 collective-permute-start.2
  9.9 0.1 collective-permute-start.3
  10.0 2.4 %tables.1 = (bf16[4,384,256]{2,1,0:T(8,128)(2,1)S(1)}, bf16[2,2,256,256]{3,2,1,0:T(8,128)(2,1)S(1)}, bf16[4,128,256]{2,1,0:T(8,128)(2,1)S(1)}, f32[4,128,1]{2,1,0:T(8,128)S(1)}, f32[4,8,256]{2,1,0:T(8,128)S(1)}) custom-call(s32[1]{0:T(128)} %bitcast.me_ref, s32[1]{0:T(128)} %bitcast.1.strip_ref, s32[4]{0:T(128)} %radius_hbm.3, s32[4,15]{1,0:T(4,128)} %phase_hbm.3, ...), custom_call_target="tpu_custom_call" | custom-call | bytes 6000000 | tf_op jit(solution)/shard_map/tables/pallas_call | solution.py:477
  12.4 0.0 collective-permute-done.1.refs_0_
  12.5 1.4 %collective-permute-done.2.refs_1_ = bf16[2,80,256]{2,1,0:T(8,128)(2,1)S(1)} collective-permute-done((bf16[2,80,256]{2,1,0:T(8,128)(2,1)S(1)}, bf16[2,80,256]{2,1,0:T(8,128)(2,1)S(1)}, u32[]{:S(2)}, u32[]{:S(2)}) %collective-permute-start.2) | collective-permute-done | bytes 81952 | tf_op jit(solution)/shard_map/ppermute | solution.py:602
  13.9 0.4 collective-permute-done.3.refs_2_
  14.3 0.1 chip_sum.2
  14.5 1.4 %collective-permute-start.4 = (bf16[2,64,256]{2,1,0:T(8,128)(2,1)S(1)}, bf16[2,64,256]{2,1,0:T(8,128)(2,1)S(1)}, u32[]{:S(2)}, u32[]{:S(2)}) collective-permute-start(bf16[2,64,256]{2,1,0:T(8,128)(2,1)S(1)} %get-tuple-element.36), channel_id=1, source_target_pairs={{5,4},{4,5},{2,1},{1,2},{7,6},{6,7},{0,8},{3,11},{13,12},{12,13},{... | collective-permute-start | bytes 196616 | tf_op jit(solution)/shard_map/ppermute | solution.py:610
  15.8 2.0 %blocks.2.after_ref.before_ref = f32[2,8,120,256]{3,2,1,0:T(8,128)S(1)} custom-call(f32[4,120,1920]{2,1,0:T(8,128)} %vol_hbm.5, f32[2,80,256]{2,1,0:T(8,128)S(1)} %get-tuple-element.35.after_ref.sum_ref), custom_call_target="tpu_custom_call" | custom-call | bytes 6000000 | tf_op jit(solution)/shard_map/blocks/pallas_call | solution.py:477
  17.8 1.0 %collective-permute-done.4.edge_ref.first_edge_ref = bf16[2,64,256]{2,1,0:T(8,128)(2,1)S(1)} collective-permute-done((bf16[2,64,256]{2,1,0:T(8,128)(2,1)S(1)}, bf16[2,64,256]{2,1,0:T(8,128)(2,1)S(1)}, u32[]{:S(2)}, u32[]{:S(2)}) %collective-permute-start.4) | collective-permute-done | bytes 65568 | tf_op jit(solution)/shard_map/ppermute | solution.py:610
  18.8 0.1 ratio.2.after_ref.refs_0_
  18.9 1.5 %collective-permute-start.7 = (bf16[2,80,256]{2,1,0:T(8,128)(2,1)S(1)}, bf16[2,80,256]{2,1,0:T(8,128)(2,1)S(1)}, u32[]{:S(2)}, u32[]{:S(2)}) collective-permute-start(bf16[2,80,256]{2,1,0:T(8,128)(2,1)S(1)} %ratio.2.after_ref.refs_0_), channel_id=1, source_target_pairs={{0,24},{4,28},{8,16},{12,20},{16,8},{20,12},{24,0},{28,4},{1,25},{... | collective-permute-start | bytes 245768 | tf_op jit(solution)/shard_map/ppermute | solution.py:622
  20.4 1.3 %collective-permute-start.6 = (bf16[2,80,256]{2,1,0:T(8,128)(2,1)S(1)}, bf16[2,80,256]{2,1,0:T(8,128)(2,1)S(1)}, u32[]{:S(2)}, u32[]{:S(2)}) collective-permute-start(bf16[2,80,256]{2,1,0:T(8,128)(2,1)S(1)} %ratio.2.after_ref.refs_0_), channel_id=1, source_target_pairs={{0,16},{4,20},{8,24},{12,28},{16,0},{20,4},{24,8},{28,12},{1,17},{... | collective-permute-start | bytes 245768 | tf_op jit(solution)/shard_map/ppermute | solution.py:622
  21.7 0.7 %collective-permute-start.5 = (bf16[2,80,256]{2,1,0:T(8,128)(2,1)S(1)}, bf16[2,80,256]{2,1,0:T(8,128)(2,1)S(1)}, u32[]{:S(2)}, u32[]{:S(2)}) collective-permute-start(bf16[2,80,256]{2,1,0:T(8,128)(2,1)S(1)} %ratio.2.after_ref.refs_0_), channel_id=1, source_target_pairs={{0,8},{4,12},{8,0},{12,4},{16,24},{20,28},{24,16},{28,20},{1,9},{5... | collective-permute-start | bytes 245768 | tf_op jit(solution)/shard_map/ppermute | solution.py:622
  22.4 2.0 %blocks.3.after_ref = f32[2,8,120,256]{3,2,1,0:T(8,128)S(1)} custom-call(f32[4,120,1920]{2,1,0:T(8,128)} %vol_hbm.5, bf16[2,80,256]{2,1,0:T(8,128)(2,1)S(1)} %ratio.2.after_ref.refs_0_), custom_call_target="tpu_custom_call" | custom-call | bytes 6000000 | tf_op jit(solution)/shard_map/blocks/pallas_call | solution.py:477
  24.4 0.0 collective-permute-done.7.refs_3_
  24.4 0.7 %collective-permute-done.6.refs_2_ = bf16[2,80,256]{2,1,0:T(8,128)(2,1)S(1)} collective-permute-done((bf16[2,80,256]{2,1,0:T(8,128)(2,1)S(1)}, bf16[2,80,256]{2,1,0:T(8,128)(2,1)S(1)}, u32[]{:S(2)}, u32[]{:S(2)}) %collective-permute-start.6) | collective-permute-done | bytes 81952 | tf_op jit(solution)/shard_map/ppermute | solution.py:622
  25.2 1.0 %collective-permute-done.5.refs_1_ = bf16[2,80,256]{2,1,0:T(8,128)(2,1)S(1)} collective-permute-done((bf16[2,80,256]{2,1,0:T(8,128)(2,1)S(1)}, bf16[2,80,256]{2,1,0:T(8,128)(2,1)S(1)}, u32[]{:S(2)}, u32[]{:S(2)}) %collective-permute-start.5) | collective-permute-done | bytes 81952 | tf_op jit(solution)/shard_map/ppermute | solution.py:622
  26.2 0.1 collective-permute-start.8
  26.3 0.7 %ahead.2.own_ref = bf16[4,8,128,256]{3,2,1,0:T(8,128)(2,1)S(1)} custom-call(s32[1]{0:T(128)} %bitcast.me_ref, bf16[4,2,80,256]{3,2,1,0:T(8,128)(2,1)S(1)} %stack.14.same_ref, bf16[2,2,256,256]{3,2,1,0:T(8,128)(2,1)S(1)} %get-tuple-element.37.wb_ref), custom_call_target="tpu_custom_call" | custom-call | bytes 3000000 | tf_op jit(solution)/shard_map/ahead/pallas_call | solution.py:477
  27.0 0.9 %collective-permute-done.8.other_ref = bf16[4,2,80,256]{3,2,1,0:T(8,128)(2,1)S(1)} collective-permute-done((bf16[4,2,80,256]{3,2,1,0:T(8,128)(2,1)S(1)}, bf16[4,2,80,256]{3,2,1,0:T(8,128)(2,1)S(1)}, u32[]{:S(2)}, u32[]{:S(2)}) %collective-permute-start.8) | collective-permute-done | bytes 327712 | tf_op jit(solution)/shard_map/ppermute | solution.py:630
  27.9 3.0 %middle.1 = (f32[4,8,120,256]{3,2,1,0:T(8,128)S(1)}, f32[8,80,256]{2,1,0:T(8,128)S(1)}, bf16[8,80,256]{2,1,0:T(8,128)(2,1)S(1)}) custom-call(s32[1]{0:T(128)} %bitcast.me_ref, bf16[4,8,128,256]{3,2,1,0:T(8,128)(2,1)S(1)} %ahead.2.own_ref, bf16[4,2,80,256]{3,2,1,0:T(8,128)(2,1)S(1)} %collective-permute-done.8.other_ref, ...), custom_call_target="tpu_custom_call" | custom-call | bytes 15000000 | tf_op jit(solution)/shard_map/middle/pallas_call | solution.py:477
  30.9 0.2 collective-permute-start.9
  31.1 1.5 %collective-permute-done.9.recv_ref = bf16[8,80,256]{2,1,0:T(8,128)(2,1)S(1)} collective-permute-done((bf16[8,80,256]{2,1,0:T(8,128)(2,1)S(1)}, bf16[8,80,256]{2,1,0:T(8,128)(2,1)S(1)}, u32[]{:S(2)}, u32[]{:S(2)}) %collective-permute-start.9) | collective-permute-done | bytes 327712 | tf_op jit(solution)/shard_map/ppermute | solution.py:578
  32.6 0.2 core_sum.3
  32.8 1.7 %collective-permute-start.10 = (bf16[2,80,256]{2,1,0:T(8,128)(2,1)S(1)}, bf16[2,80,256]{2,1,0:T(8,128)(2,1)S(1)}, u32[]{:S(2)}, u32[]{:S(2)}) collective-permute-start(bf16[2,80,256]{2,1,0:T(8,128)(2,1)S(1)} %get-tuple-element.45), channel_id=1, source_target_pairs={{0,24},{4,28},{8,16},{12,20},{16,8},{20,12},{24,0},{28,4},{1,25},{... | collective-permute-start | bytes 245768 | tf_op jit(solution)/shard_map/ppermute | solution.py:602
  34.5 0.5 collective-permute-start.11
  35.0 1.3 %collective-permute-start.12 = (bf16[2,80,256]{2,1,0:T(8,128)(2,1)S(1)}, bf16[2,80,256]{2,1,0:T(8,128)(2,1)S(1)}, u32[]{:S(2)}, u32[]{:S(2)}) collective-permute-start(bf16[2,80,256]{2,1,0:T(8,128)(2,1)S(1)} %get-tuple-element.47), channel_id=1, source_target_pairs={{0,8},{4,12},{8,0},{12,4},{16,24},{20,28},{24,16},{28,20},{1,9},{5... | collective-permute-start | bytes 245768 | tf_op jit(solution)/shard_map/ppermute | solution.py:602
  36.3 2.0 %collective-permute-done.10.refs_0_ = bf16[2,80,256]{2,1,0:T(8,128)(2,1)S(1)} collective-permute-done((bf16[2,80,256]{2,1,0:T(8,128)(2,1)S(1)}, bf16[2,80,256]{2,1,0:T(8,128)(2,1)S(1)}, u32[]{:S(2)}, u32[]{:S(2)}) %collective-permute-start.10) | collective-permute-done | bytes 81952 | tf_op jit(solution)/shard_map/ppermute | solution.py:602
  38.3 1.6 %collective-permute-done.11.refs_1_ = bf16[2,80,256]{2,1,0:T(8,128)(2,1)S(1)} collective-permute-done((bf16[2,80,256]{2,1,0:T(8,128)(2,1)S(1)}, bf16[2,80,256]{2,1,0:T(8,128)(2,1)S(1)}, u32[]{:S(2)}, u32[]{:S(2)}) %collective-permute-start.11) | collective-permute-done | bytes 81952 | tf_op jit(solution)/shard_map/ppermute | solution.py:602
  40.0 0.0 collective-permute-done.12.refs_2_
  40.0 0.1 chip_sum.3
  40.1 0.8 %collective-permute-start.13 = (bf16[2,32,256]{2,1,0:T(8,128)(2,1)S(1)}, bf16[2,32,256]{2,1,0:T(8,128)(2,1)S(1)}, u32[]{:S(2)}, u32[]{:S(2)}) collective-permute-start(bf16[2,32,256]{2,1,0:T(8,128)(2,1)S(1)} %get-tuple-element.49), channel_id=1, source_target_pairs={{5,4},{4,5},{2,1},{1,2},{7,6},{6,7},{0,8},{3,11},{13,12},{12,13},{... | collective-permute-start | bytes 98312 | tf_op jit(solution)/shard_map/ppermute | solution.py:610
  41.0 3.1 %collective-permute-done.13.edge_ref = bf16[2,32,256]{2,1,0:T(8,128)(2,1)S(1)} collective-permute-done((bf16[2,32,256]{2,1,0:T(8,128)(2,1)S(1)}, bf16[2,32,256]{2,1,0:T(8,128)(2,1)S(1)}, u32[]{:S(2)}, u32[]{:S(2)}) %collective-permute-start.13) | collective-permute-done | bytes 32800 | tf_op jit(solution)/shard_map/ppermute | solution.py:610
  44.1 0.3 ratio.3.refs_0_
  44.4 1.7 %collective-permute-start.16 = (bf16[2,80,256]{2,1,0:T(8,128)(2,1)S(1)}, bf16[2,80,256]{2,1,0:T(8,128)(2,1)S(1)}, u32[]{:S(2)}, u32[]{:S(2)}) collective-permute-start(bf16[2,80,256]{2,1,0:T(8,128)(2,1)S(1)} %ratio.3.refs_0_), channel_id=1, source_target_pairs={{0,24},{4,28},{8,16},{12,20},{16,8},{20,12},{24,0},{28,4},{1,25},{... | collective-permute-start | bytes 245768 | tf_op jit(solution)/shard_map/ppermute | solution.py:622
  46.1 0.6 %collective-permute-start.15 = (bf16[2,80,256]{2,1,0:T(8,128)(2,1)S(1)}, bf16[2,80,256]{2,1,0:T(8,128)(2,1)S(1)}, u32[]{:S(2)}, u32[]{:S(2)}) collective-permute-start(bf16[2,80,256]{2,1,0:T(8,128)(2,1)S(1)} %ratio.3.refs_0_), channel_id=1, source_target_pairs={{0,16},{4,20},{8,24},{12,28},{16,0},{20,4},{24,8},{28,12},{1,17},{... | collective-permute-start | bytes 245768 | tf_op jit(solution)/shard_map/ppermute | solution.py:622
  46.7 1.2 %collective-permute-start.14 = (bf16[2,80,256]{2,1,0:T(8,128)(2,1)S(1)}, bf16[2,80,256]{2,1,0:T(8,128)(2,1)S(1)}, u32[]{:S(2)}, u32[]{:S(2)}) collective-permute-start(bf16[2,80,256]{2,1,0:T(8,128)(2,1)S(1)} %ratio.3.refs_0_), channel_id=1, source_target_pairs={{0,8},{4,12},{8,0},{12,4},{16,24},{20,28},{24,16},{28,20},{1,9},{5... | collective-permute-start | bytes 245768 | tf_op jit(solution)/shard_map/ppermute | solution.py:622
  47.9 2.4 %collective-permute-done.16.refs_3_ = bf16[2,80,256]{2,1,0:T(8,128)(2,1)S(1)} collective-permute-done((bf16[2,80,256]{2,1,0:T(8,128)(2,1)S(1)}, bf16[2,80,256]{2,1,0:T(8,128)(2,1)S(1)}, u32[]{:S(2)}, u32[]{:S(2)}) %collective-permute-start.16) | collective-permute-done | bytes 81952 | tf_op jit(solution)/shard_map/ppermute | solution.py:622
  50.3 0.7 %collective-permute-done.15.refs_2_ = bf16[2,80,256]{2,1,0:T(8,128)(2,1)S(1)} collective-permute-done((bf16[2,80,256]{2,1,0:T(8,128)(2,1)S(1)}, bf16[2,80,256]{2,1,0:T(8,128)(2,1)S(1)}, u32[]{:S(2)}, u32[]{:S(2)}) %collective-permute-start.15) | collective-permute-done | bytes 81952 | tf_op jit(solution)/shard_map/ppermute | solution.py:622
  51.0 0.1 collective-permute-done.14.refs_1_
  51.2 0.1 collective-permute-start.17
  51.2 0.7 %ahead.3.own_ref = bf16[4,8,128,256]{3,2,1,0:T(8,128)(2,1)S(1)} custom-call(s32[1]{0:T(128)} %bitcast.me_ref, bf16[4,2,80,256]{3,2,1,0:T(8,128)(2,1)S(1)} %stack.15.same_ref, bf16[2,2,256,256]{3,2,1,0:T(8,128)(2,1)S(1)} %get-tuple-element.37.wb_ref), custom_call_target="tpu_custom_call" | custom-call | bytes 3000000 | tf_op jit(solution)/shard_map/ahead/pallas_call | solution.py:477
  51.9 0.9 %collective-permute-done.17.other_ref = bf16[4,2,80,256]{3,2,1,0:T(8,128)(2,1)S(1)} collective-permute-done((bf16[4,2,80,256]{3,2,1,0:T(8,128)(2,1)S(1)}, bf16[4,2,80,256]{3,2,1,0:T(8,128)(2,1)S(1)}, u32[]{:S(2)}, u32[]{:S(2)}) %collective-permute-start.17) | collective-permute-done | bytes 327712 | tf_op jit(solution)/shard_map/ppermute | solution.py:630
  52.9 2.7 %last.1 = f32[4,120,1920]{2,1,0:T(8,128)} custom-call(s32[1]{0:T(128)} %bitcast.me_ref, bf16[4,8,128,256]{3,2,1,0:T(8,128)(2,1)S(1)} %ahead.3.own_ref, bf16[4,2,80,256]{3,2,1,0:T(8,128)(2,1)S(1)} %collective-permute-done.17.other_ref, bf16[2,2,256,256]{3,2,1,0:T(8,128)(2,1)S(1)} %get-tuple-element.37.wb_ref, ...), custom_call_target="tpu_custom_call" | custom-call | bytes 15000000 | tf_op jit(solution)/shard_map/last/pallas_call | solution.py:477
  (3 shorter events, 0.1 us)
Async XLA Ops:
  3.5 1.8 %collective-permute-start = (bf16[8,80,256]{2,1,0:T(8,128)(2,1)S(1)}, bf16[8,80,256]{2,1,0:T(8,128)(2,1)S(1)}, u32[]{:S(2)}, u32[]{:S(2)}) collective-permute-start(bf16[8,80,256]{2,1,0:T(8,128)(2,1)S(1)} %get-tuple-element.29), channel_id=1, source_target_pairs={{0,4},{4,0},{8,12},{12,8},{16,20},{20,16},{24,28},{28,24},{1,5},{5... | collective-permute-start | bytes 983048 | tf_op jit(solution)/shard_map/ppermute | solution.py:578
  5.5 7.0 %collective-permute-start.1 = (bf16[2,80,256]{2,1,0:T(8,128)(2,1)S(1)}, bf16[2,80,256]{2,1,0:T(8,128)(2,1)S(1)}, u32[]{:S(2)}, u32[]{:S(2)}) collective-permute-start(bf16[2,80,256]{2,1,0:T(8,128)(2,1)S(1)} %get-tuple-element.32), channel_id=1, source_target_pairs={{0,24},{4,28},{8,16},{12,20},{16,8},{20,12},{24,0},{28,4},{1,25},{... | collective-permute-start | bytes 245768 | tf_op jit(solution)/shard_map/ppermute | solution.py:602
  9.4 4.5 %collective-permute-start.2 = (bf16[2,80,256]{2,1,0:T(8,128)(2,1)S(1)}, bf16[2,80,256]{2,1,0:T(8,128)(2,1)S(1)}, u32[]{:S(2)}, u32[]{:S(2)}) collective-permute-start(bf16[2,80,256]{2,1,0:T(8,128)(2,1)S(1)} %get-tuple-element.33), channel_id=1, source_target_pairs={{0,16},{4,20},{8,24},{12,28},{16,0},{20,4},{24,8},{28,12},{1,17},{... | collective-permute-start | bytes 245768 | tf_op jit(solution)/shard_map/ppermute | solution.py:602
  9.9 4.4 %collective-permute-start.3 = (bf16[2,80,256]{2,1,0:T(8,128)(2,1)S(1)}, bf16[2,80,256]{2,1,0:T(8,128)(2,1)S(1)}, u32[]{:S(2)}, u32[]{:S(2)}) collective-permute-start(bf16[2,80,256]{2,1,0:T(8,128)(2,1)S(1)} %get-tuple-element.34), channel_id=1, source_target_pairs={{0,8},{4,12},{8,0},{12,4},{16,24},{20,28},{24,16},{28,20},{1,9},{5... | collective-permute-start | bytes 245768 | tf_op jit(solution)/shard_map/ppermute | solution.py:602
  14.5 4.3 %collective-permute-start.4 = (bf16[2,64,256]{2,1,0:T(8,128)(2,1)S(1)}, bf16[2,64,256]{2,1,0:T(8,128)(2,1)S(1)}, u32[]{:S(2)}, u32[]{:S(2)}) collective-permute-start(bf16[2,64,256]{2,1,0:T(8,128)(2,1)S(1)} %get-tuple-element.36), channel_id=1, source_target_pairs={{5,4},{4,5},{2,1},{1,2},{7,6},{6,7},{0,8},{3,11},{13,12},{12,13},{... | collective-permute-start | bytes 196616 | tf_op jit(solution)/shard_map/ppermute | solution.py:610
  18.9 5.5 %collective-permute-start.7 = (bf16[2,80,256]{2,1,0:T(8,128)(2,1)S(1)}, bf16[2,80,256]{2,1,0:T(8,128)(2,1)S(1)}, u32[]{:S(2)}, u32[]{:S(2)}) collective-permute-start(bf16[2,80,256]{2,1,0:T(8,128)(2,1)S(1)} %ratio.2.after_ref.refs_0_), channel_id=1, source_target_pairs={{0,24},{4,28},{8,16},{12,20},{16,8},{20,12},{24,0},{28,4},{1,25},{... | collective-permute-start | bytes 245768 | tf_op jit(solution)/shard_map/ppermute | solution.py:622
  20.4 4.7 %collective-permute-start.6 = (bf16[2,80,256]{2,1,0:T(8,128)(2,1)S(1)}, bf16[2,80,256]{2,1,0:T(8,128)(2,1)S(1)}, u32[]{:S(2)}, u32[]{:S(2)}) collective-permute-start(bf16[2,80,256]{2,1,0:T(8,128)(2,1)S(1)} %ratio.2.after_ref.refs_0_), channel_id=1, source_target_pairs={{0,16},{4,20},{8,24},{12,28},{16,0},{20,4},{24,8},{28,12},{1,17},{... | collective-permute-start | bytes 245768 | tf_op jit(solution)/shard_map/ppermute | solution.py:622
  21.7 4.4 %collective-permute-start.5 = (bf16[2,80,256]{2,1,0:T(8,128)(2,1)S(1)}, bf16[2,80,256]{2,1,0:T(8,128)(2,1)S(1)}, u32[]{:S(2)}, u32[]{:S(2)}) collective-permute-start(bf16[2,80,256]{2,1,0:T(8,128)(2,1)S(1)} %ratio.2.after_ref.refs_0_), channel_id=1, source_target_pairs={{0,8},{4,12},{8,0},{12,4},{16,24},{20,28},{24,16},{28,20},{1,9},{5... | collective-permute-start | bytes 245768 | tf_op jit(solution)/shard_map/ppermute | solution.py:622
  26.2 1.7 %collective-permute-start.8 = (bf16[4,2,80,256]{3,2,1,0:T(8,128)(2,1)S(1)}, bf16[4,2,80,256]{3,2,1,0:T(8,128)(2,1)S(1)}, u32[]{:S(2)}, u32[]{:S(2)}) collective-permute-start(bf16[4,2,80,256]{3,2,1,0:T(8,128)(2,1)S(1)} %stack.14.same_ref), channel_id=1, source_target_pairs={{0,4},{4,0},{8,12},{12,8},{16,20},{20,16},{24,28},{28,24},{1,5},{5... | collective-permute-start | bytes 983048 | tf_op jit(solution)/shard_map/ppermute | solution.py:630
  30.9 1.7 %collective-permute-start.9 = (bf16[8,80,256]{2,1,0:T(8,128)(2,1)S(1)}, bf16[8,80,256]{2,1,0:T(8,128)(2,1)S(1)}, u32[]{:S(2)}, u32[]{:S(2)}) collective-permute-start(bf16[8,80,256]{2,1,0:T(8,128)(2,1)S(1)} %get-tuple-element.43), channel_id=1, source_target_pairs={{0,4},{4,0},{8,12},{12,8},{16,20},{20,16},{24,28},{28,24},{1,5},{5... | collective-permute-start | bytes 983048 | tf_op jit(solution)/shard_map/ppermute | solution.py:578
  32.8 5.6 %collective-permute-start.10 = (bf16[2,80,256]{2,1,0:T(8,128)(2,1)S(1)}, bf16[2,80,256]{2,1,0:T(8,128)(2,1)S(1)}, u32[]{:S(2)}, u32[]{:S(2)}) collective-permute-start(bf16[2,80,256]{2,1,0:T(8,128)(2,1)S(1)} %get-tuple-element.45), channel_id=1, source_target_pairs={{0,24},{4,28},{8,16},{12,20},{16,8},{20,12},{24,0},{28,4},{1,25},{... | collective-permute-start | bytes 245768 | tf_op jit(solution)/shard_map/ppermute | solution.py:602
  34.5 5.5 %collective-permute-start.11 = (bf16[2,80,256]{2,1,0:T(8,128)(2,1)S(1)}, bf16[2,80,256]{2,1,0:T(8,128)(2,1)S(1)}, u32[]{:S(2)}, u32[]{:S(2)}) collective-permute-start(bf16[2,80,256]{2,1,0:T(8,128)(2,1)S(1)} %get-tuple-element.46), channel_id=1, source_target_pairs={{0,16},{4,20},{8,24},{12,28},{16,0},{20,4},{24,8},{28,12},{1,17},{... | collective-permute-start | bytes 245768 | tf_op jit(solution)/shard_map/ppermute | solution.py:602
  35.0 5.0 %collective-permute-start.12 = (bf16[2,80,256]{2,1,0:T(8,128)(2,1)S(1)}, bf16[2,80,256]{2,1,0:T(8,128)(2,1)S(1)}, u32[]{:S(2)}, u32[]{:S(2)}) collective-permute-start(bf16[2,80,256]{2,1,0:T(8,128)(2,1)S(1)} %get-tuple-element.47), channel_id=1, source_target_pairs={{0,8},{4,12},{8,0},{12,4},{16,24},{20,28},{24,16},{28,20},{1,9},{5... | collective-permute-start | bytes 245768 | tf_op jit(solution)/shard_map/ppermute | solution.py:602
  40.1 4.0 %collective-permute-start.13 = (bf16[2,32,256]{2,1,0:T(8,128)(2,1)S(1)}, bf16[2,32,256]{2,1,0:T(8,128)(2,1)S(1)}, u32[]{:S(2)}, u32[]{:S(2)}) collective-permute-start(bf16[2,32,256]{2,1,0:T(8,128)(2,1)S(1)} %get-tuple-element.49), channel_id=1, source_target_pairs={{5,4},{4,5},{2,1},{1,2},{7,6},{6,7},{0,8},{3,11},{13,12},{12,13},{... | collective-permute-start | bytes 98312 | tf_op jit(solution)/shard_map/ppermute | solution.py:610
  44.4 5.9 %collective-permute-start.16 = (bf16[2,80,256]{2,1,0:T(8,128)(2,1)S(1)}, bf16[2,80,256]{2,1,0:T(8,128)(2,1)S(1)}, u32[]{:S(2)}, u32[]{:S(2)}) collective-permute-start(bf16[2,80,256]{2,1,0:T(8,128)(2,1)S(1)} %ratio.3.refs_0_), channel_id=1, source_target_pairs={{0,24},{4,28},{8,16},{12,20},{16,8},{20,12},{24,0},{28,4},{1,25},{... | collective-permute-start | bytes 245768 | tf_op jit(solution)/shard_map/ppermute | solution.py:622
  46.1 4.9 %collective-permute-start.15 = (bf16[2,80,256]{2,1,0:T(8,128)(2,1)S(1)}, bf16[2,80,256]{2,1,0:T(8,128)(2,1)S(1)}, u32[]{:S(2)}, u32[]{:S(2)}) collective-permute-start(bf16[2,80,256]{2,1,0:T(8,128)(2,1)S(1)} %ratio.3.refs_0_), channel_id=1, source_target_pairs={{0,16},{4,20},{8,24},{12,28},{16,0},{20,4},{24,8},{28,12},{1,17},{... | collective-permute-start | bytes 245768 | tf_op jit(solution)/shard_map/ppermute | solution.py:622
  46.7 4.4 %collective-permute-start.14 = (bf16[2,80,256]{2,1,0:T(8,128)(2,1)S(1)}, bf16[2,80,256]{2,1,0:T(8,128)(2,1)S(1)}, u32[]{:S(2)}, u32[]{:S(2)}) collective-permute-start(bf16[2,80,256]{2,1,0:T(8,128)(2,1)S(1)} %ratio.3.refs_0_), channel_id=1, source_target_pairs={{0,8},{4,12},{8,0},{12,4},{16,24},{20,28},{24,16},{28,20},{1,9},{5... | collective-permute-start | bytes 245768 | tf_op jit(solution)/shard_map/ppermute | solution.py:622
  51.2 1.7 %collective-permute-start.17 = (bf16[4,2,80,256]{3,2,1,0:T(8,128)(2,1)S(1)}, bf16[4,2,80,256]{3,2,1,0:T(8,128)(2,1)S(1)}, u32[]{:S(2)}, u32[]{:S(2)}) collective-permute-start(bf16[4,2,80,256]{3,2,1,0:T(8,128)(2,1)S(1)} %stack.15.same_ref), channel_id=1, source_target_pairs={{0,4},{4,0},{8,12},{12,8},{16,20},{20,16},{24,28},{28,24},{1,5},{5... | collective-permute-start | bytes 983048 | tf_op jit(solution)/shard_map/ppermute | solution.py:630
